TPU v7x, 128 devices: a whole 4x4x4 slice. The times are simulated.
128 devices in a mesh: row: 8 (over x, core), col: 16 (over z, y).
Axes of the slice: x: 4, y: 4, z: 4, core: 2. Of those that a mesh axis runs over, the one named last changes fastest.
Arguments:
- right_side: float32 [4, 128, 512, 128], P(None, 'row', 'col'), may hold values from -8 to 8
- material: int32 [128, 512, 128], P('row', 'col'), may hold values 0 or 1
- reaction: float32 [4, 2], replicated, may hold values from 0.05 to 1
- coarse_inverse: float32 [4, 1024, 1024], P(None, ('row', 'col')), may hold values from -0.000100708008 to 0.02
Outputs:
- corrected: float32 [4, 128, 512, 128], P(None, 'row', 'col')
All inputs are finite; a program needn't handle non-finite values. No bound on the sum of `material` on one device may be relied on, other than what follows from the above.
Results may differ from a plain program's by a relative error of at most 0.00007.
Values sent between devices are 32-bit elements; how exact they have to be, the bound alone decides.
No kernel may reach another device: no remote copies, remote signals or barrier semaphores. Data moves between devices by JAX's collectives and lax.ppermute only.
A program may use at most 128 MiB of HBM per device.

v0:
```python
import jax
import jax.numpy as jnp
from jax import lax
from jax.sharding import PartitionSpec as P

SWEEPS_FINE = 4
SWEEPS_COARSE = 4


LOW_BOUND = 0.25
HIGH_BOUND = 2.0
THETA = (HIGH_BOUND + LOW_BOUND) / 2.0
DELTA = (HIGH_BOUND - LOW_BOUND) / 2.0


def with_halo(cells, sides, width):
    for axis, dim in sides:
        count = lax.axis_size(axis)
        ends = count - 1
        head = lax.slice_in_dim(cells, 0, width, axis=dim)
        tail = lax.slice_in_dim(cells, cells.shape[dim] - width, cells.shape[dim], axis=dim)
        cells = jnp.concatenate(
            [
                lax.ppermute(tail, axis, [(i, (i + 1) % count) for i in range(ends)]),
                cells,
                lax.ppermute(head, axis, [((i + 1) % count, i) for i in range(ends)]),
            ],
            axis=dim,
        )
    return cells


def cell_diagonal(reaction, material):
    base = reaction[:, 0][:, None, None, None]
    jump = (reaction[:, 1] - reaction[:, 0])[:, None, None, None]
    return 6.0 + base + jump * material.astype(jnp.float32)[None]


def stencil_trim(padded, diagonal):
    inner = padded[:, 1:-1, 1:-1, :]
    deeper = jnp.pad(inner, ((0, 0), (0, 0), (0, 0), (1, 1)))
    beside = padded[:, 2:, 1:-1, :] + padded[:, :-2, 1:-1, :]
    beside = beside + padded[:, 1:-1, 2:, :] + padded[:, 1:-1, :-2, :]
    beside = beside + deeper[:, :, :, 2:] + deeper[:, :, :, :-2]
    return diagonal * inner - beside


def restrict_sum(field):
    f, a, b, z = field.shape
    return field.reshape(f, a // 2, 2, b // 2, 2, z // 2, 2).sum(axis=(2, 4, 6))


def prolong(field):
    f, a, b, z = field.shape
    wide = jnp.broadcast_to(field[:, :, None, :, None, :, None], (f, a, 2, b, 2, z, 2))
    return wide.reshape(f, 2 * a, 2 * b, 2 * z)


def chebyshev(operator, diagonal, source, initial, sweeps):
    inverse = 1.0 / diagonal
    if initial is None:
        solution = jnp.zeros_like(source)
        residue = source
    else:
        solution = initial
        residue = source - operator(initial)
    update = inverse * residue / THETA
    damping = DELTA / THETA
    for sweep in range(sweeps):
        solution = solution + update
        if sweep + 1 < sweeps:
            residue = residue - operator(update)
            following = 1.0 / (2.0 * THETA / DELTA - damping)
            update = following * damping * update + 2.0 * following / DELTA * inverse * residue
            damping = following
    return solution


def fine_apply(field, diagonal):
    padded = with_halo(field, (("row", 1), ("col", 2)), 1)
    return stencil_trim(padded, diagonal)


def coarse_apply(field, diagonal):
    padded = with_halo(field, (("row", 1), ("col", 2)), 1)
    return stencil_trim(padded, diagonal)


def coarsest_step(coarse_first, coarse_residue, coarse_inverse):
    fields, half_x, half_y, half_z = coarse_residue.shape
    groups = coarse_inverse.shape[1]
    grouped = (fields, half_x, half_y, groups, half_z // groups)
    local_sums = coarse_residue.reshape(grouped).sum(axis=(1, 2, 4))
    whole = lax.all_gather(local_sums, ("row", "col"), axis=1, tiled=True)
    correction = jnp.einsum("fic,fc->fi", coarse_inverse, whole, precision=lax.Precision.HIGHEST)
    return (coarse_first.reshape(grouped) + correction[:, None, None, :, None]).reshape(
        coarse_first.shape
    )


def body(right_side, material, reaction, coarse_inverse):
    diagonal = cell_diagonal(reaction, material)
    coarse_excess = 0.5 * restrict_sum(diagonal - 6.0)
    coarse_diagonal = 6.0 + coarse_excess
    first = chebyshev(
        lambda field: fine_apply(field, diagonal), diagonal, right_side, None, SWEEPS_FINE
    )
    fine_residue = right_side - fine_apply(first, diagonal)
    coarse_source = 0.5 * restrict_sum(fine_residue)
    coarse_first = chebyshev(
        lambda field: coarse_apply(field, coarse_diagonal),
        coarse_diagonal,
        coarse_source,
        None,
        SWEEPS_COARSE,
    )
    coarse_residue = coarse_source - coarse_apply(coarse_first, coarse_diagonal)
    coarse_second = coarsest_step(coarse_first, coarse_residue, coarse_inverse)
    coarse_final = chebyshev(
        lambda field: coarse_apply(field, coarse_diagonal),
        coarse_diagonal,
        coarse_source,
        coarse_second,
        SWEEPS_COARSE,
    )
    second = first + prolong(coarse_final)
    corrected = chebyshev(
        lambda field: fine_apply(field, diagonal), diagonal, right_side, second, SWEEPS_FINE
    )
    return corrected


def solution(mesh):
    placed = (
        P(None, "row", "col", None),
        P("row", "col", None),
        P(),
        P(None, ("row", "col"), None),
    )
    return jax.shard_map(
        body, mesh=mesh, in_specs=placed, out_specs=P(None, "row", "col", None), check_vma=False
    )
```

profile of v0, /device:TPU:34, one launch (start us, length us, event | category | flops | bytes accessed | tf_op | source)
XLA Modules:
  0.0 463.2 jit_solution(4112517444644844658)
XLA Ops:
  7.7 3.2 collective-permute-done.1
  10.9 4.5 collective-permute-start.2
  17.4 6.0 %collective-permute-done.3 = f32[4,18,1,128]{3,0,2,1:T(4,128)S(1)} collective-permute-done((f32[4,18,1,128]{3,0,2,1:T(4,128)S(1)}, f32[4,18,1,128]{3,0,2,1:T(4,128)S(1)}, u32[]{:S(2)}, u32[]{:S(2)}) %collective-permute-start.3) | collective-permute-done | bytes 36896 | tf_op jit(solution)/shard_map/ppermute | solution.py:24
  28.7 3.2 collective-permute-done.5
  33.8 3.9 collective-permute-start.7
  37.8 4.0 collective-permute-done.7
  47.0 3.2 collective-permute-done.9
  52.2 3.9 collective-permute-start.11
  56.2 4.0 collective-permute-done.11
  66.0 18.1 %mul.206 = f32[8,2,16,2,64,2]{5,4,3,2,1,0:T(8,128)} reshape(f32[16,32,128]{2,1,0:T(8,128)S(1)} %convert_element_type.21) | data formatting | bytes 524288 | tf_op jit(solution)/shard_map/mul | solution.py:36
  84.1 10.3 %copy.784 = f32[8,2,16,2,64,2]{4,2,5,3,1,0:T(8,128)S(1)} copy(f32[8,2,16,2,64,2]{5,4,3,2,1,0:T(8,128)} %mul.206) | data formatting | bytes 524288 | tf_op jit(solution)/shard_map/mul | solution.py:36
  96.4 3.9 collective-permute-start.15
  100.8 3.8 collective-permute-done.15
  106.4 17.8 %copy.789 = f32[4,16,32,128]{0,3,2,1:T(8,128)} copy(f32[4,16,32,128]{3,2,1,0:T(8,128)} %fusion.18) | data formatting | bytes 2097152 | tf_op jit(solution)/shard_map/sub | solution.py:108
  124.2 24.2 %reduce_sum.35 = f32[4,8,16,64]{0,3,2,1:T(8,128)} reduce(f32[4,8,2,16,2,64,2]{0,6,5,4,3,2,1:T(2,128)} %bitcast.18, f32[]{:T(128)} %constant.17.clone.1), dimensions={2,4,6}, to_apply=%region_1.2 | reduce | flops 229376 | bytes 1179652 | tf_op jit(solution)/shard_map/reduce_sum | solution.py:50
  160.6 3.9 collective-permute-start.19
  164.5 3.8 collective-permute-done.19
  177.9 3.9 collective-permute-start.23
  181.8 3.8 collective-permute-done.23
  195.1 3.9 collective-permute-start.27
  199.0 3.8 collective-permute-done.27
  212.6 3.9 collective-permute-start.31
  216.5 3.8 collective-permute-done.31
  220.8 53.5 %all-gather = f32[128,8,4]{1,2,0:T(4,128)S(1)} all-gather(f32[1,8,4]{1,2,0:T(4,128)S(1)} %bitcast.22), channel_id=1, replica_groups=mesh['row'=8,'col'=16] {'row','col'}, dimensions={0}, use_global_device_ids=true | all-gather | bytes 16512 | tf_op jit(solution)/shard_map/all_gather | solution.py:94
  275.1 4.8 %collective-permute-start.32 = (f32[4,1,16,64]{3,2,1,0:T(8,128)S(1)}, f32[4,1,16,64]{3,2,1,0:T(8,128)S(1)}, u32[]{:S(2)}, u32[]{:S(2)}) collective-permute-start(f32[4,1,16,64]{3,2,1,0:T(8,128)S(1)} %get-tuple-element.76), channel_id=1, source_target_pairs={{16,0},{32,16},{48,32},{64,48},{80,64},{96,80},{112,96},{17,1},{33... | collective-permute-start | bytes 49160 | tf_op jit(solution)/shard_map/ppermute | solution.py:26
  281.8 3.3 collective-permute-done.33
  285.2 4.5 collective-permute-start.34
  291.6 5.8 %collective-permute-done.35 = f32[4,10,1,64]{3,2,1,0:T(1,128)S(1)} collective-permute-done((f32[4,10,1,64]{3,2,1,0:T(1,128)S(1)}, f32[4,10,1,64]{3,2,1,0:T(1,128)S(1)}, u32[]{:S(2)}, u32[]{:S(2)}) %collective-permute-start.35) | collective-permute-done | bytes 10272 | tf_op jit(solution)/shard_map/ppermute | solution.py:24
  306.9 3.9 collective-permute-start.39
  310.8 3.8 collective-permute-done.39
  324.2 3.9 collective-permute-start.43
  328.1 3.8 collective-permute-done.43
  341.4 3.9 collective-permute-start.47
  345.3 3.8 collective-permute-done.47
  352.5 15.9 %broadcast_in_dim.2 = f32[4,8,2,16,2,64,2]{0,6,5,4,3,2,1:T(2,128)} broadcast(f32[4,8,16,64]{0,3,2,1:T(8,128)} %copy.794), dimensions={0,1,3,5} | broadcast | bytes 1179648 | tf_op jit(solution)/shard_map/broadcast_in_dim | solution.py:55
  368.5 19.5 %copy.795 = f32[4,16,32,128]{3,2,1,0:T(8,128)S(1)} copy(f32[4,16,32,128]{0,3,2,1:T(8,128)} %bitcast.19) | data formatting | bytes 2097152 | tf_op jit(solution)/shard_map/reshape | solution.py:56
  392.6 3.2 collective-permute-done.49
  397.8 3.9 collective-permute-start.51
  401.7 4.0 collective-permute-done.51
  410.9 3.2 collective-permute-done.53
  416.1 3.9 collective-permute-start.55
  420.1 4.0 collective-permute-done.55
  429.3 3.2 collective-permute-done.57
  434.5 3.9 collective-permute-start.59
  438.5 4.0 collective-permute-done.59
  447.7 3.2 collective-permute-done.61
  452.9 3.9 collective-permute-start.63
  456.9 4.0 collective-permute-done.63
  (198 shorter events, 142.0 us)
Async XLA Ops:
  5.3 5.6 %collective-permute-start.1 = (f32[4,1,32,128]{3,2,1,0:T(8,128)S(1)}, f32[4,1,32,128]{3,2,1,0:T(8,128)S(1)}, u32[]{:S(2)}, u32[]{:S(2)}) collective-permute-start(f32[4,1,32,128]{3,2,1,0:T(8,128)S(1)} %get-tuple-element.51), channel_id=1, source_target_pairs={{0,16},{16,32},{32,48},{48,64},{64,80},{80,96},{96,112},{1,17},{17... | collective-permute-start | bytes 196616 | tf_op jit(solution)/shard_map/ppermute | solution.py:24
  10.9 6.4 %collective-permute-start.2 = (f32[4,18,1,128]{3,0,2,1:T(4,128)S(1)}, f32[4,18,1,128]{3,0,2,1:T(4,128)S(1)}, u32[]{:S(2)}, u32[]{:S(2)}) collective-permute-start(f32[4,18,1,128]{3,0,2,1:T(4,128)S(1)} %copy.772), channel_id=1, source_target_pairs={{1,0},{2,1},{3,2},{4,3},{5,4},{6,5},{7,6},{8,7},{9,8},{10,9},{11,1... | collective-permute-start | bytes 110600 | tf_op jit(solution)/shard_map/ppermute | solution.py:26
  15.4 8.0 %collective-permute-start.3 = (f32[4,18,1,128]{3,0,2,1:T(4,128)S(1)}, f32[4,18,1,128]{3,0,2,1:T(4,128)S(1)}, u32[]{:S(2)}, u32[]{:S(2)}) collective-permute-start(f32[4,18,1,128]{3,0,2,1:T(4,128)S(1)} %copy.774), channel_id=1, source_target_pairs={{0,1},{1,2},{2,3},{3,4},{4,5},{5,6},{6,7},{7,8},{8,9},{9,10},{10,1... | collective-permute-start | bytes 110600 | tf_op jit(solution)/shard_map/ppermute | solution.py:24
  26.2 5.6 %collective-permute-start.5 = (f32[4,1,32,128]{3,2,1,0:T(8,128)S(1)}, f32[4,1,32,128]{3,2,1,0:T(8,128)S(1)}, u32[]{:S(2)}, u32[]{:S(2)}) collective-permute-start(f32[4,1,32,128]{3,2,1,0:T(8,128)S(1)} %get-tuple-element.49), channel_id=1, source_target_pairs={{0,16},{16,32},{32,48},{48,64},{64,80},{80,96},{96,112},{1,17},{17... | collective-permute-start | bytes 196616 | tf_op jit(solution)/shard_map/ppermute | solution.py:24
  31.9 5.9 %collective-permute-start.6 = (f32[4,18,1,128]{3,0,2,1:T(4,128)S(1)}, f32[4,18,1,128]{3,0,2,1:T(4,128)S(1)}, u32[]{:S(2)}, u32[]{:S(2)}) collective-permute-start(f32[4,18,1,128]{3,0,2,1:T(4,128)S(1)} %copy.776), channel_id=1, source_target_pairs={{1,0},{2,1},{3,2},{4,3},{5,4},{6,5},{7,6},{8,7},{9,8},{10,9},{11,1... | collective-permute-start | bytes 110600 | tf_op jit(solution)/shard_map/ppermute | solution.py:26
  33.8 8.0 %collective-permute-start.7 = (f32[4,18,1,128]{3,0,2,1:T(4,128)S(1)}, f32[4,18,1,128]{3,0,2,1:T(4,128)S(1)}, u32[]{:S(2)}, u32[]{:S(2)}) collective-permute-start(f32[4,18,1,128]{3,0,2,1:T(4,128)S(1)} %copy.778), channel_id=1, source_target_pairs={{0,1},{1,2},{2,3},{3,4},{4,5},{5,6},{6,7},{7,8},{8,9},{9,10},{10,1... | collective-permute-start | bytes 110600 | tf_op jit(solution)/shard_map/ppermute | solution.py:24
  44.6 5.6 %collective-permute-start.9 = (f32[4,1,32,128]{3,2,1,0:T(8,128)S(1)}, f32[4,1,32,128]{3,2,1,0:T(8,128)S(1)}, u32[]{:S(2)}, u32[]{:S(2)}) collective-permute-start(f32[4,1,32,128]{3,2,1,0:T(8,128)S(1)} %get-tuple-element.47), channel_id=1, source_target_pairs={{0,16},{16,32},{32,48},{48,64},{64,80},{80,96},{96,112},{1,17},{17... | collective-permute-start | bytes 196616 | tf_op jit(solution)/shard_map/ppermute | solution.py:24
  50.3 5.9 %collective-permute-start.10 = (f32[4,18,1,128]{3,0,2,1:T(4,128)S(1)}, f32[4,18,1,128]{3,0,2,1:T(4,128)S(1)}, u32[]{:S(2)}, u32[]{:S(2)}) collective-permute-start(f32[4,18,1,128]{3,0,2,1:T(4,128)S(1)} %copy.780), channel_id=1, source_target_pairs={{1,0},{2,1},{3,2},{4,3},{5,4},{6,5},{7,6},{8,7},{9,8},{10,9},{11,1... | collective-permute-start | bytes 110600 | tf_op jit(solution)/shard_map/ppermute | solution.py:26
  52.2 8.0 %collective-permute-start.11 = (f32[4,18,1,128]{3,0,2,1:T(4,128)S(1)}, f32[4,18,1,128]{3,0,2,1:T(4,128)S(1)}, u32[]{:S(2)}, u32[]{:S(2)}) collective-permute-start(f32[4,18,1,128]{3,0,2,1:T(4,128)S(1)} %copy.782), channel_id=1, source_target_pairs={{0,1},{1,2},{2,3},{3,4},{4,5},{5,6},{6,7},{7,8},{8,9},{9,10},{10,1... | collective-permute-start | bytes 110600 | tf_op jit(solution)/shard_map/ppermute | solution.py:24
  61.6 32.7 %collective-permute-start.12 = (f32[4,1,32,128]{3,2,1,0:T(8,128)S(1)}, f32[4,1,32,128]{3,2,1,0:T(8,128)S(1)}, u32[]{:S(2)}, u32[]{:S(2)}) collective-permute-start(f32[4,1,32,128]{3,2,1,0:T(8,128)S(1)} %get-tuple-element.46), channel_id=1, source_target_pairs={{16,0},{32,16},{48,32},{64,48},{80,64},{96,80},{112,96},{17,1},{33... | collective-permute-start | bytes 196616 | tf_op jit(solution)/shard_map/ppermute | solution.py:26
  63.6 30.8 %collective-permute-start.13 = (f32[4,1,32,128]{3,2,1,0:T(8,128)S(1)}, f32[4,1,32,128]{3,2,1,0:T(8,128)S(1)}, u32[]{:S(2)}, u32[]{:S(2)}) collective-permute-start(f32[4,1,32,128]{3,2,1,0:T(8,128)S(1)} %get-tuple-element.45), channel_id=1, source_target_pairs={{0,16},{16,32},{32,48},{48,64},{64,80},{80,96},{96,112},{1,17},{17... | collective-permute-start | bytes 196616 | tf_op jit(solution)/shard_map/ppermute | solution.py:24
  94.5 6.3 %collective-permute-start.14 = (f32[4,18,1,128]{3,0,2,1:T(4,128)S(1)}, f32[4,18,1,128]{3,0,2,1:T(4,128)S(1)}, u32[]{:S(2)}, u32[]{:S(2)}) collective-permute-start(f32[4,18,1,128]{3,0,2,1:T(4,128)S(1)} %copy.785), channel_id=1, source_target_pairs={{1,0},{2,1},{3,2},{4,3},{5,4},{6,5},{7,6},{8,7},{9,8},{10,9},{11,1... | collective-permute-start | bytes 110600 | tf_op jit(solution)/shard_map/ppermute | solution.py:26
  96.4 8.2 %collective-permute-start.15 = (f32[4,18,1,128]{3,0,2,1:T(4,128)S(1)}, f32[4,18,1,128]{3,0,2,1:T(4,128)S(1)}, u32[]{:S(2)}, u32[]{:S(2)}) collective-permute-start(f32[4,18,1,128]{3,0,2,1:T(4,128)S(1)} %copy.787), channel_id=1, source_target_pairs={{0,1},{1,2},{2,3},{3,4},{4,5},{5,6},{6,7},{7,8},{8,9},{9,10},{10,1... | collective-permute-start | bytes 110600 | tf_op jit(solution)/shard_map/ppermute | solution.py:24
  153.4 5.2 %collective-permute-start.17 = (f32[4,1,16,64]{3,2,1,0:T(8,128)S(1)}, f32[4,1,16,64]{3,2,1,0:T(8,128)S(1)}, u32[]{:S(2)}, u32[]{:S(2)}) collective-permute-start(f32[4,1,16,64]{3,2,1,0:T(8,128)S(1)} %get-tuple-element.83), channel_id=1, source_target_pairs={{0,16},{16,32},{32,48},{48,64},{64,80},{80,96},{96,112},{1,17},{17... | collective-permute-start | bytes 49160 | tf_op jit(solution)/shard_map/ppermute | solution.py:24
  158.7 5.9 %collective-permute-start.18 = (f32[4,10,1,64]{3,2,1,0:T(1,128)S(1)}, f32[4,10,1,64]{3,2,1,0:T(1,128)S(1)}, u32[]{:S(2)}, u32[]{:S(2)}) collective-permute-start(f32[4,10,1,64]{3,2,1,0:T(1,128)S(1)} %get-tuple-element.67), channel_id=1, source_target_pairs={{1,0},{2,1},{3,2},{4,3},{5,4},{6,5},{7,6},{8,7},{9,8},{10,9},{11,1... | collective-permute-start | bytes 30728 | tf_op jit(solution)/shard_map/ppermute | solution.py:26
  160.6 7.8 %collective-permute-start.19 = (f32[4,10,1,64]{3,2,1,0:T(1,128)S(1)}, f32[4,10,1,64]{3,2,1,0:T(1,128)S(1)}, u32[]{:S(2)}, u32[]{:S(2)}) collective-permute-start(f32[4,10,1,64]{3,2,1,0:T(1,128)S(1)} %get-tuple-element.68), channel_id=1, source_target_pairs={{0,1},{1,2},{2,3},{3,4},{4,5},{5,6},{6,7},{7,8},{8,9},{9,10},{10,1... | collective-permute-start | bytes 30728 | tf_op jit(solution)/shard_map/ppermute | solution.py:24
  170.7 5.2 %collective-permute-start.21 = (f32[4,1,16,64]{3,2,1,0:T(8,128)S(1)}, f32[4,1,16,64]{3,2,1,0:T(8,128)S(1)}, u32[]{:S(2)}, u32[]{:S(2)}) collective-permute-start(f32[4,1,16,64]{3,2,1,0:T(8,128)S(1)} %get-tuple-element.81), channel_id=1, source_target_pairs={{0,16},{16,32},{32,48},{48,64},{64,80},{80,96},{96,112},{1,17},{17... | collective-permute-start | bytes 49160 | tf_op jit(solution)/shard_map/ppermute | solution.py:24
  175.9 5.9 %collective-permute-start.22 = (f32[4,10,1,64]{3,2,1,0:T(1,128)S(1)}, f32[4,10,1,64]{3,2,1,0:T(1,128)S(1)}, u32[]{:S(2)}, u32[]{:S(2)}) collective-permute-start(f32[4,10,1,64]{3,2,1,0:T(1,128)S(1)} %get-tuple-element.65), channel_id=1, source_target_pairs={{1,0},{2,1},{3,2},{4,3},{5,4},{6,5},{7,6},{8,7},{9,8},{10,9},{11,1... | collective-permute-start | bytes 30728 | tf_op jit(solution)/shard_map/ppermute | solution.py:26
  177.9 7.8 %collective-permute-start.23 = (f32[4,10,1,64]{3,2,1,0:T(1,128)S(1)}, f32[4,10,1,64]{3,2,1,0:T(1,128)S(1)}, u32[]{:S(2)}, u32[]{:S(2)}) collective-permute-start(f32[4,10,1,64]{3,2,1,0:T(1,128)S(1)} %get-tuple-element.66), channel_id=1, source_target_pairs={{0,1},{1,2},{2,3},{3,4},{4,5},{5,6},{6,7},{7,8},{8,9},{9,10},{10,1... | collective-permute-start | bytes 30728 | tf_op jit(solution)/shard_map/ppermute | solution.py:24
  187.9 5.2 %collective-permute-start.25 = (f32[4,1,16,64]{3,2,1,0:T(8,128)S(1)}, f32[4,1,16,64]{3,2,1,0:T(8,128)S(1)}, u32[]{:S(2)}, u32[]{:S(2)}) collective-permute-start(f32[4,1,16,64]{3,2,1,0:T(8,128)S(1)} %get-tuple-element.79), channel_id=1, source_target_pairs={{0,16},{16,32},{32,48},{48,64},{64,80},{80,96},{96,112},{1,17},{17... | collective-permute-start | bytes 49160 | tf_op jit(solution)/shard_map/ppermute | solution.py:24
  193.2 5.9 %collective-permute-start.26 = (f32[4,10,1,64]{3,2,1,0:T(1,128)S(1)}, f32[4,10,1,64]{3,2,1,0:T(1,128)S(1)}, u32[]{:S(2)}, u32[]{:S(2)}) collective-permute-start(f32[4,10,1,64]{3,2,1,0:T(1,128)S(1)} %get-tuple-element.63), channel_id=1, source_target_pairs={{1,0},{2,1},{3,2},{4,3},{5,4},{6,5},{7,6},{8,7},{9,8},{10,9},{11,1... | collective-permute-start | bytes 30728 | tf_op jit(solution)/shard_map/ppermute | solution.py:26
  195.1 7.8 %collective-permute-start.27 = (f32[4,10,1,64]{3,2,1,0:T(1,128)S(1)}, f32[4,10,1,64]{3,2,1,0:T(1,128)S(1)}, u32[]{:S(2)}, u32[]{:S(2)}) collective-permute-start(f32[4,10,1,64]{3,2,1,0:T(1,128)S(1)} %get-tuple-element.64), channel_id=1, source_target_pairs={{0,1},{1,2},{2,3},{3,4},{4,5},{5,6},{6,7},{7,8},{8,9},{9,10},{10,1... | collective-permute-start | bytes 30728 | tf_op jit(solution)/shard_map/ppermute | solution.py:24
  205.4 5.2 %collective-permute-start.29 = (f32[4,1,16,64]{3,2,1,0:T(8,128)S(1)}, f32[4,1,16,64]{3,2,1,0:T(8,128)S(1)}, u32[]{:S(2)}, u32[]{:S(2)}) collective-permute-start(f32[4,1,16,64]{3,2,1,0:T(8,128)S(1)} %get-tuple-element.77), channel_id=1, source_target_pairs={{0,16},{16,32},{32,48},{48,64},{64,80},{80,96},{96,112},{1,17},{17... | collective-permute-start | bytes 49160 | tf_op jit(solution)/shard_map/ppermute | solution.py:24
  210.7 5.9 %collective-permute-start.30 = (f32[4,10,1,64]{3,2,1,0:T(1,128)S(1)}, f32[4,10,1,64]{3,2,1,0:T(1,128)S(1)}, u32[]{:S(2)}, u32[]{:S(2)}) collective-permute-start(f32[4,10,1,64]{3,2,1,0:T(1,128)S(1)} %get-tuple-element.61), channel_id=1, source_target_pairs={{1,0},{2,1},{3,2},{4,3},{5,4},{6,5},{7,6},{8,7},{9,8},{10,9},{11,1... | collective-permute-start | bytes 30728 | tf_op jit(solution)/shard_map/ppermute | solution.py:26
  212.6 7.8 %collective-permute-start.31 = (f32[4,10,1,64]{3,2,1,0:T(1,128)S(1)}, f32[4,10,1,64]{3,2,1,0:T(1,128)S(1)}, u32[]{:S(2)}, u32[]{:S(2)}) collective-permute-start(f32[4,10,1,64]{3,2,1,0:T(1,128)S(1)} %get-tuple-element.62), channel_id=1, source_target_pairs={{0,1},{1,2},{2,3},{3,4},{4,5},{5,6},{6,7},{7,8},{8,9},{9,10},{10,1... | collective-permute-start | bytes 30728 | tf_op jit(solution)/shard_map/ppermute | solution.py:24
  275.1 6.8 %collective-permute-start.32 = (f32[4,1,16,64]{3,2,1,0:T(8,128)S(1)}, f32[4,1,16,64]{3,2,1,0:T(8,128)S(1)}, u32[]{:S(2)}, u32[]{:S(2)}) collective-permute-start(f32[4,1,16,64]{3,2,1,0:T(8,128)S(1)} %get-tuple-element.76), channel_id=1, source_target_pairs={{16,0},{32,16},{48,32},{64,48},{80,64},{96,80},{112,96},{17,1},{33... | collective-permute-start | bytes 49160 | tf_op jit(solution)/shard_map/ppermute | solution.py:26
  279.9 5.2 %collective-permute-start.33 = (f32[4,1,16,64]{3,2,1,0:T(8,128)S(1)}, f32[4,1,16,64]{3,2,1,0:T(8,128)S(1)}, u32[]{:S(2)}, u32[]{:S(2)}) collective-permute-start(f32[4,1,16,64]{3,2,1,0:T(8,128)S(1)} %get-tuple-element.75), channel_id=1, source_target_pairs={{0,16},{16,32},{32,48},{48,64},{64,80},{80,96},{96,112},{1,17},{17... | collective-permute-start | bytes 49160 | tf_op jit(solution)/shard_map/ppermute | solution.py:24
  285.2 6.4 %collective-permute-start.34 = (f32[4,10,1,64]{3,2,1,0:T(1,128)S(1)}, f32[4,10,1,64]{3,2,1,0:T(1,128)S(1)}, u32[]{:S(2)}, u32[]{:S(2)}) collective-permute-start(f32[4,10,1,64]{3,2,1,0:T(1,128)S(1)} %get-tuple-element.59), channel_id=1, source_target_pairs={{1,0},{2,1},{3,2},{4,3},{5,4},{6,5},{7,6},{8,7},{9,8},{10,9},{11,1... | collective-permute-start | bytes 30728 | tf_op jit(solution)/shard_map/ppermute | solution.py:26
  289.7 7.8 %collective-permute-start.35 = (f32[4,10,1,64]{3,2,1,0:T(1,128)S(1)}, f32[4,10,1,64]{3,2,1,0:T(1,128)S(1)}, u32[]{:S(2)}, u32[]{:S(2)}) collective-permute-start(f32[4,10,1,64]{3,2,1,0:T(1,128)S(1)} %get-tuple-element.60), channel_id=1, source_target_pairs={{0,1},{1,2},{2,3},{3,4},{4,5},{5,6},{6,7},{7,8},{8,9},{9,10},{10,1... | collective-permute-start | bytes 30728 | tf_op jit(solution)/shard_map/ppermute | solution.py:24
  299.7 5.2 %collective-permute-start.37 = (f32[4,1,16,64]{3,2,1,0:T(8,128)S(1)}, f32[4,1,16,64]{3,2,1,0:T(8,128)S(1)}, u32[]{:S(2)}, u32[]{:S(2)}) collective-permute-start(f32[4,1,16,64]{3,2,1,0:T(8,128)S(1)} %get-tuple-element.73), channel_id=1, source_target_pairs={{0,16},{16,32},{32,48},{48,64},{64,80},{80,96},{96,112},{1,17},{17... | collective-permute-start | bytes 49160 | tf_op jit(solution)/shard_map/ppermute | solution.py:24
  305.0 5.9 %collective-permute-start.38 = (f32[4,10,1,64]{3,2,1,0:T(1,128)S(1)}, f32[4,10,1,64]{3,2,1,0:T(1,128)S(1)}, u32[]{:S(2)}, u32[]{:S(2)}) collective-permute-start(f32[4,10,1,64]{3,2,1,0:T(1,128)S(1)} %get-tuple-element.57), channel_id=1, source_target_pairs={{1,0},{2,1},{3,2},{4,3},{5,4},{6,5},{7,6},{8,7},{9,8},{10,9},{11,1... | collective-permute-start | bytes 30728 | tf_op jit(solution)/shard_map/ppermute | solution.py:26
  306.9 7.8 %collective-permute-start.39 = (f32[4,10,1,64]{3,2,1,0:T(1,128)S(1)}, f32[4,10,1,64]{3,2,1,0:T(1,128)S(1)}, u32[]{:S(2)}, u32[]{:S(2)}) collective-permute-start(f32[4,10,1,64]{3,2,1,0:T(1,128)S(1)} %get-tuple-element.58), channel_id=1, source_target_pairs={{0,1},{1,2},{2,3},{3,4},{4,5},{5,6},{6,7},{7,8},{8,9},{9,10},{10,1... | collective-permute-start | bytes 30728 | tf_op jit(solution)/shard_map/ppermute | solution.py:24
  322.2 5.9 %collective-permute-start.42 = (f32[4,10,1,64]{3,2,1,0:T(1,128)S(1)}, f32[4,10,1,64]{3,2,1,0:T(1,128)S(1)}, u32[]{:S(2)}, u32[]{:S(2)}) collective-permute-start(f32[4,10,1,64]{3,2,1,0:T(1,128)S(1)} %get-tuple-element.55), channel_id=1, source_target_pairs={{1,0},{2,1},{3,2},{4,3},{5,4},{6,5},{7,6},{8,7},{9,8},{10,9},{11,1... | collective-permute-start | bytes 30728 | tf_op jit(solution)/shard_map/ppermute | solution.py:26
  324.2 7.8 %collective-permute-start.43 = (f32[4,10,1,64]{3,2,1,0:T(1,128)S(1)}, f32[4,10,1,64]{3,2,1,0:T(1,128)S(1)}, u32[]{:S(2)}, u32[]{:S(2)}) collective-permute-start(f32[4,10,1,64]{3,2,1,0:T(1,128)S(1)} %get-tuple-element.56), channel_id=1, source_target_pairs={{0,1},{1,2},{2,3},{3,4},{4,5},{5,6},{6,7},{7,8},{8,9},{9,10},{10,1... | collective-permute-start | bytes 30728 | tf_op jit(solution)/shard_map/ppermute | solution.py:24
  339.5 5.9 %collective-permute-start.46 = (f32[4,10,1,64]{3,2,1,0:T(1,128)S(1)}, f32[4,10,1,64]{3,2,1,0:T(1,128)S(1)}, u32[]{:S(2)}, u32[]{:S(2)}) collective-permute-start(f32[4,10,1,64]{3,2,1,0:T(1,128)S(1)} %get-tuple-element.53), channel_id=1, source_target_pairs={{1,0},{2,1},{3,2},{4,3},{5,4},{6,5},{7,6},{8,7},{9,8},{10,9},{11,1... | collective-permute-start | bytes 30728 | tf_op jit(solution)/shard_map/ppermute | solution.py:26
  341.4 7.8 %collective-permute-start.47 = (f32[4,10,1,64]{3,2,1,0:T(1,128)S(1)}, f32[4,10,1,64]{3,2,1,0:T(1,128)S(1)}, u32[]{:S(2)}, u32[]{:S(2)}) collective-permute-start(f32[4,10,1,64]{3,2,1,0:T(1,128)S(1)} %get-tuple-element.54), channel_id=1, source_target_pairs={{0,1},{1,2},{2,3},{3,4},{4,5},{5,6},{6,7},{7,8},{8,9},{9,10},{10,1... | collective-permute-start | bytes 30728 | tf_op jit(solution)/shard_map/ppermute | solution.py:24
  390.1 5.6 %collective-permute-start.49 = (f32[4,1,32,128]{3,2,1,0:T(8,128)S(1)}, f32[4,1,32,128]{3,2,1,0:T(8,128)S(1)}, u32[]{:S(2)}, u32[]{:S(2)}) collective-permute-start(f32[4,1,32,128]{3,2,1,0:T(8,128)S(1)} %get-tuple-element.43), channel_id=1, source_target_pairs={{0,16},{16,32},{32,48},{48,64},{64,80},{80,96},{96,112},{1,17},{17... | collective-permute-start | bytes 196616 | tf_op jit(solution)/shard_map/ppermute | solution.py:24
  395.8 5.9 %collective-permute-start.50 = (f32[4,18,1,128]{3,0,2,1:T(4,128)S(1)}, f32[4,18,1,128]{3,0,2,1:T(4,128)S(1)}, u32[]{:S(2)}, u32[]{:S(2)}) collective-permute-start(f32[4,18,1,128]{3,0,2,1:T(4,128)S(1)} %copy.796), channel_id=1, source_target_pairs={{1,0},{2,1},{3,2},{4,3},{5,4},{6,5},{7,6},{8,7},{9,8},{10,9},{11,1... | collective-permute-start | bytes 110600 | tf_op jit(solution)/shard_map/ppermute | solution.py:26
  397.8 8.0 %collective-permute-start.51 = (f32[4,18,1,128]{3,0,2,1:T(4,128)S(1)}, f32[4,18,1,128]{3,0,2,1:T(4,128)S(1)}, u32[]{:S(2)}, u32[]{:S(2)}) collective-permute-start(f32[4,18,1,128]{3,0,2,1:T(4,128)S(1)} %copy.798), channel_id=1, source_target_pairs={{0,1},{1,2},{2,3},{3,4},{4,5},{5,6},{6,7},{7,8},{8,9},{9,10},{10,1... | collective-permute-start | bytes 110600 | tf_op jit(solution)/shard_map/ppermute | solution.py:24
  408.5 5.6 %collective-permute-start.53 = (f32[4,1,32,128]{3,2,1,0:T(8,128)S(1)}, f32[4,1,32,128]{3,2,1,0:T(8,128)S(1)}, u32[]{:S(2)}, u32[]{:S(2)}) collective-permute-start(f32[4,1,32,128]{3,2,1,0:T(8,128)S(1)} %get-tuple-element.41), channel_id=1, source_target_pairs={{0,16},{16,32},{32,48},{48,64},{64,80},{80,96},{96,112},{1,17},{17... | collective-permute-start | bytes 196616 | tf_op jit(solution)/shard_map/ppermute | solution.py:24
  414.2 5.9 %collective-permute-start.54 = (f32[4,18,1,128]{3,0,2,1:T(4,128)S(1)}, f32[4,18,1,128]{3,0,2,1:T(4,128)S(1)}, u32[]{:S(2)}, u32[]{:S(2)}) collective-permute-start(f32[4,18,1,128]{3,0,2,1:T(4,128)S(1)} %copy.800), channel_id=1, source_target_pairs={{1,0},{2,1},{3,2},{4,3},{5,4},{6,5},{7,6},{8,7},{9,8},{10,9},{11,1... | collective-permute-start | bytes 110600 | tf_op jit(solution)/shard_map/ppermute | solution.py:26
  416.1 8.0 %collective-permute-start.55 = (f32[4,18,1,128]{3,0,2,1:T(4,128)S(1)}, f32[4,18,1,128]{3,0,2,1:T(4,128)S(1)}, u32[]{:S(2)}, u32[]{:S(2)}) collective-permute-start(f32[4,18,1,128]{3,0,2,1:T(4,128)S(1)} %copy.802), channel_id=1, source_target_pairs={{0,1},{1,2},{2,3},{3,4},{4,5},{5,6},{6,7},{7,8},{8,9},{9,10},{10,1... | collective-permute-start | bytes 110600 | tf_op jit(solution)/shard_map/ppermute | solution.py:24
  426.9 5.6 %collective-permute-start.57 = (f32[4,1,32,128]{3,2,1,0:T(8,128)S(1)}, f32[4,1,32,128]{3,2,1,0:T(8,128)S(1)}, u32[]{:S(2)}, u32[]{:S(2)}) collective-permute-start(f32[4,1,32,128]{3,2,1,0:T(8,128)S(1)} %get-tuple-element.39), channel_id=1, source_target_pairs={{0,16},{16,32},{32,48},{48,64},{64,80},{80,96},{96,112},{1,17},{17... | collective-permute-start | bytes 196616 | tf_op jit(solution)/shard_map/ppermute | solution.py:24
  432.6 5.9 %collective-permute-start.58 = (f32[4,18,1,128]{3,0,2,1:T(4,128)S(1)}, f32[4,18,1,128]{3,0,2,1:T(4,128)S(1)}, u32[]{:S(2)}, u32[]{:S(2)}) collective-permute-start(f32[4,18,1,128]{3,0,2,1:T(4,128)S(1)} %copy.804), channel_id=1, source_target_pairs={{1,0},{2,1},{3,2},{4,3},{5,4},{6,5},{7,6},{8,7},{9,8},{10,9},{11,1... | collective-permute-start | bytes 110600 | tf_op jit(solution)/shard_map/ppermute | solution.py:26
  434.5 8.0 %collective-permute-start.59 = (f32[4,18,1,128]{3,0,2,1:T(4,128)S(1)}, f32[4,18,1,128]{3,0,2,1:T(4,128)S(1)}, u32[]{:S(2)}, u32[]{:S(2)}) collective-permute-start(f32[4,18,1,128]{3,0,2,1:T(4,128)S(1)} %copy.806), channel_id=1, source_target_pairs={{0,1},{1,2},{2,3},{3,4},{4,5},{5,6},{6,7},{7,8},{8,9},{9,10},{10,1... | collective-permute-start | bytes 110600 | tf_op jit(solution)/shard_map/ppermute | solution.py:24
  445.3 5.6 %collective-permute-start.61 = (f32[4,1,32,128]{3,2,1,0:T(8,128)S(1)}, f32[4,1,32,128]{3,2,1,0:T(8,128)S(1)}, u32[]{:S(2)}, u32[]{:S(2)}) collective-permute-start(f32[4,1,32,128]{3,2,1,0:T(8,128)S(1)} %get-tuple-element.37), channel_id=1, source_target_pairs={{0,16},{16,32},{32,48},{48,64},{64,80},{80,96},{96,112},{1,17},{17... | collective-permute-start | bytes 196616 | tf_op jit(solution)/shard_map/ppermute | solution.py:24
  451.0 5.9 %collective-permute-start.62 = (f32[4,18,1,128]{3,0,2,1:T(4,128)S(1)}, f32[4,18,1,128]{3,0,2,1:T(4,128)S(1)}, u32[]{:S(2)}, u32[]{:S(2)}) collective-permute-start(f32[4,18,1,128]{3,0,2,1:T(4,128)S(1)} %copy.808), channel_id=1, source_target_pairs={{1,0},{2,1},{3,2},{4,3},{5,4},{6,5},{7,6},{8,7},{9,8},{10,9},{11,1... | collective-permute-start | bytes 110600 | tf_op jit(solution)/shard_map/ppermute | solution.py:26
  452.9 8.0 %collective-permute-start.63 = (f32[4,18,1,128]{3,0,2,1:T(4,128)S(1)}, f32[4,18,1,128]{3,0,2,1:T(4,128)S(1)}, u32[]{:S(2)}, u32[]{:S(2)}) collective-permute-start(f32[4,18,1,128]{3,0,2,1:T(4,128)S(1)} %copy.810), channel_id=1, source_target_pairs={{0,1},{1,2},{2,3},{3,4},{4,5},{5,6},{6,7},{7,8},{8,9},{9,10},{10,1... | collective-permute-start | bytes 110600 | tf_op jit(solution)/shard_map/ppermute | solution.py:24
  (23 other events, 613.3 us)
where the time goes:
time: 466 us; the launch traced here: 463 us
  starting transfers between devices  166 us (36%)
  waiting for transfers between devices  112 us (24%)
  local copies, waits for them, and re-layouts  88.9 us (19%)
  blocking collectives  53.5 us (11%)
  other arithmetic  41.3 us (9%)
    ppermute x32, waiting for transfers between devices, with_halo(): lax.ppermute(tail, axis, [(i, (i + 1) % count) for i in range(ends)])  111 us
    ppermute x32, starting transfers between devices, with_halo(): lax.ppermute(tail, axis, [(i, (i + 1) % count) for i in range(ends)])  96.8 us
    ppermute x32, starting transfers between devices, with_halo(): lax.ppermute(head, axis, [((i + 1) % count, i) for i in range(ends)])  69.5 us
    all_gather x1, blocking collectives, coarsest_step(): whole = lax.all_gather(local_sums, ('row', 'col'), axis=1, tiled=True)  53.5 us
    mul x2, local copies, waits for them, and re-layouts, cell_diagonal(): return 6.0 + base + jump * material.astype(jnp.float32)[None]  28.4 us
    reduce_sum x2, other arithmetic, restrict_sum(): return field.reshape(f, a // 2, 2, b // 2, 2, z // 2, 2).sum(axis=(2, 4, 6))  24.6 us
    reshape x1, local copies, waits for them, and re-layouts, prolong(): return wide.reshape(f, 2 * a, 2 * b, 2 * z)  19.5 us
    sub x1, local copies, waits for them, and re-layouts, body(): fine_residue = right_side - fine_apply(first, diagonal)  17.8 us
  transfers between devices with their start and end apart: 64, of which 31 were waited for; matrix products, arithmetic and copies ran while one was open for 6% of the time, Pallas kernels for 0%

commit v1 on v0

v1 whole, which is shorter than its diff:
```python
import functools

import jax
import jax.numpy as jnp
from jax import lax
from jax.experimental import pallas as pl
from jax.experimental.pallas import tpu as pltpu
from jax.sharding import PartitionSpec as P

FIELDS = 4
CX, CY, CZ = 16, 32, 128
HX, HY = CX // 2, CY // 2
GROUPS = 8
SWEEPS = 4
LOW_BOUND = 0.25
HIGH_BOUND = 2.0
THETA = (HIGH_BOUND + LOW_BOUND) / 2.0
DELTA = (HIGH_BOUND - LOW_BOUND) / 2.0

FX, FY, FO = CX + 8, CY + 32, 16
QX, QY, QO = HX + 18, HY + 32, 16
EX = HX + 12
CORNER_AT = {1: 0, 2: 8, 3: 16, 9: 23, 4: 24, 8: 30, 5: 32, 7: 37, 6: 40}
CORNER_LINES = 48


def corner_size(j):
    return min(HX, 10 - j)


def coefficients():
    rho = DELTA / THETA
    pairs = []
    for _ in range(SWEEPS - 1):
        following = 1.0 / (2.0 * THETA / DELTA - rho)
        pairs.append((following * rho, 2.0 * following / DELTA))
        rho = following
    return pairs


def lanes():
    return lax.broadcasted_iota(jnp.int32, (1, CZ), 1)


def beside(ref, f, x, low, count, width):
    here = ref[f, x, low : low + count, :]
    lane = lanes()
    total = ref[f, x + 1, low : low + count, :] + ref[f, x - 1, low : low + count, :]
    total = total + ref[f, x, low + 1 : low + 1 + count, :]
    total = total + ref[f, x, low - 1 : low - 1 + count, :]
    total = total + jnp.where(lane < CZ - width, pltpu.roll(here, CZ - width, 1), 0.0)
    total = total + jnp.where(lane >= width, pltpu.roll(here, width, 1), 0.0)
    return here, total


def diagonal_values(reaction, f):
    low = reaction[f, 0]
    jump = reaction[f, 1] - low
    return 6.0 + low, 6.0 + low + jump


def inverse_of(code, reaction, f):
    fluid, solid = diagonal_values(reaction, f)
    ones = jnp.ones((8, CZ), jnp.float32)
    fluid, solid = (ones / (ones * fluid))[:1], (ones / (ones * solid))[:1]
    return jnp.where(code == 0.0, fluid, jnp.where(code == 1.0, solid, 0.0))


def place():
    return lax.axis_index("row"), lax.axis_index("col")


def pack_layers(b, material, up, down, right, left):
    for f in range(FIELDS + 1):
        if f < FIELDS:
            take = lambda start, size, step: b[f, pl.ds(start, size, stride=step), :]
        else:
            take = lambda start, size, step: material[pl.ds(start, size, stride=step), :].astype(
                jnp.float32
            )
        for i in range(4):
            up[f, i] = take((CX - 4 + i) * CY, CY, 1)
            down[f, i] = take(i * CY, CY, 1)
            right[f, i] = take(CY - 4 + i, CX, CY)
            left[f, i] = take(i, CX, CY)


def pack_corners(low, high, up, down):
    for f in range(FIELDS + 1):
        for side, (ref, rows) in enumerate(((low, (3, 2, 1)), (high, (0, 1, 2)))):
            at = 8 * side
            for j, row in enumerate(rows):
                size = 3 - j
                up[f, at : at + size, :] = ref[f, row, CX - size : CX, :]
                down[f, at : at + size, :] = ref[f, row, 0:size, :]
                at += size
            up[f, at : at + 2, :] = jnp.zeros((2, CZ), jnp.float32)
            down[f, at : at + 2, :] = jnp.zeros((2, CZ), jnp.float32)


def smooth_first(
    nrow, ncol, reaction, b, material, above, below, low, high, kabove, kbelow,
    first, scaled, code, coarse, up, down, right, left,
    s, inv, p0, p1, p2, p3, pair,
):
    row, col = place()
    parts = (p0, p1, p2, p3)
    zeros = jnp.zeros((FY, CZ), jnp.float32)
    for x in (*range(4), *range(FX - 4, FX)):
        for f in range(FIELDS):
            s[f, x] = zeros
        code[x] = zeros + 2.0

    def own(i, carry):
        x = i + 4
        for f in range(FIELDS):
            s[f, x, 8:16, :] = zeros[:8]
            s[f, x, 16:48, :] = b[f, pl.ds(pl.multiple_of(i * CY, CY), CY), :]
            s[f, x, 48:56, :] = zeros[:8]
        code[x, 0:16, :] = zeros[:16] + 2.0
        code[x, 16:48, :] = material[pl.ds(pl.multiple_of(i * CY, CY), CY), :].astype(jnp.float32)
        code[x, 48:64, :] = zeros[:16] + 2.0
        return carry

    lax.fori_loop(0, CX, own, 0, unroll=2)
    sflat = s.reshape(FIELDS, FX * FY, CZ)
    cflat = code.reshape(FX * FY, CZ)

    def put(f, start, size, value):
        if f < FIELDS:
            sflat[f, pl.ds(start, size, stride=FY), :] = value
        else:
            cflat[pl.ds(start, size, stride=FY), :] = value

    def rows(first_x, ref):
        for i in range(4):
            for f in range(FIELDS):
                s[f, first_x + i, 16:48, :] = ref[f, i]
            code[first_x + i, 16:48, :] = ref[FIELDS, i]

    @pl.when(row > 0)
    def _():
        rows(0, above)

    @pl.when(row < nrow - 1)
    def _():
        rows(FX - 4, below)

    @pl.when(col > 0)
    def _():
        for f in range(FIELDS + 1):
            for i in range(4):
                put(f, 4 * FY + FO - 4 + i, CX, low[f, i])

    @pl.when(col < ncol - 1)
    def _():
        for f in range(FIELDS + 1):
            for i in range(4):
                put(f, 4 * FY + FO + CY + i, CX, high[f, i])

    def corners(ref, is_above, is_high):
        for f in range(FIELDS + 1):
            at = 8 * is_high
            for j in range(3):
                size = 3 - j
                x = 4 - size if is_above else 4 + CX
                y = FO + CY + j if is_high else FO - 1 - j
                put(f, x * FY + y, size, ref[f, at : at + size, :])
                at += size

    for ref, is_above, in_x in ((kabove, 1, row > 0), (kbelow, 0, row < nrow - 1)):
        for is_high, in_y in ((0, col > 0), (1, col < ncol - 1)):
            pl.when(in_x & in_y)(functools.partial(corners, ref, is_above, is_high))

    def scale(x, carry):
        kind = code[x, 8:56, :]
        for f in range(FIELDS):
            inverse = inverse_of(kind, reaction, f)
            value = inverse * s[f, x, 8:56, :]
            inv[f, x, 8:56, :] = inverse
            s[f, x, 8:56, :] = value
            p0[f, x, 8:56, :] = value * (1.0 / THETA)
        return carry

    lax.fori_loop(0, FX, scale, 0)

    for k, (keep, gain) in enumerate(coefficients()):
        def sweep(x, carry):
            for f in range(FIELDS):
                here, total = beside(parts[k], f, x, 8, 48, 1)
                value = s[f, x, 8:56, :] - here + inv[f, x, 8:56, :] * total
                s[f, x, 8:56, :] = value
                parts[k + 1][f, x, 8:56, :] = keep * here + gain * value
            return carry

        lax.fori_loop(k + 1, FX - k - 1, sweep, 0)

    parity = lanes() % 2 == 0

    def finish(i, carry):
        at_y = pl.multiple_of(i * 2 * CY, 2 * CY)
        sums = []
        for f in range(FIELDS):
            fluid, solid = diagonal_values(reaction, f)
            residue = jnp.zeros((CY, CZ), jnp.float32)
            for h in range(2):
                x = i * 2 + h + 4
                here, total = beside(p3, f, x, 16, CY, 1)
                value = s[f, x, 16:48, :] - here + inv[f, x, 16:48, :] * total
                out = pl.ds(at_y + h * CY, CY)
                scaled[f, out, :] = value
                first[f, out, :] = (
                    p0[f, x, 16:48, :] + p1[f, x, 16:48, :] + p2[f, x, 16:48, :] + here
                )
                residue = residue + jnp.where(code[x, 16:48, :] == 1.0, solid, fluid) * value
            sums.append(residue)
        sums.append(code[i * 2 + 4, 16:48, :] + code[i * 2 + 5, 16:48, :])
        halves = []
        for f, value in enumerate(sums):
            pair[f] = value
            halves.append(pair[f, pl.ds(0, HY, stride=2), :] + pair[f, pl.ds(1, HY, stride=2), :])
        halves.append(halves[4])
        out = pl.ds(pl.multiple_of(i * HY, HY), HY)
        for plane in range(3):
            even, odd = halves[2 * plane], halves[2 * plane + 1]
            merged = jnp.where(
                parity, even + pltpu.roll(even, CZ - 1, 1), odd + pltpu.roll(odd, 1, 1)
            )
            coarse[plane, out, :] = merged * 0.5 if plane < 2 else merged
        return carry

    lax.fori_loop(0, HX, finish, 0)

    for f in range(FIELDS):
        for i in range(3):
            up[f, i] = scaled[f, pl.ds((CX - 3 + i) * CY, CY), :]
            down[f, i] = scaled[f, pl.ds(i * CY, CY), :]
            at = 27 * HX + (f * 3 + i) * CX
            right[at : at + CX, :] = scaled[f, pl.ds(CY - 3 + i, CX, stride=CY), :]
            left[at : at + CX, :] = scaled[f, pl.ds(i, CX, stride=CY), :]
    for plane in range(3):
        for i in range(9):
            at = (plane * 9 + i) * HX
            right[at : at + HX, :] = coarse[plane, pl.ds(HY - 9 + i, HX, stride=HY), :]
            left[at : at + HX, :] = coarse[plane, pl.ds(i, HX, stride=HY), :]


SIDE_LINES = 27 * HX + 12 * CX
KNOT_LINES = 6 * CORNER_LINES + FIELDS * 8
EDGE_LINES = 3 * 24


def pack_knots(coarse, low, high, up, down, far_up, far_down):
    for plane in range(3):
        base = plane * 24
        far_up[base : base + HY, :] = coarse[plane, (HX - 1) * HY : HX * HY, :]
        far_down[base : base + HY, :] = coarse[plane, 0:HY, :]
        far_up[base + HY : base + 24, :] = jnp.zeros((8, CZ), jnp.float32)
        far_down[base + HY : base + 24, :] = jnp.zeros((8, CZ), jnp.float32)
        for side, ref in enumerate((low, high)):
            line = (plane * 9 + (0 if side else 8)) * HX
            at = base + HY + side
            far_up[at : at + 1, :] = ref[line + HX - 1 : line + HX, :]
            far_down[at : at + 1, :] = ref[line : line + 1, :]
            base_at = (plane * 2 + side) * CORNER_LINES
            up[base_at + 40 : base_at + 48, :] = jnp.zeros((8, CZ), jnp.float32)
            down[base_at + 40 : base_at + 48, :] = jnp.zeros((8, CZ), jnp.float32)
            for j, offset in CORNER_AT.items():
                size = corner_size(j)
                line = (plane * 9 + (j - 1 if side else 9 - j)) * HX
                at = base_at + offset
                up[at : at + size, :] = ref[line + HX - size : line + HX, :]
                down[at : at + size, :] = ref[line : line + size, :]
    for f in range(FIELDS):
        base = 6 * CORNER_LINES + f * 8
        up[base : base + 8, :] = jnp.zeros((8, CZ), jnp.float32)
        down[base : base + 8, :] = jnp.zeros((8, CZ), jnp.float32)
        for side, ref in enumerate((low, high)):
            for j in range(2):
                size = 2 - j
                line = 27 * HX + (f * 3 + (j if side else 2 - j)) * CX
                at = base + side * 4 + 2 * j
                up[at : at + size, :] = ref[line + CX - size : line + CX, :]
                down[at : at + size, :] = ref[line : line + size, :]


def coarse_constants(reaction, plane):
    parity = lanes() % 2 == 0
    low = jnp.where(parity, reaction[2 * plane, 0], reaction[2 * plane + 1, 0])
    jump = jnp.where(
        parity,
        reaction[2 * plane, 1] - reaction[2 * plane, 0],
        reaction[2 * plane + 1, 1] - reaction[2 * plane + 1, 0],
    )
    return 8.0 * low, jump


def smooth_coarse(
    nrow, ncol, reaction, coarse, above, below, low, high, kabove, kbelow, far_above, far_below,
    start, scaled, inverse_out, sums,
    s, inv, count, p0, p1, p2, p3,
):
    row, col = place()
    parts = (p0, p1, p2, p3)
    zeros = jnp.zeros((QY, CZ), jnp.float32)

    def clear(x, carry):
        for plane in range(2):
            s[plane, x] = zeros
        count[x] = zeros - 1.0
        return carry

    lax.fori_loop(0, QX, clear, 0)
    sflat = s.reshape(2, QX * QY, CZ)
    cflat = count.reshape(QX * QY, CZ)

    def put(plane, start_row, size, value):
        if plane < 2:
            sflat[plane, pl.ds(start_row, size, stride=QY), :] = value
        else:
            cflat[pl.ds(start_row, size, stride=QY), :] = value

    def block(plane, x, value):
        if plane < 2:
            s[plane, x, QO : QO + HY, :] = value
        else:
            count[x, QO : QO + HY, :] = value

    def rows(first_x, ref):
        for plane in range(3):
            for i in range(HX):
                block(plane, first_x + i, ref[plane, i * HY : (i + 1) * HY, :])

    rows(9, coarse)

    @pl.when(row > 0)
    def _():
        rows(1, above)

    @pl.when(row < nrow - 1)
    def _():
        rows(9 + HX, below)

    def edge(ref, x):
        for plane in range(3):
            base = plane * 24
            block(plane, x, ref[base : base + HY, :])
            for is_high, in_y in ((0, col > 0), (1, col < ncol - 1)):
                @pl.when(in_y)
                def _():
                    y = QO + HY if is_high else QO - 1
                    at = base + HY + is_high
                    put(plane, x * QY + y, 1, ref[at : at + 1, :])

    pl.when(row > 1)(functools.partial(edge, far_above, 0))
    pl.when(row < nrow - 2)(functools.partial(edge, far_below, QX - 1))

    def side(ref, first_y):
        for plane in range(3):
            for i in range(9):
                line = (plane * 9 + i) * HX
                put(plane, 9 * QY + first_y + i, HX, ref[line : line + HX, :])

    pl.when(col > 0)(functools.partial(side, low, QO - 9))
    pl.when(col < ncol - 1)(functools.partial(side, high, QO + HY))

    def corners(ref, is_above, is_high):
        for plane in range(3):
            base = (plane * 2 + is_high) * CORNER_LINES
            for j, at in CORNER_AT.items():
                size = corner_size(j)
                x = 9 - size if is_above else 9 + HX
                y = QO + HY - 1 + j if is_high else QO - j
                put(plane, x * QY + y, size, ref[base + at : base + at + size, :])

    for ref, is_above, in_x in ((kabove, 1, row > 0), (kbelow, 0, row < nrow - 1)):
        for is_high, in_y in ((0, col > 0), (1, col < ncol - 1)):
            pl.when(in_x & in_y)(functools.partial(corners, ref, is_above, is_high))

    def scale(x, carry):
        number = count[x]
        for plane in range(2):
            low8, jump = coarse_constants(reaction, plane)
            inverse = jnp.where(number < 0.0, 0.0, 1.0 / (6.0 + 0.5 * (low8 + jump * number)))
            value = inverse * s[plane, x]
            inv[plane, x] = inverse
            s[plane, x] = value
            p0[plane, x] = value * (1.0 / THETA)
        return carry

    lax.fori_loop(0, QX, scale, 0)

    for k, (keep, gain) in enumerate(coefficients()):
        def sweep(x, carry):
            for plane in range(2):
                here, total = beside(parts[k], plane, x, 8, 32, 2)
                value = s[plane, x, 8:40, :] - here + inv[plane, x, 8:40, :] * total
                s[plane, x, 8:40, :] = value
                parts[k + 1][plane, x, 8:40, :] = keep * here + gain * value
            return carry

        lax.fori_loop(k + 1, QX - k - 1, sweep, 0)

    def finish(x, carry):
        for plane in range(2):
            here, total = beside(p3, plane, x, 8, 32, 2)
            value = s[plane, x, 8:40, :] - here + inv[plane, x, 8:40, :] * total
            scaled[plane, x - 4] = value
            inverse_out[plane, x - 4] = inv[plane, x, 8:40, :]
        return carry

    lax.fori_loop(4, QX - 4, finish, 0)

    def add(x, carry):
        for plane in range(2):
            start[plane, x - 7] = (
                p0[plane, x, 8:40, :] + p1[plane, x, 8:40, :]
                + p2[plane, x, 8:40, :] + p3[plane, x, 8:40, :]
            )
        return carry

    lax.fori_loop(7, QX - 7, add, 0)

    lane = lanes()
    message = jnp.zeros((8, CZ), jnp.float32)
    for plane in range(2):
        low8, jump = coarse_constants(reaction, plane)
        total = jnp.zeros((HY, CZ), jnp.float32)
        for x in range(9, 9 + HX):
            diagonal = 6.0 + 0.5 * (low8 + jump * count[x, QO : QO + HY, :])
            total = total + diagonal * scaled[plane, x - 4, 8 : 8 + HY, :]
        total = total[:8] + total[8:]
        for shift in (4, 2, 1):
            total = total + pltpu.roll(total, shift, 0)
        for shift in (2, 4, 8):
            total = total + pltpu.roll(total, CZ - shift, 1)
        for odd in range(2):
            for g in range(GROUPS):
                to = (2 * plane + odd) * GROUPS + g
                moved = pltpu.roll(total, (to - 16 * g - odd) % CZ, 1)
                message = jnp.where(lane == to, moved, message)
    sums[...] = jnp.broadcast_to(message[:1], sums.shape)


def smooth_second(
    nrow, ncol, reaction, gathered, mine, kin_above, kin_below, kin_low, kin_high,
    start, qscaled, qinverse, first, scaled, code, above, below, low, high, kabove, kbelow,
    out,
    wide, spread, e, q0, q1, q2, q3, qs, fs, inv, f0, p0, p1, p2, p3,
):
    row, col = place()
    lane = lanes()
    width = ncol * GROUPS
    fields = [jnp.zeros((nrow, CZ), jnp.float32) for _ in range(FIELDS)]
    for c in range(ncol):
        some = gathered[pl.ds(c, nrow, stride=ncol), :]
        for f in range(FIELDS):
            moved = pltpu.roll(some, (c * GROUPS - f * GROUPS) % CZ, 1)
            here = (lane >= c * GROUPS) & (lane < (c + 1) * GROUPS)
            fields[f] = jnp.where(here, moved, fields[f])
    for f in range(FIELDS):
        wide[f] = fields[f]

    group = lax.broadcasted_iota(jnp.int32, (GROUPS, CZ), 0)
    spot = lax.broadcasted_iota(jnp.int32, (GROUPS, CZ), 1)
    mask = [(spot // 16 == group) & (spot % 2 == odd) for odd in range(2)]
    e[...] = jnp.zeros_like(e)

    def product(rows_of, f):
        total = jnp.zeros((GROUPS, width), jnp.float32)
        for k in range(nrow):
            total = total + rows_of(f, k) * wide[f, k : k + 1, 0:width]
        return jnp.sum(total, axis=1, keepdims=True)

    def neighbour(rows_of, dx, dy):
        for plane in range(2):
            even = product(rows_of, 2 * plane)
            odd = product(rows_of, 2 * plane + 1)
            full = jnp.where(mask[0], even, jnp.where(mask[1], odd, 0.0))
            line = jnp.sum(full, axis=0, keepdims=True)
            x_from, x_to = {-1: (0, 6), 0: (6, 6 + HX), 1: (6 + HX, EX)}[dx]
            y_from, y_to = {-1: (8, QO), 0: (QO, QO + HY), 1: (QO + HY, QO + HY + 8)}[dy]
            for x in range(x_from, x_to):
                e[plane, x, y_from:y_to, :] = jnp.broadcast_to(line, (y_to - y_from, CZ))

    def slab(ref, part):
        if part is None:
            return lambda f, k: ref[f, :, k * width : (k + 1) * width]
        return lambda f, k: ref[part, f, :, k * width : (k + 1) * width]

    neighbour(slab(mine, None), 0, 0)
    in_x = {-1: row > 0, 1: row < nrow - 1}
    in_y = {-1: col > 0, 1: col < ncol - 1}
    pl.when(in_x[-1])(functools.partial(neighbour, slab(kin_above, None), -1, 0))
    pl.when(in_x[1])(functools.partial(neighbour, slab(kin_below, None), 1, 0))
    for dy, ref in ((-1, kin_low), (1, kin_high)):
        pl.when(in_y[dy])(functools.partial(neighbour, slab(ref, 0), 0, dy))
        for part, dx in ((1, -1), (2, 1)):
            pl.when(in_y[dy] & in_x[dx])(
                functools.partial(neighbour, slab(ref, part), dx, dy)
            )

    parts = (q0, q1, q2, q3)

    def begin(x, carry):
        for plane in range(2):
            here, total = beside(e, plane, x, 8, 32, 2)
            value = qscaled[plane, x - 1] - here + qinverse[plane, x - 1] * total
            qs[plane, x] = value
            q0[plane, x, 8:40, :] = value * (1.0 / THETA)
        return carry

    lax.fori_loop(1, EX - 1, begin, 0)
    for k, (keep, gain) in enumerate(coefficients()):
        def sweep(x, carry):
            for plane in range(2):
                here, total = beside(parts[k], plane, x, 8, 32, 2)
                value = qs[plane, x] - here + qinverse[plane, x - 1] * total
                qs[plane, x] = value
                parts[k + 1][plane, x, 8:40, :] = keep * here + gain * value
            return carry

        lax.fori_loop(k + 2, EX - k - 2, sweep, 0)

    parity = lane % 2 == 0

    def lift(i, carry):
        for plane in range(2):
            total = start[plane, i] + e[plane, i + 4, 8:40, :]
            total = total + q0[plane, i + 4, 8:40, :] + q1[plane, i + 4, 8:40, :]
            total = total + q2[plane, i + 4, 8:40, :] + q3[plane, i + 4, 8:40, :]
            for odd in range(2):
                if odd:
                    value = jnp.where(parity, pltpu.roll(total, CZ - 1, 1), total)
                else:
                    value = jnp.where(parity, total, pltpu.roll(total, 1, 1))
                spread[...] = value
                some = spread[4:28, :]
                for h in range(2):
                    for y in range(2):
                        f0[2 * plane + odd, i * 2 + h, pl.ds(8 + y, 24, stride=2), :] = some
        return carry

    lax.fori_loop(0, HX + 4, lift, 0)

    zeros = jnp.zeros((FY, CZ), jnp.float32)
    for x in (*range(4), *range(FX - 4, FX)):
        for f in range(FIELDS):
            fs[f, x] = zeros

    def own(i, carry):
        for f in range(FIELDS):
            fs[f, i + 4, 8:16, :] = zeros[:8]
            fs[f, i + 4, 16:48, :] = scaled[f, pl.ds(pl.multiple_of(i * CY, CY), CY), :]
            fs[f, i + 4, 48:56, :] = zeros[:8]
        return carry

    lax.fori_loop(0, CX, own, 0, unroll=2)
    sflat = fs.reshape(FIELDS, FX * FY, CZ)

    def rows(first_x, ref):
        for f in range(FIELDS):
            for i in range(3):
                fs[f, first_x + i, 16:48, :] = ref[f, i]

    pl.when(in_x[-1])(functools.partial(rows, 1, above))
    pl.when(in_x[1])(functools.partial(rows, 4 + CX, below))

    def side(ref, first_y):
        for f in range(FIELDS):
            for i in range(3):
                line = 27 * HX + (f * 3 + i) * CX
                sflat[f, pl.ds(4 * FY + first_y + i, CX, stride=FY), :] = ref[line : line + CX, :]

    pl.when(in_y[-1])(functools.partial(side, low, FO - 3))
    pl.when(in_y[1])(functools.partial(side, high, FO + CY))

    def corners(ref, is_above, is_high):
        for f in range(FIELDS):
            base = 6 * CORNER_LINES + f * 8 + is_high * 4
            for j in range(2):
                size = 2 - j
                x = 4 - size if is_above else 4 + CX
                y = FO + CY + j if is_high else FO - 1 - j
                at = base + 2 * j
                sflat[f, pl.ds(x * FY + y, size, stride=FY), :] = ref[at : at + size, :]

    for ref, is_above, dx in ((kabove, 1, -1), (kbelow, 0, 1)):
        for is_high, dy in ((0, -1), (1, 1)):
            pl.when(in_x[dx] & in_y[dy])(functools.partial(corners, ref, is_above, is_high))

    parts = (p0, p1, p2, p3)

    def open_fine(x, carry):
        kind = code[x, 8:56, :]
        for f in range(FIELDS):
            here, total = beside(f0, f, x, 8, 48, 1)
            inverse = inverse_of(kind, reaction, f)
            inv[f, x, 8:56, :] = inverse
            value = fs[f, x, 8:56, :] - here + inverse * total
            fs[f, x, 8:56, :] = value
            p0[f, x, 8:56, :] = value * (1.0 / THETA)
        return carry

    lax.fori_loop(1, FX - 1, open_fine, 0)
    for k, (keep, gain) in enumerate(coefficients()[:2]):
        def sweep(x, carry):
            for f in range(FIELDS):
                here, total = beside(parts[k], f, x, 8, 48, 1)
                value = fs[f, x, 8:56, :] - here + inv[f, x, 8:56, :] * total
                fs[f, x, 8:56, :] = value
                parts[k + 1][f, x, 8:56, :] = keep * here + gain * value
            return carry

        lax.fori_loop(k + 2, FX - k - 2, sweep, 0)

    keep, gain = coefficients()[2]

    def close(i, carry):
        x = i + 4
        at = pl.ds(pl.multiple_of(i * CY, CY), CY)
        for f in range(FIELDS):
            here, total = beside(p2, f, x, 16, CY, 1)
            value = fs[f, x, 16:48, :] - here + inv[f, x, 16:48, :] * total
            result = first[f, at, :] + f0[f, x, 16:48, :] + p0[f, x, 16:48, :]
            result = result + p1[f, x, 16:48, :] + here
            out[f, at, :] = result + (keep * here + gain * value)
        return carry

    lax.fori_loop(0, CX, close, 0)


def call(kernel, out_shapes, scratch, *args, smem=0, limit=40):
    vmem = pl.BlockSpec(memory_space=pltpu.VMEM)
    specs = [pl.BlockSpec(memory_space=pltpu.SMEM)] * smem + [vmem] * (len(args) - smem)
    return pl.pallas_call(
        kernel,
        out_shape=[jax.ShapeDtypeStruct(shape, jnp.float32) for shape in out_shapes],
        in_specs=specs,
        out_specs=[vmem] * len(out_shapes),
        scratch_shapes=[pltpu.VMEM(shape, jnp.float32) for shape in scratch],
        compiler_params=pltpu.CompilerParams(vmem_limit_bytes=limit * 1024 * 1024),
    )(*args)


def ahead(value, axis, steps=1):
    count = lax.axis_size(axis)
    return lax.ppermute(value, axis, [(i, (i + steps) % count) for i in range(count)])


def back(value, axis, steps=1):
    count = lax.axis_size(axis)
    return lax.ppermute(value, axis, [((i + steps) % count, i) for i in range(count)])


def body(right_side, material, reaction, coarse_inverse):
    nrow, ncol = lax.axis_size("row"), lax.axis_size("col")
    b = right_side.reshape(FIELDS, CX * CY, CZ)
    material = material.reshape(CX * CY, CZ)

    x_layer, y_layer = (FIELDS + 1, 4, CY, CZ), (FIELDS + 1, 4, CX, CZ)
    up, down, right, left = call(
        pack_layers, [x_layer, x_layer, y_layer, y_layer], [], b, material
    )
    above, below = ahead(up, "row"), back(down, "row")
    low, high = ahead(right, "col"), back(left, "col")
    up, down = call(pack_corners, [(FIELDS + 1, 16, CZ)] * 2, [], low, high)
    kabove, kbelow = ahead(up, "row"), back(down, "row")

    kin_above, kin_below = ahead(coarse_inverse, "row"), back(coarse_inverse, "row")
    kin = jnp.stack([coarse_inverse, kin_above, kin_below])
    kin_low, kin_high = ahead(kin, "col"), back(kin, "col")

    fine = (FIELDS, CX * CY, CZ)
    padded = (FIELDS, FX, FY, CZ)
    x_layer = (FIELDS, 3, CY, CZ)
    first, scaled, code, coarse, up, down, right, left = call(
        functools.partial(smooth_first, nrow, ncol),
        [fine, fine, padded[1:], (3, HX * HY, CZ), x_layer, x_layer]
        + [(SIDE_LINES, CZ)] * 2,
        [padded] * 6 + [(FIELDS + 1, CY, CZ)],
        reaction, b, material, above, below, low, high, kabove, kbelow,
        smem=1,
    )

    qabove, qbelow = ahead(coarse, "row"), back(coarse, "row")
    low, high = ahead(right, "col"), back(left, "col")
    above, below = ahead(up, "row"), back(down, "row")
    up, down, far_up, far_down = call(
        pack_knots, [(KNOT_LINES, CZ)] * 2 + [(EDGE_LINES, CZ)] * 2, [], coarse, low, high
    )
    kabove, kbelow = ahead(up, "row"), back(down, "row")
    far_above, far_below = ahead(far_up, "row", 2), back(far_down, "row", 2)

    qpadded = (2, QX, QY, CZ)
    start, qscaled, qinverse, sums = call(
        functools.partial(smooth_coarse, nrow, ncol),
        [(2, HX + 4, 32, CZ), (2, HX + 10, 32, CZ), (2, HX + 10, 32, CZ), (nrow * ncol, CZ)],
        [qpadded, qpadded, qpadded[1:]] + [qpadded] * 4,
        reaction, coarse, qabove, qbelow, low, high, kabove, kbelow, far_above, far_below,
        smem=1,
    )

    gathered = lax.all_to_all(sums, ("row", "col"), 0, 0)

    epadded = (2, EX, QY, CZ)
    (out,) = call(
        functools.partial(smooth_second, nrow, ncol),
        [fine],
        [(FIELDS, nrow, CZ), (32, CZ)] + [epadded] * 5 + [(2, EX, 32, CZ)] + [padded] * 7,
        reaction, gathered, coarse_inverse, kin_above, kin_below, kin_low, kin_high,
        start, qscaled, qinverse, first, scaled, code, above, below, low, high, kabove, kbelow,
        smem=1, limit=48,
    )
    return out.reshape(right_side.shape)


def solution(mesh):
    placed = (
        P(None, "row", "col", None),
        P("row", "col", None),
        P(),
        P(None, ("row", "col"), None),
    )
    return jax.shard_map(
        body, mesh=mesh, in_specs=placed, out_specs=P(None, "row", "col", None), check_vma=False
    )
```

time: 466 us -> 117 us (0.25)
  the two profiles are of different devices: /device:TPU:34 before, /device:TPU:1 now
where the time goes in v1:
time: 117 us; the launch traced here: 116 us
  Pallas kernels  42.2 us (36%)
  starting transfers between devices  38.6 us (33%)
  waiting for transfers between devices  20 us (17%)
  local copies, waits for them, and re-layouts  13.5 us (12%)
  other arithmetic  1.81 us (2%)
    pallas_call x6, Pallas kernels, call(): pl.pallas_call(kernel, out_shape=[jax.ShapeDtypeStruct(shape, jnp.float32...  42.2 us
    ppermute x10, starting transfers between devices, back(): lax.ppermute(value, axis, [((i + steps) % count, i) for i in range(count)])  19.8 us
    unnamed x37, local copies, waits for them, and re-layouts  13.5 us
    ppermute x10, starting transfers between devices, ahead(): lax.ppermute(value, axis, [(i, (i + steps) % count) for i in range(count)])  12.4 us
    all_to_all x1, waiting for transfers between devices, body(): gathered = lax.all_to_all(sums, ('row', 'col'), 0, 0)  9.74 us
    all_to_all x1, starting transfers between devices, body(): gathered = lax.all_to_all(sums, ('row', 'col'), 0, 0)  6.34 us
    ppermute x10, waiting for transfers between devices, ahead(): lax.ppermute(value, axis, [(i, (i + steps) % count) for i in range(count)])  6.14 us
    ppermute x10, waiting for transfers between devices, back(): lax.ppermute(value, axis, [((i + steps) % count, i) for i in range(count)])  4.09 us
  transfers between devices with their start and end apart: 21, of which 5 were waited for; matrix products, arithmetic and copies ran while one was open for 2% of the time, Pallas kernels for 19%

profile of v1, /device:TPU:1, one launch (start us, length us, event | category | flops | bytes accessed | tf_op | source)
XLA Modules:
  0.0 116.1 jit_solution(7982298199813573893)
XLA Ops:
  0.0 1.2 %copy-done = f32[4,16,32,128]{3,2,1,0:T(8,128)S(1)} copy-done((f32[4,16,32,128]{3,2,1,0:T(8,128)S(1)}, f32[4,16,32,128]{3,2,1,0:T(8,128)}, u32[]{:S(2)}) %copy-start) | copy-done | bytes 1048600
  1.2 0.9 copy-done.3
  2.2 0.2 shard_map.46
  2.4 0.0 copy-start.4
  2.4 2.6 %collective-permute-start = (f32[5,4,32,128]{3,2,1,0:T(8,128)S(1)}, f32[5,4,32,128]{3,2,1,0:T(8,128)S(1)}, u32[]{:S(2)}, u32[]{:S(2)}) collective-permute-start(f32[5,4,32,128]{3,2,1,0:T(8,128)S(1)} %get-tuple-element.27), channel_id=1, source_target_pairs={{0,16},{16,32},{32,48},{48,64},{64,80},{80,96},{96,112},{112,0},{1... | collective-permute-start | bytes 983048 | tf_op jit(solution)/shard_map/ppermute | solution.py:648
  5.0 0.0 collective-permute-start.1
  5.0 1.3 %collective-permute-start.2 = (f32[5,4,16,128]{3,2,1,0:T(8,128)S(1)}, f32[5,4,16,128]{3,2,1,0:T(8,128)S(1)}, u32[]{:S(2)}, u32[]{:S(2)}) collective-permute-start(f32[5,4,16,128]{3,2,1,0:T(8,128)S(1)} %get-tuple-element.29), channel_id=1, source_target_pairs={{0,1},{1,2},{2,3},{3,4},{4,5},{5,6},{6,7},{7,8},{8,9},{9,10},{10,1... | collective-permute-start | bytes 491528 | tf_op jit(solution)/shard_map/ppermute | solution.py:648
  6.3 4.9 %collective-permute-start.3 = (f32[5,4,16,128]{3,2,1,0:T(8,128)S(1)}, f32[5,4,16,128]{3,2,1,0:T(8,128)S(1)}, u32[]{:S(2)}, u32[]{:S(2)}) collective-permute-start(f32[5,4,16,128]{3,2,1,0:T(8,128)S(1)} %get-tuple-element.30), channel_id=1, source_target_pairs={{1,0},{2,1},{3,2},{4,3},{5,4},{6,5},{7,6},{8,7},{9,8},{10,9},{11,1... | collective-permute-start | bytes 491528 | tf_op jit(solution)/shard_map/ppermute | solution.py:653
  11.2 2.7 %collective-permute-done.2.low = f32[5,4,16,128]{3,2,1,0:T(8,128)S(1)} collective-permute-done((f32[5,4,16,128]{3,2,1,0:T(8,128)S(1)}, f32[5,4,16,128]{3,2,1,0:T(8,128)S(1)}, u32[]{:S(2)}, u32[]{:S(2)}) %collective-permute-start.2) | collective-permute-done | bytes 163872 | tf_op jit(solution)/shard_map/ppermute | solution.py:648
  13.9 0.0 collective-permute-done.3.high
  14.0 0.0 copy-start.17
  14.0 3.6 %collective-permute-start.4 = (f32[5,16,128]{2,1,0:T(8,128)S(1)}, f32[5,16,128]{2,1,0:T(8,128)S(1)}, u32[]{:S(2)}, u32[]{:S(2)}) collective-permute-start(f32[5,16,128]{2,1,0:T(8,128)S(1)} %get-tuple-element.31), channel_id=1, source_target_pairs={{0,16},{16,32},{32,48},{48,64},{64,80},{80,96},{96,112},{112,0},{1... | collective-permute-start | bytes 122888 | tf_op jit(solution)/shard_map/ppermute | solution.py:648
  17.5 0.0 collective-permute-start.15
  17.5 1.7 %collective-permute-start.14 = (f32[4,8,1024]{2,1,0:T(8,128)}, f32[4,8,1024]{2,1,0:T(8,128)}, u32[]{:S(2)}, u32[]{:S(2)}) collective-permute-start(f32[4,8,1024]{2,1,0:T(8,128)} %mine.1), channel_id=1, source_target_pairs={{0,16},{16,32},{32,48},{48,64},{64,80},{80,96},{96,112},{112,0},{1... | collective-permute-start | bytes 393224 | tf_op jit(solution)/shard_map/ppermute | solution.py:648
  19.3 0.0 collective-permute-done.4.kabove
  19.3 2.1 %collective-permute-start.5 = (f32[5,16,128]{2,1,0:T(8,128)S(1)}, f32[5,16,128]{2,1,0:T(8,128)S(1)}, u32[]{:S(2)}, u32[]{:S(2)}) collective-permute-start(f32[5,16,128]{2,1,0:T(8,128)S(1)} %get-tuple-element.32), channel_id=1, source_target_pairs={{16,0},{32,16},{48,32},{64,48},{80,64},{96,80},{112,96},{0,112},{1... | collective-permute-start | bytes 122888 | tf_op jit(solution)/shard_map/ppermute | solution.py:653
  21.4 0.7 copy.11.reaction
  22.0 0.7 collective-permute-done.5.kbelow
  22.7 0.0 collective-permute-done.above
  22.7 0.7 copy-done.11
  23.4 0.7 copy-done.13
  24.2 1.0 copy-done.12
  25.2 1.0 copy-done.14
  26.1 0.7 copy-done.15
  26.8 11.9 %shard_map.48 = (f32[4,512,128]{2,1,0:T(8,128)S(1)}, f32[4,512,128]{2,1,0:T(8,128)S(1)}, f32[24,64,128]{2,1,0:T(8,128)S(1)}, f32[3,128,128]{2,1,0:T(8,128)S(1)},...) custom-call(f32[4,2]{1,0:T(4,128)S(1)} %copy-done.15, ...), custom_call_target="tpu_custom_call" | custom-call | tf_op jit(solution)/shard_map/pallas_call | solution.py:636
  38.8 1.0 copy-done.2
  39.7 4.8 %collective-permute-start.9 = (f32[408,128]{1,0:T(8,128)S(1)}, f32[408,128]{1,0:T(8,128)S(1)}, u32[]{:S(2)}, u32[]{:S(2)}) collective-permute-start(f32[408,128]{1,0:T(8,128)S(1)} %get-tuple-element.35), channel_id=1, source_target_pairs={{1,0},{2,1},{3,2},{4,3},{5,4},{6,5},{7,6},{8,7},{9,8},{10,9},{11,1... | collective-permute-start | bytes 626696 | tf_op jit(solution)/shard_map/ppermute | solution.py:653
  44.5 2.1 %collective-permute-start.7 = (f32[3,128,128]{2,1,0:T(8,128)S(1)}, f32[3,128,128]{2,1,0:T(8,128)S(1)}, u32[]{:S(2)}, u32[]{:S(2)}) collective-permute-start(f32[3,128,128]{2,1,0:T(8,128)S(1)} %get-tuple-element.33.coarse), channel_id=1, source_target_pairs={{16,0},{32,16},{48,32},{64,48},{80,64},{96,80},{112,96},{0,112},{1... | collective-permute-start | bytes 589832 | tf_op jit(solution)/shard_map/ppermute | solution.py:653
  46.7 1.8 %pad_maximum_fusion = f32[3,4,8,1024]{3,2,1,0:T(8,128)} fusion(f32[1,4,8,1024]{3,2,1,0:T(8,128)} %bitcast.7, f32[1,4,8,1024]{3,2,1,0:T(8,128)} %bitcast.6, f32[1,4,8,1024]{3,2,1,0:T(8,128)} %bitcast.5), kind=kLoop, calls=%fused_computation | loop fusion | flops 196608 | bytes 786432 | tf_op jit(solution)/shard_map/stack | solution.py:671
  48.5 1.7 %collective-permute-start.17 = (f32[3,4,8,1024]{3,2,1,0:T(8,128)}, f32[3,4,8,1024]{3,2,1,0:T(8,128)S(1)}, u32[]{:S(2)}, u32[]{:S(2)}) collective-permute-start(f32[3,4,8,1024]{3,2,1,0:T(8,128)} %pad_maximum_fusion), channel_id=1, source_target_pairs={{1,0},{2,1},{3,2},{4,3},{5,4},{6,5},{7,6},{8,7},{9,8},{10,9},{11,1... | collective-permute-start | bytes 1179656 | tf_op jit(solution)/shard_map/ppermute | solution.py:653
  50.2 0.1 shard_map.49
  50.3 0.5 collective-permute-start.10
  50.8 0.0 collective-permute-done.7.below
  50.8 1.0 collective-permute-start.12
  51.8 4.1 %collective-permute-start.13 = (f32[72,128]{1,0:T(8,128)S(1)}, f32[72,128]{1,0:T(8,128)S(1)}, u32[]{:S(2)}, u32[]{:S(2)}) collective-permute-start(f32[72,128]{1,0:T(8,128)S(1)} %get-tuple-element.39), channel_id=1, source_target_pairs={{32,0},{48,16},{64,32},{80,48},{96,64},{112,80},{0,96},{16,112},{3... | collective-permute-start | bytes 110600 | tf_op jit(solution)/shard_map/ppermute | solution.py:653
  55.9 3.4 %collective-permute-done.12.far_above = f32[72,128]{1,0:T(8,128)S(1)} collective-permute-done((f32[72,128]{1,0:T(8,128)S(1)}, f32[72,128]{1,0:T(8,128)S(1)}, u32[]{:S(2)}, u32[]{:S(2)}) %collective-permute-start.12) | collective-permute-done | bytes 36896 | tf_op jit(solution)/shard_map/ppermute | solution.py:648
  59.3 1.7 %collective-permute-start.18 = (f32[4,3,32,128]{3,2,1,0:T(8,128)}, f32[4,3,32,128]{3,2,1,0:T(8,128)}, u32[]{:S(2)}, u32[]{:S(2)}) collective-permute-start(f32[4,3,32,128]{3,2,1,0:T(8,128)} %get-tuple-element.47), channel_id=1, source_target_pairs={{0,16},{16,32},{32,48},{48,64},{64,80},{80,96},{96,112},{112,0},{1... | collective-permute-start | bytes 589832 | tf_op jit(solution)/shard_map/ppermute | solution.py:648
  61.1 3.4 %collective-permute-done.11.kbelow = f32[320,128]{1,0:T(8,128)S(1)} collective-permute-done((f32[320,128]{1,0:T(8,128)S(1)}, f32[320,128]{1,0:T(8,128)S(1)}, u32[]{:S(2)}, u32[]{:S(2)}) %collective-permute-start.11) | collective-permute-done | bytes 163872 | tf_op jit(solution)/shard_map/ppermute | solution.py:653
  64.5 10.5 %shard_map.50 = (f32[2,12,32,128]{3,2,1,0:T(8,128)S(1)}, f32[2,18,32,128]{3,2,1,0:T(8,128)S(1)}, f32[2,18,32,128]{3,2,1,0:T(8,128)S(1)}, f32[128,128]{1,0:T(8,128)}) custom-call(f32[4,2]{1,0:T(4,128)S(1)} %copy-done.16, f32[3,128,128]{2,1,0:T(8,128)S(1)} %get-tuple-element.33.coarse, f32[3,128,128]{2,1,0:T(8,128)S(1)} %collective-permute-done.6.above, ...), custom_call_target="tpu_custom_call" | custom-call | tf_op jit(solution)/shard_map/pallas_call | solution.py:636
  74.9 0.8 copy-done.5
  75.7 0.8 copy-done.7
  76.6 0.8 copy-done.9
  77.4 6.3 %all-to-all-start = ((f32[128,1,128]{2,1,0:T(1,128)}), f32[128,1,128]{2,1,0:T(1,128)S(1)}, u32[]{:S(2)}, u32[]{:S(2)}) async-start(f32[128,1,128]{2,1,0:T(1,128)} %bitcast.3), calls=%async_computation | async-start | bytes 131072 | tf_op jit(solution)/shard_map/all_to_all | solution.py:704
  83.7 9.7 %all-to-all-done = f32[128,1,128]{2,1,0:T(1,128)S(1)} async-done(((f32[128,1,128]{2,1,0:T(1,128)}), f32[128,1,128]{2,1,0:T(1,128)S(1)}, u32[]{:S(2)}, u32[]{:S(2)}) %all-to-all-start) | async-done | bytes 65568 | tf_op jit(solution)/shard_map/all_to_all | solution.py:704
  93.5 1.1 copy-done.6
  94.6 1.1 copy-done.8
  95.6 1.0 copy-done.10
  96.6 19.5 %shard_map.51 = f32[4,512,128]{2,1,0:T(8,128)} custom-call(f32[4,2]{1,0:T(4,128)S(1)} %copy-done.16, f32[128,128]{1,0:T(8,128)S(1)} %bitcast.14, f32[4,8,1024]{2,1,0:T(8,128)} %mine.1, f32[4,8,1024]{2,1,0:T(8,128)} %collective-permute-done.14.kin_above, f32[4,8,1024]{2,1,0:T(8,128)} %collective-permute-done.15.kin_below, ...), custom_call_target="tpu_custom_call" | custom-call | tf_op jit(solution)/shard_map/pallas_call | solution.py:636
  (38 shorter events, 0.1 us)
Async XLA Ops:
  0.0 1.2 %copy-start = (f32[4,16,32,128]{3,2,1,0:T(8,128)S(1)}, f32[4,16,32,128]{3,2,1,0:T(8,128)}, u32[]{:S(2)}) copy-start(f32[4,16,32,128]{3,2,1,0:T(8,128)} %param.4) | copy-start | bytes 3145732
  1.2 0.9 copy-start.3
  2.2 22.0 %copy-start.1 = (f32[4,16,32,128]{3,2,1,0:T(8,128)S(1)}, f32[4,16,32,128]{3,2,1,0:T(8,128)}, u32[]{:S(2)}) copy-start(f32[4,16,32,128]{3,2,1,0:T(8,128)} %param.4) | copy-start | bytes 3145732
  2.4 21.8 %copy-start.4 = (s32[16,32,128]{2,1,0:T(8,128)S(1)}, s32[16,32,128]{2,1,0:T(8,128)}, u32[]{:S(2)}) copy-start(s32[16,32,128]{2,1,0:T(8,128)} %param.5) | copy-start | bytes 786436
  2.4 20.3 %collective-permute-start = (f32[5,4,32,128]{3,2,1,0:T(8,128)S(1)}, f32[5,4,32,128]{3,2,1,0:T(8,128)S(1)}, u32[]{:S(2)}, u32[]{:S(2)}) collective-permute-start(f32[5,4,32,128]{3,2,1,0:T(8,128)S(1)} %get-tuple-element.27), channel_id=1, source_target_pairs={{0,16},{16,32},{32,48},{48,64},{64,80},{80,96},{96,112},{112,0},{1... | collective-permute-start | bytes 983048 | tf_op jit(solution)/shard_map/ppermute | solution.py:648
  5.0 18.4 %collective-permute-start.1 = (f32[5,4,32,128]{3,2,1,0:T(8,128)S(1)}, f32[5,4,32,128]{3,2,1,0:T(8,128)S(1)}, u32[]{:S(2)}, u32[]{:S(2)}) collective-permute-start(f32[5,4,32,128]{3,2,1,0:T(8,128)S(1)} %get-tuple-element.28), channel_id=1, source_target_pairs={{16,0},{32,16},{48,32},{64,48},{80,64},{96,80},{112,96},{0,112},{1... | collective-permute-start | bytes 983048 | tf_op jit(solution)/shard_map/ppermute | solution.py:653
  5.0 8.9 %collective-permute-start.2 = (f32[5,4,16,128]{3,2,1,0:T(8,128)S(1)}, f32[5,4,16,128]{3,2,1,0:T(8,128)S(1)}, u32[]{:S(2)}, u32[]{:S(2)}) collective-permute-start(f32[5,4,16,128]{3,2,1,0:T(8,128)S(1)} %get-tuple-element.29), channel_id=1, source_target_pairs={{0,1},{1,2},{2,3},{3,4},{4,5},{5,6},{6,7},{7,8},{8,9},{9,10},{10,1... | collective-permute-start | bytes 491528 | tf_op jit(solution)/shard_map/ppermute | solution.py:648
  6.3 7.6 %collective-permute-start.3 = (f32[5,4,16,128]{3,2,1,0:T(8,128)S(1)}, f32[5,4,16,128]{3,2,1,0:T(8,128)S(1)}, u32[]{:S(2)}, u32[]{:S(2)}) collective-permute-start(f32[5,4,16,128]{3,2,1,0:T(8,128)S(1)} %get-tuple-element.30), channel_id=1, source_target_pairs={{1,0},{2,1},{3,2},{4,3},{5,4},{6,5},{7,6},{8,7},{9,8},{10,9},{11,1... | collective-permute-start | bytes 491528 | tf_op jit(solution)/shard_map/ppermute | solution.py:653
  14.0 7.4 %copy-start.17 = (f32[4,2]{0,1:T(2,128)S(1)}, f32[4,2]{0,1:T(2,128)}, u32[]{:S(2)}) copy-start(f32[4,2]{0,1:T(2,128)} %param.6) | copy-start | bytes 100
  14.0 5.3 %collective-permute-start.4 = (f32[5,16,128]{2,1,0:T(8,128)S(1)}, f32[5,16,128]{2,1,0:T(8,128)S(1)}, u32[]{:S(2)}, u32[]{:S(2)}) collective-permute-start(f32[5,16,128]{2,1,0:T(8,128)S(1)} %get-tuple-element.31), channel_id=1, source_target_pairs={{0,16},{16,32},{32,48},{48,64},{64,80},{80,96},{96,112},{112,0},{1... | collective-permute-start | bytes 122888 | tf_op jit(solution)/shard_map/ppermute | solution.py:648
  17.5 29.1 %collective-permute-start.15 = (f32[4,8,1024]{2,1,0:T(8,128)}, f32[4,8,1024]{2,1,0:T(8,128)}, u32[]{:S(2)}, u32[]{:S(2)}) collective-permute-start(f32[4,8,1024]{2,1,0:T(8,128)} %mine.1), channel_id=1, source_target_pairs={{16,0},{32,16},{48,32},{64,48},{80,64},{96,80},{112,96},{0,112},{1... | collective-permute-start | bytes 393224 | tf_op jit(solution)/shard_map/ppermute | solution.py:653
  17.5 29.1 %collective-permute-start.14 = (f32[4,8,1024]{2,1,0:T(8,128)}, f32[4,8,1024]{2,1,0:T(8,128)}, u32[]{:S(2)}, u32[]{:S(2)}) collective-permute-start(f32[4,8,1024]{2,1,0:T(8,128)} %mine.1), channel_id=1, source_target_pairs={{0,16},{16,32},{32,48},{48,64},{64,80},{80,96},{96,112},{112,0},{1... | collective-permute-start | bytes 393224 | tf_op jit(solution)/shard_map/ppermute | solution.py:648
  19.3 3.4 %collective-permute-start.5 = (f32[5,16,128]{2,1,0:T(8,128)S(1)}, f32[5,16,128]{2,1,0:T(8,128)S(1)}, u32[]{:S(2)}, u32[]{:S(2)}) collective-permute-start(f32[5,16,128]{2,1,0:T(8,128)S(1)} %get-tuple-element.32), channel_id=1, source_target_pairs={{16,0},{32,16},{48,32},{64,48},{80,64},{96,80},{112,96},{0,112},{1... | collective-permute-start | bytes 122888 | tf_op jit(solution)/shard_map/ppermute | solution.py:653
  22.7 0.7 copy-start.11
  23.4 0.7 copy-start.13
  24.2 1.0 copy-start.12
  25.2 1.0 copy-start.14
  26.1 0.7 copy-start.15
  38.8 1.0 copy-start.2
  39.7 10.5 %collective-permute-start.8 = (f32[408,128]{1,0:T(8,128)S(1)}, f32[408,128]{1,0:T(8,128)S(1)}, u32[]{:S(2)}, u32[]{:S(2)}) collective-permute-start(f32[408,128]{1,0:T(8,128)S(1)} %get-tuple-element.34), channel_id=1, source_target_pairs={{0,1},{1,2},{2,3},{3,4},{4,5},{5,6},{6,7},{7,8},{8,9},{9,10},{10,1... | collective-permute-start | bytes 626696 | tf_op jit(solution)/shard_map/ppermute | solution.py:648
  39.7 10.5 %collective-permute-start.9 = (f32[408,128]{1,0:T(8,128)S(1)}, f32[408,128]{1,0:T(8,128)S(1)}, u32[]{:S(2)}, u32[]{:S(2)}) collective-permute-start(f32[408,128]{1,0:T(8,128)S(1)} %get-tuple-element.35), channel_id=1, source_target_pairs={{1,0},{2,1},{3,2},{4,3},{5,4},{6,5},{7,6},{8,7},{9,8},{10,9},{11,1... | collective-permute-start | bytes 626696 | tf_op jit(solution)/shard_map/ppermute | solution.py:653
  44.5 6.3 %collective-permute-start.7 = (f32[3,128,128]{2,1,0:T(8,128)S(1)}, f32[3,128,128]{2,1,0:T(8,128)S(1)}, u32[]{:S(2)}, u32[]{:S(2)}) collective-permute-start(f32[3,128,128]{2,1,0:T(8,128)S(1)} %get-tuple-element.33.coarse), channel_id=1, source_target_pairs={{16,0},{32,16},{48,32},{64,48},{80,64},{96,80},{112,96},{0,112},{1... | collective-permute-start | bytes 589832 | tf_op jit(solution)/shard_map/ppermute | solution.py:653
  46.7 5.1 %collective-permute-start.6 = (f32[3,128,128]{2,1,0:T(8,128)S(1)}, f32[3,128,128]{2,1,0:T(8,128)S(1)}, u32[]{:S(2)}, u32[]{:S(2)}) collective-permute-start(f32[3,128,128]{2,1,0:T(8,128)S(1)} %get-tuple-element.33.coarse), channel_id=1, source_target_pairs={{0,16},{16,32},{32,48},{48,64},{64,80},{80,96},{96,112},{112,0},{1... | collective-permute-start | bytes 589832 | tf_op jit(solution)/shard_map/ppermute | solution.py:648
  48.5 35.2 %collective-permute-start.17 = (f32[3,4,8,1024]{3,2,1,0:T(8,128)}, f32[3,4,8,1024]{3,2,1,0:T(8,128)S(1)}, u32[]{:S(2)}, u32[]{:S(2)}) collective-permute-start(f32[3,4,8,1024]{3,2,1,0:T(8,128)} %pad_maximum_fusion), channel_id=1, source_target_pairs={{1,0},{2,1},{3,2},{4,3},{5,4},{6,5},{7,6},{8,7},{9,8},{10,9},{11,1... | collective-permute-start | bytes 1179656 | tf_op jit(solution)/shard_map/ppermute | solution.py:653
  50.2 33.5 %collective-permute-start.16 = (f32[3,4,8,1024]{3,2,1,0:T(8,128)}, f32[3,4,8,1024]{3,2,1,0:T(8,128)S(1)}, u32[]{:S(2)}, u32[]{:S(2)}) collective-permute-start(f32[3,4,8,1024]{3,2,1,0:T(8,128)} %pad_maximum_fusion), channel_id=1, source_target_pairs={{0,1},{1,2},{2,3},{3,4},{4,5},{5,6},{6,7},{7,8},{8,9},{9,10},{10,1... | collective-permute-start | bytes 1179656 | tf_op jit(solution)/shard_map/ppermute | solution.py:648
  50.3 10.8 %collective-permute-start.10 = (f32[320,128]{1,0:T(8,128)S(1)}, f32[320,128]{1,0:T(8,128)S(1)}, u32[]{:S(2)}, u32[]{:S(2)}) collective-permute-start(f32[320,128]{1,0:T(8,128)S(1)} %get-tuple-element.36), channel_id=1, source_target_pairs={{0,16},{16,32},{32,48},{48,64},{64,80},{80,96},{96,112},{112,0},{1... | collective-permute-start | bytes 491528 | tf_op jit(solution)/shard_map/ppermute | solution.py:648
  50.8 8.5 %collective-permute-start.12 = (f32[72,128]{1,0:T(8,128)S(1)}, f32[72,128]{1,0:T(8,128)S(1)}, u32[]{:S(2)}, u32[]{:S(2)}) collective-permute-start(f32[72,128]{1,0:T(8,128)S(1)} %get-tuple-element.38), channel_id=1, source_target_pairs={{0,32},{16,48},{32,64},{48,80},{64,96},{80,112},{96,0},{112,16},{1... | collective-permute-start | bytes 110600 | tf_op jit(solution)/shard_map/ppermute | solution.py:648
  51.8 7.5 %collective-permute-start.13 = (f32[72,128]{1,0:T(8,128)S(1)}, f32[72,128]{1,0:T(8,128)S(1)}, u32[]{:S(2)}, u32[]{:S(2)}) collective-permute-start(f32[72,128]{1,0:T(8,128)S(1)} %get-tuple-element.39), channel_id=1, source_target_pairs={{32,0},{48,16},{64,32},{80,48},{96,64},{112,80},{0,96},{16,112},{3... | collective-permute-start | bytes 110600 | tf_op jit(solution)/shard_map/ppermute | solution.py:653
  59.3 5.1 %copy-start.16 = (f32[4,2]{1,0:T(4,128)S(1)}, f32[4,2]{1,0:T(4,128)}, u32[]{:S(2)}) copy-start(f32[4,2]{1,0:T(4,128)} %copy.11.reaction) | copy-start | bytes 100
  59.3 5.1 %collective-permute-start.11 = (f32[320,128]{1,0:T(8,128)S(1)}, f32[320,128]{1,0:T(8,128)S(1)}, u32[]{:S(2)}, u32[]{:S(2)}) collective-permute-start(f32[320,128]{1,0:T(8,128)S(1)} %get-tuple-element.37), channel_id=1, source_target_pairs={{16,0},{32,16},{48,32},{64,48},{80,64},{96,80},{112,96},{0,112},{1... | collective-permute-start | bytes 491528 | tf_op jit(solution)/shard_map/ppermute | solution.py:653
  59.3 24.4 %collective-permute-start.18 = (f32[4,3,32,128]{3,2,1,0:T(8,128)}, f32[4,3,32,128]{3,2,1,0:T(8,128)}, u32[]{:S(2)}, u32[]{:S(2)}) collective-permute-start(f32[4,3,32,128]{3,2,1,0:T(8,128)} %get-tuple-element.47), channel_id=1, source_target_pairs={{0,16},{16,32},{32,48},{48,64},{64,80},{80,96},{96,112},{112,0},{1... | collective-permute-start | bytes 589832 | tf_op jit(solution)/shard_map/ppermute | solution.py:648
  61.1 22.7 %collective-permute-start.19 = (f32[4,3,32,128]{3,2,1,0:T(8,128)}, f32[4,3,32,128]{3,2,1,0:T(8,128)}, u32[]{:S(2)}, u32[]{:S(2)}) collective-permute-start(f32[4,3,32,128]{3,2,1,0:T(8,128)} %get-tuple-element.48), channel_id=1, source_target_pairs={{16,0},{32,16},{48,32},{64,48},{80,64},{96,80},{112,96},{0,112},{1... | collective-permute-start | bytes 589832 | tf_op jit(solution)/shard_map/ppermute | solution.py:653
  74.9 0.8 copy-start.5
  75.7 0.8 copy-start.7
  76.6 0.8 copy-start.9
  77.4 16.1 %all-to-all-start = ((f32[128,1,128]{2,1,0:T(1,128)}), f32[128,1,128]{2,1,0:T(1,128)S(1)}, u32[]{:S(2)}, u32[]{:S(2)}) async-start(f32[128,1,128]{2,1,0:T(1,128)} %bitcast.3), calls=%async_computation | async-start | bytes 131072 | tf_op jit(solution)/shard_map/all_to_all | solution.py:704
  93.5 1.1 copy-start.6
  94.6 1.1 copy-start.8
  95.6 1.0 copy-start.10

commit v2 on v1

v2 whole, which is shorter than its diff:
```python
import functools

import jax
import jax.numpy as jnp
from jax import lax
from jax.experimental import pallas as pl
from jax.experimental.pallas import tpu as pltpu
from jax.sharding import PartitionSpec as P

FIELDS = 4
CX, CY, CZ = 16, 32, 128
HX, HY = CX // 2, CY // 2
GROUPS = 8
SWEEPS = 4
LOW_BOUND = 0.25
HIGH_BOUND = 2.0
THETA = (HIGH_BOUND + LOW_BOUND) / 2.0
DELTA = (HIGH_BOUND - LOW_BOUND) / 2.0

WX = CX + 4
GX, FY, FO = CX + 12, CY + 32, 16
FX = CX + 8
VX = HX + 2
QX, QY, QO = HX + 18, HY + 32, 16
EX = HX + 12
CORNER_AT = {1: 0, 2: 9, 3: 17, 4: 24, 5: 30, 6: 35, 7: 39, 8: 42, 9: 44}
CORNER_LINES = 48
FINE_CORNER_AT = {1: 0, 2: 5, 3: 9, 4: 12}

LAYER_LINES = (FIELDS + 1) * 6 * CY
BAND_LINES = (FIELDS + 1) * 4 * CX
KIN_LINES = FIELDS * GROUPS * 8
COARSE_LINES = 3 * (HX + 1) * HY
FACE_LINES = COARSE_LINES + FIELDS * CY
STRIP_LINES = 272
STRIP_AT = {1: 0, 2: WX, 3: 2 * WX - 2}
SIDE_LINES = STRIP_LINES + FIELDS * (3 * WX - 6)
KNOT_LINES = 6 * CORNER_LINES


def coefficients():
    rho = DELTA / THETA
    pairs = []
    for _ in range(SWEEPS - 1):
        following = 1.0 / (2.0 * THETA / DELTA - rho)
        pairs.append((following * rho, 2.0 * following / DELTA))
        rho = following
    return pairs


def every(low, high, step):
    for i in range(low, high):
        step(i)


def lanes():
    return lax.broadcasted_iota(jnp.int32, (1, CZ), 1)


def beside(ref, f, x, low, count, width):
    here = ref[f, x, low : low + count, :]
    lane = lanes()
    total = ref[f, x + 1, low : low + count, :] + ref[f, x - 1, low : low + count, :]
    total = total + ref[f, x, low + 1 : low + 1 + count, :]
    total = total + ref[f, x, low - 1 : low - 1 + count, :]
    total = total + jnp.where(lane < CZ - width, pltpu.roll(here, CZ - width, 1), 0.0)
    total = total + jnp.where(lane >= width, pltpu.roll(here, width, 1), 0.0)
    return here, total


def diagonal_values(reaction, f):
    low = reaction[2 * f : 2 * f + 1, :]
    jump = reaction[2 * f + 1 : 2 * f + 2, :] - low
    return 6.0 + low, 6.0 + low + jump


def inverse_of(code, reaction, f):
    fluid, solid = diagonal_values(reaction, f)
    fluid, solid = 1.0 / fluid, 1.0 / solid
    return jnp.where(code == 0.0, fluid, jnp.where(code == 1.0, solid, 0.0))


def place():
    return lax.axis_index("row"), lax.axis_index("col")


def by_parity(step, first, second):
    even = lax.rem(lax.axis_index("col"), 2) == 0
    pl.when(even)(functools.partial(step, second, first))
    pl.when(jnp.logical_not(even))(functools.partial(step, first, second))


def pack_layers(
    b, material, inverse, up, down, first, second, b_here, material_here, inverse_here, sems,
):
    copies = [pltpu.make_async_copy(b.at[f], b_here.at[f], sems.at[f]) for f in range(FIELDS)]
    copies.append(pltpu.make_async_copy(material, material_here, sems.at[FIELDS]))
    copies.append(pltpu.make_async_copy(inverse, inverse_here, sems.at[FIELDS + 1]))
    for copy in copies:
        copy.start()
    for f in range(FIELDS + 1):
        copies[f].wait()
        if f < FIELDS:
            take = lambda start, size, step: b_here[f, pl.ds(start, size, stride=step), :]
        else:
            take = lambda start, size, step: material_here[
                pl.ds(start, size, stride=step), :
            ].astype(jnp.float32)
        at = f * 6 * CY
        up[at : at + 6 * CY, :] = take((CX - 6) * CY, 6 * CY, 1)
        down[at : at + 6 * CY, :] = take(0, 6 * CY, 1)

        def bands(left, right):
            for i in range(4):
                at = (f * 4 + i) * CX
                right[at : at + CX, :] = take(CY - 4 + i, CX, CY)
                left[at : at + CX, :] = take(i, CX, CY)

        by_parity(bands, first, second)
    copies[FIELDS + 1].wait()
    for f in range(FIELDS):
        for k in range(inverse.shape[2] // CZ):
            at = BAND_LINES + (f * GROUPS + k) * GROUPS
            value = inverse_here[f, :, k * CZ : (k + 1) * CZ]
            first[at : at + GROUPS, :] = value
            second[at : at + GROUPS, :] = value


def pack_corners(mine, first, second, reaction, up, down, kin, constants):
    for f in range(FIELDS):
        for i in range(2):
            constants[2 * f + i : 2 * f + i + 1, :] = jnp.broadcast_to(
                reaction[i : i + 1, f : f + 1], (1, CZ)
            )
    for f in range(FIELDS):
        for k in range(mine.shape[2] // CZ):
            at = (f * GROUPS + k) * GROUPS
            kin[0, at : at + GROUPS, :] = mine[f, :, k * CZ : (k + 1) * CZ]

    def pack(low, high):
        for side, ref in enumerate((low, high)):
            kin[1 + side] = ref[BAND_LINES : BAND_LINES + KIN_LINES, :]
            for f in range(FIELDS + 1):
                for j, offset in FINE_CORNER_AT.items():
                    size = 6 - j
                    line = (f * 4 + (j - 1 if side else 4 - j)) * CX
                    at = (f * 2 + side) * 16 + offset
                    up[at : at + size, :] = ref[line + CX - size : line + CX, :]
                    down[at : at + size, :] = ref[line : line + size, :]
                at = (f * 2 + side) * 16 + 14
                up[at : at + 2, :] = jnp.zeros((2, CZ), jnp.float32)
                down[at : at + 2, :] = jnp.zeros((2, CZ), jnp.float32)

    by_parity(pack, first, second)


def smooth_first(
    nrow, ncol, reaction, b, material, above, below, even, odd, kabove, kbelow,
    first, scaled, code, coarse, up, down, side_even, side_odd,
    s, inv, p0, p1, p2, p3, pair,
):
    row, col = place()
    parts = (p0, p1, p2, p3)
    zeros = jnp.zeros((FY, CZ), jnp.float32)
    for x in (*range(6), *range(GX - 6, GX)):
        for f in range(FIELDS):
            s[f, x, 8:56, :] = zeros[:48]
        code[x] = zeros + 2.0

    def own(i):
        x = i + 6
        for f in range(FIELDS):
            s[f, x, 8:16, :] = zeros[:8]
            s[f, x, 16:48, :] = b[f, i * CY : i * CY + CY, :]
            s[f, x, 48:56, :] = zeros[:8]
        code[x, 0:16, :] = zeros[:16] + 2.0
        code[x, 16:48, :] = material[i * CY : i * CY + CY, :].astype(jnp.float32)
        code[x, 48:64, :] = zeros[:16] + 2.0

    every(0, CX, own)
    sflat = s.reshape(FIELDS, GX * FY, CZ)
    cflat = code.reshape(GX * FY, CZ)

    def put(f, start, size, value):
        if f < FIELDS:
            sflat[f, pl.ds(start, size, stride=FY), :] = value
        else:
            cflat[pl.ds(start, size, stride=FY), :] = value

    def rows(first_x, ref):
        for i in range(6):
            for f in range(FIELDS):
                at = (f * 6 + i) * CY
                s[f, first_x + i, 16:48, :] = ref[at : at + CY, :]
            at = (FIELDS * 6 + i) * CY
            code[first_x + i, 16:48, :] = ref[at : at + CY, :]

    pl.when(row > 0)(functools.partial(rows, 0, above))
    pl.when(row < nrow - 1)(functools.partial(rows, GX - 6, below))

    def bands(ref, first_y):
        for f in range(FIELDS + 1):
            for i in range(4):
                at = (f * 4 + i) * CX
                put(f, 6 * FY + first_y + i, CX, ref[at : at + CX, :])

    def sides(low, high):
        pl.when(col > 0)(functools.partial(bands, low, FO - 4))
        pl.when(col < ncol - 1)(functools.partial(bands, high, FO + CY))

    by_parity(sides, even, odd)

    def corners(ref, is_above, is_high):
        for f in range(FIELDS + 1):
            for j, offset in FINE_CORNER_AT.items():
                size = 6 - j
                at = (f * 2 + is_high) * 16 + offset
                x = 6 - size if is_above else 6 + CX
                y = FO + CY - 1 + j if is_high else FO - j
                put(f, x * FY + y, size, ref[at : at + size, :])

    for ref, is_above, in_x in ((kabove, 1, row > 0), (kbelow, 0, row < nrow - 1)):
        for is_high, in_y in ((0, col > 0), (1, col < ncol - 1)):
            pl.when(in_x & in_y)(functools.partial(corners, ref, is_above, is_high))

    def scale(x):
        kind = code[x, 8:56, :]
        for f in range(FIELDS):
            inverse = inverse_of(kind, reaction, f)
            value = inverse * s[f, x, 8:56, :]
            inv[f, x, 8:56, :] = inverse
            s[f, x, 8:56, :] = value
            p0[f, x, 8:56, :] = value * (1.0 / THETA)

    every(0, GX, scale)

    for k, (keep, gain) in enumerate(coefficients()):
        def sweep(x):
            for f in range(FIELDS):
                here, total = beside(parts[k], f, x, 8, 48, 1)
                value = s[f, x, 8:56, :] - here + inv[f, x, 8:56, :] * total
                s[f, x, 8:56, :] = value
                parts[k + 1][f, x, 8:56, :] = keep * here + gain * value

        every(k + 1, GX - k - 1, sweep)

    parity = lanes() % 2 == 0

    def finish(i):
        at_y = i * 2 * CY
        inside = 1 <= i <= HX
        sums = []
        for f in range(FIELDS):
            fluid, solid = diagonal_values(reaction, f)
            residue = jnp.zeros((CY, CZ), jnp.float32)
            for h in range(2):
                x = i * 2 + h + 4
                row_at = (i * 2 + h - 2) * CY
                here, total = beside(p3, f, x, 16, CY, 1)
                value = s[f, x, 16:48, :] - here + inv[f, x, 16:48, :] * total
                out = pl.ds(at_y + h * CY, CY)
                scaled[f, out, :] = value
                if inside:
                    first[f, row_at : row_at + CY, :] = (
                        p0[f, x, 16:48, :] + p1[f, x, 16:48, :] + p2[f, x, 16:48, :] + here
                    )
                residue = residue + jnp.where(code[x, 16:48, :] == 1.0, solid, fluid) * value
            sums.append(residue)
        sums.append(code[i * 2 + 4, 16:48, :] + code[i * 2 + 5, 16:48, :])
        halves = []
        for f, value in enumerate(sums):
            here = pair.at[i % 2, f]
            here[...] = value
            halves.append(here[pl.ds(0, HY, stride=2), :] + here[pl.ds(1, HY, stride=2), :])
        halves.append(halves[4])
        out = pl.ds(i * HY, HY)
        for plane in range(3):
            even, odd = halves[2 * plane], halves[2 * plane + 1]
            merged = jnp.where(
                parity, even + pltpu.roll(even, CZ - 1, 1), odd + pltpu.roll(odd, 1, 1)
            )
            if plane < 2:
                coarse[plane, out, :] = merged * 0.5
            else:
                coarse[plane, out, :] = jnp.where(merged > 8.5, -1.0, merged)

    every(0, VX, finish)

    for f in range(FIELDS):
        at = COARSE_LINES + f * CY
        up[at : at + CY, :] = scaled[f, (CX - 1) * CY : CX * CY, :]
        down[at : at + CY, :] = scaled[f, 4 * CY : 5 * CY, :]
    for plane in range(3):
        at, size = plane * (HX + 1) * HY, (HX + 1) * HY
        up[at : at + size, :] = coarse[plane, 0:size, :]
        down[at : at + size, :] = coarse[plane, HY : HY + size, :]

    def strips(left, right):
        for plane in range(3):
            for i in range(9):
                at = (plane * 9 + i) * VX
                right[at : at + VX, :] = coarse[plane, pl.ds(HY - 9 + i, VX, stride=HY), :]
                left[at : at + VX, :] = coarse[plane, pl.ds(i, VX, stride=HY), :]
        for f in range(FIELDS):
            for j, offset in STRIP_AT.items():
                size = WX + 2 - 2 * j
                at = STRIP_LINES + f * (3 * WX - 6) + offset
                x = (j - 1) * CY
                right[at : at + size, :] = scaled[f, pl.ds(x + CY - j, size, stride=CY), :]
                left[at : at + size, :] = scaled[f, pl.ds(x + j - 1, size, stride=CY), :]

    by_parity(strips, side_even, side_odd)


def pack_knots(first, second, up, down):
    def pack(low, high):
        for plane in range(3):
            for side, ref in enumerate((low, high)):
                base = (plane * 2 + side) * CORNER_LINES
                up[base + 40 : base + 48, :] = jnp.zeros((8, CZ), jnp.float32)
                down[base + 40 : base + 48, :] = jnp.zeros((8, CZ), jnp.float32)
                for j, offset in CORNER_AT.items():
                    size = 10 - j
                    line = (plane * 9 + (j - 1 if side else 9 - j)) * VX
                    at = base + offset
                    up[at : at + size, :] = ref[line + VX - 1 - size : line + VX - 1, :]
                    down[at : at + size, :] = ref[line + 1 : line + 1 + size, :]

    by_parity(pack, first, second)


def coarse_constants(reaction, plane):
    parity = lanes() % 2 == 0
    even, odd = (
        [reaction[2 * f + i : 2 * f + i + 1, :] for i in range(2)]
        for f in (2 * plane, 2 * plane + 1)
    )
    low = jnp.where(parity, even[0], odd[0])
    return 8.0 * low, jnp.where(parity, even[1] - even[0], odd[1] - odd[0])


def smooth_coarse(
    nrow, ncol, reaction, coarse, above, below, even, odd, kabove, kbelow,
    start, scaled, inverse_out, sums,
    s, inv, count, p0, p1, p2, p3,
):
    row, col = place()
    parts = (p0, p1, p2, p3)
    zeros = jnp.zeros((QY, CZ), jnp.float32)

    def clear(x):
        for plane in range(2):
            s[plane, x] = zeros
        count[x] = zeros - 1.0

    every(0, QX, clear)
    sflat = s.reshape(2, QX * QY, CZ)
    cflat = count.reshape(QX * QY, CZ)

    def put(plane, start_row, size, value):
        if plane < 2:
            sflat[plane, pl.ds(start_row, size, stride=QY), :] = value
        else:
            cflat[pl.ds(start_row, size, stride=QY), :] = value

    def block(plane, x, value):
        if plane < 2:
            s[plane, x, QO : QO + HY, :] = value
        else:
            count[x, QO : QO + HY, :] = value

    def rows(first_x, ref):
        for plane in range(3):
            for i in range(HX + 1):
                at = (plane * (HX + 1) + i) * HY
                block(plane, first_x + i, ref[at : at + HY, :])

    for plane in range(3):
        for i in range(HX):
            block(plane, 9 + i, coarse[plane, (i + 1) * HY : (i + 2) * HY, :])
    pl.when(row > 0)(functools.partial(rows, 0, above))
    pl.when(row < nrow - 1)(functools.partial(rows, 9 + HX, below))

    def strips(ref, first_y):
        for plane in range(3):
            for i in range(9):
                line = (plane * 9 + i) * VX
                put(plane, 9 * QY + first_y + i, HX, ref[line + 1 : line + 1 + HX, :])

    def sides(low, high):
        pl.when(col > 0)(functools.partial(strips, low, QO - 9))
        pl.when(col < ncol - 1)(functools.partial(strips, high, QO + HY))

    by_parity(sides, even, odd)

    def corners(ref, is_above, is_high):
        for plane in range(3):
            base = (plane * 2 + is_high) * CORNER_LINES
            for j, at in CORNER_AT.items():
                size = 10 - j
                x = 9 - size if is_above else 9 + HX
                y = QO + HY - 1 + j if is_high else QO - j
                put(plane, x * QY + y, size, ref[base + at : base + at + size, :])

    for ref, is_above, in_x in ((kabove, 1, row > 0), (kbelow, 0, row < nrow - 1)):
        for is_high, in_y in ((0, col > 0), (1, col < ncol - 1)):
            pl.when(in_x & in_y)(functools.partial(corners, ref, is_above, is_high))

    def scale(x):
        number = count[x]
        for plane in range(2):
            low8, jump = coarse_constants(reaction, plane)
            inverse = jnp.where(number < 0.0, 0.0, 1.0 / (6.0 + 0.5 * (low8 + jump * number)))
            value = inverse * s[plane, x]
            inv[plane, x] = inverse
            s[plane, x] = value
            p0[plane, x] = value * (1.0 / THETA)

    every(0, QX, scale)

    for k, (keep, gain) in enumerate(coefficients()):
        def sweep(x):
            for plane in range(2):
                here, total = beside(parts[k], plane, x, 8, 32, 2)
                value = s[plane, x, 8:40, :] - here + inv[plane, x, 8:40, :] * total
                s[plane, x, 8:40, :] = value
                parts[k + 1][plane, x, 8:40, :] = keep * here + gain * value

        every(k + 1, QX - k - 1, sweep)

    def finish(x):
        for plane in range(2):
            here, total = beside(p3, plane, x, 8, 32, 2)
            value = s[plane, x, 8:40, :] - here + inv[plane, x, 8:40, :] * total
            scaled[plane, x - 4] = value
            inverse_out[plane, x - 4] = inv[plane, x, 8:40, :]

    every(4, QX - 4, finish)

    def add(x):
        for plane in range(2):
            start[plane, x - 7] = (
                p0[plane, x, 8:40, :] + p1[plane, x, 8:40, :]
                + p2[plane, x, 8:40, :] + p3[plane, x, 8:40, :]
            )

    every(7, QX - 7, add)

    lane = lanes()
    message = jnp.zeros((8, CZ), jnp.float32)
    for plane in range(2):
        low8, jump = coarse_constants(reaction, plane)
        total = jnp.zeros((HY, CZ), jnp.float32)
        for x in range(9, 9 + HX):
            diagonal = 6.0 + 0.5 * (low8 + jump * count[x, QO : QO + HY, :])
            total = total + diagonal * scaled[plane, x - 4, 8 : 8 + HY, :]
        total = total[:8] + total[8:]
        for shift in (4, 2, 1):
            total = total + pltpu.roll(total, shift, 0)
        for shift in (2, 4, 8):
            total = total + pltpu.roll(total, CZ - shift, 1)
        for odd in range(2):
            for g in range(GROUPS):
                to = (2 * plane + odd) * GROUPS + g
                moved = pltpu.roll(total, (to - 16 * g - odd) % CZ, 1)
                message = jnp.where(lane == to, moved, message)
    sums[...] = jnp.broadcast_to(message[:1], sums.shape)


def smooth_second(
    nrow, ncol, reaction, gathered, kin, kin_above, kin_below,
    start, qscaled, qinverse, first, scaled, code, above, below, even, odd,
    out,
    wide, spread, e, q0, q1, q2, q3, qs, fs, inv, f0, p0, p1, p2,
):
    row, col = place()
    lane = lanes()
    width = ncol * GROUPS
    fields = [jnp.zeros((nrow, CZ), jnp.float32) for _ in range(FIELDS)]
    for c in range(ncol):
        some = gathered[pl.ds(c, nrow, stride=ncol), :]
        for f in range(FIELDS):
            moved = pltpu.roll(some, (c * GROUPS - f * GROUPS) % CZ, 1)
            here = (lane >= c * GROUPS) & (lane < (c + 1) * GROUPS)
            fields[f] = jnp.where(here, moved, fields[f])
    for f in range(FIELDS):
        wide[f] = fields[f]

    group = lax.broadcasted_iota(jnp.int32, (GROUPS, CZ), 0)
    spot = lax.broadcasted_iota(jnp.int32, (GROUPS, CZ), 1)
    mask = [(spot // 16 == group) & (spot % 2 == odd) for odd in range(2)]
    e[...] = jnp.zeros_like(e)

    def product(rows_of, f):
        total = jnp.zeros((GROUPS, width), jnp.float32)
        for k in range(nrow):
            total = total + rows_of(f, k) * wide[f, k : k + 1, 0:width]
        return jnp.sum(total, axis=1, keepdims=True)

    def neighbour(rows_of, dx, dy):
        for plane in range(2):
            even = product(rows_of, 2 * plane)
            odd = product(rows_of, 2 * plane + 1)
            full = jnp.where(mask[0], even, jnp.where(mask[1], odd, 0.0))
            line = jnp.sum(full, axis=0, keepdims=True)
            x_from, x_to = {-1: (0, 6), 0: (6, 6 + HX), 1: (6 + HX, EX)}[dx]
            y_from, y_to = {-1: (8, QO), 0: (QO, QO + HY), 1: (QO + HY, QO + HY + 8)}[dy]
            for x in range(x_from, x_to):
                e[plane, x, y_from:y_to, :] = jnp.broadcast_to(line, (y_to - y_from, CZ))

    def slab(ref, part):
        def rows_of(f, k):
            at = (f * GROUPS + k) * GROUPS
            return ref[part, at : at + GROUPS, :]

        return rows_of

    in_x = {-1: row > 0, 0: True, 1: row < nrow - 1}
    in_y = {-1: col > 0, 0: True, 1: col < ncol - 1}
    for dx, ref in ((0, kin), (-1, kin_above), (1, kin_below)):
        for part, dy in enumerate((0, -1, 1)):
            step = functools.partial(neighbour, slab(ref, part), dx, dy)
            if dx == 0 and dy == 0:
                step()
            else:
                pl.when(in_x[dx] & in_y[dy])(step)

    parts = (q0, q1, q2, q3)

    def begin(x):
        for plane in range(2):
            here, total = beside(e, plane, x, 8, 32, 2)
            value = qscaled[plane, x - 1] - here + qinverse[plane, x - 1] * total
            qs[plane, x] = value
            q0[plane, x, 8:40, :] = value * (1.0 / THETA)

    every(1, EX - 1, begin)
    for k, (keep, gain) in enumerate(coefficients()):
        def sweep(x):
            for plane in range(2):
                here, total = beside(parts[k], plane, x, 8, 32, 2)
                value = qs[plane, x] - here + qinverse[plane, x - 1] * total
                qs[plane, x] = value
                parts[k + 1][plane, x, 8:40, :] = keep * here + gain * value

        every(k + 2, EX - k - 2, sweep)

    parity = lane % 2 == 0

    def lift(i):
        for plane in range(2):
            total = start[plane, i] + e[plane, i + 4, 8:40, :]
            total = total + q0[plane, i + 4, 8:40, :] + q1[plane, i + 4, 8:40, :]
            total = total + q2[plane, i + 4, 8:40, :] + q3[plane, i + 4, 8:40, :]
            for odd in range(2):
                if odd:
                    value = jnp.where(parity, pltpu.roll(total, CZ - 1, 1), total)
                else:
                    value = jnp.where(parity, total, pltpu.roll(total, 1, 1))
                spread[...] = value
                some = spread[4:28, :]
                for h in range(2):
                    for y in range(2):
                        f0[2 * plane + odd, i * 2 + h, pl.ds(8 + y, 24, stride=2), :] = some

    every(0, HX + 4, lift)

    zeros = jnp.zeros((48, CZ), jnp.float32)
    for f in range(FIELDS):
        for x in (1, FX - 2):
            fs[f, x, 8:56, :] = zeros
        for x in range(2, FX - 2):
            fs[f, x, 8:16, :] = zeros[:8]
            fs[f, x, 16:48, :] = scaled[f, (x - 2) * CY : (x - 1) * CY, :]
            fs[f, x, 48:56, :] = zeros[:8]
    sflat = fs.reshape(FIELDS, FX * FY, CZ)

    def face(x, ref):
        for f in range(FIELDS):
            at = COARSE_LINES + f * CY
            fs[f, x, 16:48, :] = ref[at : at + CY, :]

    pl.when(in_x[-1])(functools.partial(face, 1, above))
    pl.when(in_x[1])(functools.partial(face, FX - 2, below))

    def strips(ref, is_high):
        for f in range(FIELDS):
            for j, offset in STRIP_AT.items():
                size = WX + 2 - 2 * j
                at = STRIP_LINES + f * (3 * WX - 6) + offset
                y = FO + CY - 1 + j if is_high else FO - j
                start = (1 + j) * FY + y
                sflat[f, pl.ds(start, size, stride=FY), :] = ref[at : at + size, :]

    def sides(low, high):
        pl.when(in_y[-1])(functools.partial(strips, low, 0))
        pl.when(in_y[1])(functools.partial(strips, high, 1))

    by_parity(sides, even, odd)

    parts = (p0, p1, p2)

    def open_fine(x):
        kind = code[x + 2, 8:56, :]
        for f in range(FIELDS):
            here, total = beside(f0, f, x, 8, 48, 1)
            inverse = inverse_of(kind, reaction, f)
            inv[f, x, 8:56, :] = inverse
            value = fs[f, x, 8:56, :] - here + inverse * total
            fs[f, x, 8:56, :] = value
            p0[f, x, 8:56, :] = value * (1.0 / THETA)

    every(1, FX - 1, open_fine)
    for k, (keep, gain) in enumerate(coefficients()[:2]):
        def sweep(x):
            for f in range(FIELDS):
                here, total = beside(parts[k], f, x, 8, 48, 1)
                value = fs[f, x, 8:56, :] - here + inv[f, x, 8:56, :] * total
                fs[f, x, 8:56, :] = value
                parts[k + 1][f, x, 8:56, :] = keep * here + gain * value

        every(k + 2, FX - k - 2, sweep)

    keep, gain = coefficients()[2]

    def close(i):
        x = i + 4
        at = pl.ds(i * CY, CY)
        for f in range(FIELDS):
            here, total = beside(p2, f, x, 16, CY, 1)
            value = fs[f, x, 16:48, :] - here + inv[f, x, 16:48, :] * total
            result = first[f, at, :] + f0[f, x, 16:48, :] + p0[f, x, 16:48, :]
            result = result + p1[f, x, 16:48, :] + here
            out[f, at, :] = result + (keep * here + gain * value)

    every(0, CX, close)


def call(kernel, out_shapes, scratch, *args, limit=16, in_hbm=False):
    vmem = pl.BlockSpec(memory_space=pltpu.VMEM)
    given = pl.BlockSpec(memory_space=pltpu.HBM) if in_hbm else vmem
    return pl.pallas_call(
        kernel,
        out_shape=[jax.ShapeDtypeStruct(shape, jnp.float32) for shape in out_shapes],
        in_specs=[given] * len(args),
        out_specs=[vmem] * len(out_shapes),
        scratch_shapes=[
            pltpu.VMEM(shape, jnp.float32) if isinstance(shape, tuple) else shape
            for shape in scratch
        ],
        compiler_params=pltpu.CompilerParams(vmem_limit_bytes=int(limit * 1024 * 1024)),
    )(*args)


def ahead(value):
    count = lax.axis_size("row")
    return lax.ppermute(value, "row", [(i, (i + 1) % count) for i in range(count)])


def back(value):
    count = lax.axis_size("row")
    return lax.ppermute(value, "row", [((i + 1) % count, i) for i in range(count)])


def pairs(value, odd):
    nrow, ncol = lax.axis_size("row"), lax.axis_size("col")
    moves = []
    for r in range(nrow):
        for c in range(ncol):
            if not odd:
                to = (r, c ^ 1)
            elif c in (0, ncol - 1):
                to = (r ^ 1, c)
            else:
                to = (r, c + 1 if c % 2 else c - 1)
            moves.append((r * ncol + c, to[0] * ncol + to[1]))
    return lax.ppermute(value, ("row", "col"), moves)


def body(right_side, material, reaction, coarse_inverse):
    nrow, ncol = lax.axis_size("row"), lax.axis_size("col")
    b = right_side.reshape(FIELDS, CX * CY, CZ)
    material = material.reshape(CX * CY, CZ)

    fine = (FIELDS, CX * CY, CZ)
    up, down, even, odd = call(
        pack_layers,
        [(LAYER_LINES, CZ)] * 2 + [(BAND_LINES + KIN_LINES, CZ)] * 2,
        [fine, pltpu.VMEM(fine[1:], jnp.int32), coarse_inverse.shape,
         pltpu.SemaphoreType.DMA((FIELDS + 2,))],
        b, material, coarse_inverse,
        in_hbm=True, limit=59.27,
    )
    odd, even = pairs(odd, True), pairs(even, False)
    above, below = ahead(up), back(down)
    up, down, kin, reaction = call(
        pack_corners,
        [((FIELDS + 1) * 32, CZ)] * 2 + [(3, KIN_LINES, CZ), (2 * FIELDS, CZ)], [],
        coarse_inverse, even, odd, reaction.T,
    )
    kabove, kbelow = ahead(up), back(down)
    kin, kabove, kbelow = lax.optimization_barrier((kin, kabove, kbelow))
    kin_above, kin_below = ahead(kin), back(kin)

    wide = (FIELDS, WX * CY, CZ)
    padded = (FIELDS, GX, FY, CZ)
    first, scaled, code, coarse, up, down, side_even, side_odd = call(
        functools.partial(smooth_first, nrow, ncol),
        [fine, wide, padded[1:], (3, VX * HY, CZ)]
        + [(FACE_LINES, CZ)] * 2 + [(SIDE_LINES, CZ)] * 2,
        [padded] * 6 + [(2, FIELDS + 1, CY, CZ)],
        reaction, b, material, above, below, even, odd, kabove, kbelow,
        limit=30,
    )
    up, down, side_even, side_odd, kin_above, kin_below = lax.optimization_barrier(
        (up, down, side_even, side_odd, kin_above, kin_below)
    )

    odd, even = pairs(side_odd, True), pairs(side_even, False)
    above, below = ahead(up), back(down)
    up, down = call(pack_knots, [(KNOT_LINES, CZ)] * 2, [], even, odd)
    kabove, kbelow = ahead(up), back(down)

    qpadded = (2, QX, QY, CZ)
    start, qscaled, qinverse, sums = call(
        functools.partial(smooth_coarse, nrow, ncol),
        [(2, HX + 4, 32, CZ), (2, HX + 10, 32, CZ), (2, HX + 10, 32, CZ), (nrow * ncol, CZ)],
        [qpadded, qpadded, qpadded[1:]] + [qpadded] * 4,
        reaction, coarse, above, below, even, odd, kabove, kbelow,
        limit=14,
    )

    gathered = lax.all_to_all(sums, ("row", "col"), 0, 0)

    epadded = (2, EX, QY, CZ)
    padded = (FIELDS, FX, FY, CZ)
    (out,) = call(
        functools.partial(smooth_second, nrow, ncol),
        [fine],
        [(FIELDS, nrow, CZ), (32, CZ)] + [epadded] * 5 + [(2, EX, 32, CZ)] + [padded] * 6,
        reaction, gathered, kin, kin_above, kin_below,
        start, qscaled, qinverse, first, scaled, code, above, below, even, odd,
        limit=32,
    )
    return out.reshape(right_side.shape)


def solution(mesh):
    placed = (
        P(None, "row", "col", None),
        P("row", "col", None),
        P(),
        P(None, ("row", "col"), None),
    )
    return jax.shard_map(
        body, mesh=mesh, in_specs=placed, out_specs=P(None, "row", "col", None), check_vma=False
    )
```

time: 117 us -> 75.7 us (0.65)
  blocking collectives: 0 us -> 24.9 us
  Pallas kernels: 42.2 us -> 19.2 us
  starting transfers between devices: 38.6 us -> 18 us
  local copies, waits for them, and re-layouts: 13.5 us -> 0.02 us
  waiting for transfers between devices: 20 us -> 13.3 us
  other arithmetic: 1.81 us -> 0 us
    all_to_all x0 -> x1, blocking collectives: none -> 24.9 us  [body(): gathered = lax.all_to_all(sums, ('row', 'col'), 0, 0)]
    pallas_call x6, Pallas kernels: 42.2 us -> 19.2 us  [call(): pl.pallas_call(kernel, out_shape=[jax.ShapeDtypeStruct(shape, jnp.float32...]
    ppermute x20 -> x14, starting transfers between devices: 32.2 us -> 18 us  [the longest x4 8.67 us: pairs(): return lax.ppermute(value, ('row', 'col'), moves)]
    unnamed x37 -> x8, local copies, waits for them, and re-layouts: 13.5 us -> 0.02 us
    all_to_all x1 -> x0, waiting for transfers between devices: 9.74 us -> none  [body(): gathered = lax.all_to_all(sums, ('row', 'col'), 0, 0)]
    all_to_all x1 -> x0, starting transfers between devices: 6.34 us -> none  [body(): gathered = lax.all_to_all(sums, ('row', 'col'), 0, 0)]
    ppermute x20 -> x14, waiting for transfers between devices: 10.2 us -> 13.3 us  [the longest x5 6.73 us: back(): lax.ppermute(value, 'row', [((i + 1) % count, i) for i in range(count)])]
    another operation x1 -> x0, other arithmetic: 1.81 us -> none  [body(): kin = jnp.stack([coarse_inverse, kin_above, kin_below])]
  transfers between devices with their start and end apart: 21 -> 14, of which waited for: 5 -> 7; matrix products, arithmetic and copies ran while one was open for 2% -> 0% of each run, Pallas kernels for 19% -> 9%
where the time goes in v2:
time: 75.7 us; the launch traced here: 75.6 us
  blocking collectives  24.9 us (33%)
  Pallas kernels  19.2 us (25%)
  starting transfers between devices  18 us (24%)
  waiting for transfers between devices  13.3 us (18%)
    all_to_all x1, blocking collectives, body(): gathered = lax.all_to_all(sums, ('row', 'col'), 0, 0)  24.9 us
    pallas_call x6, Pallas kernels, call(): pl.pallas_call(kernel, out_shape=[jax.ShapeDtypeStruct(shape, jnp.float32...  19.2 us
    ppermute x4, starting transfers between devices, pairs(): return lax.ppermute(value, ('row', 'col'), moves)  8.67 us
    ppermute x5, starting transfers between devices, ahead(): lax.ppermute(value, 'row', [(i, (i + 1) % count) for i in range(count)])  8.35 us
    ppermute x5, waiting for transfers between devices, back(): lax.ppermute(value, 'row', [((i + 1) % count, i) for i in range(count)])  6.73 us
    ppermute x4, waiting for transfers between devices, pairs(): return lax.ppermute(value, ('row', 'col'), moves)  5.12 us
  transfers between devices with their start and end apart: 14, of which 7 were waited for; matrix products, arithmetic and copies ran while one was open for 0% of the time, Pallas kernels for 9%

profile of v2, /device:TPU:1, one launch (start us, length us, event | category | flops | bytes accessed | tf_op | source)
XLA Modules:
  0.0 75.6 jit_solution(11686374086337798527)
XLA Ops:
  0.0 0.0 copy-start.2
  0.0 0.0 copy-start.1
  0.0 0.0 copy-start
  0.0 0.0 copy-start.3
  0.0 2.6 %shard_map.46 = (f32[960,128]{1,0:T(8,128)}, f32[960,128]{1,0:T(8,128)}, f32[576,128]{1,0:T(8,128)}, f32[576,128]{1,0:T(8,128)}) custom-call(f32[4,512,128]{2,1,0:T(8,128)} %bitcast.8, s32[512,128]{1,0:T(8,128)} %bitcast.10, f32[4,8,1024]{2,1,0:T(8,128)} %mine.1), custom_call_target="tpu_custom_call" | custom-call | tf_op jit(solution)/shard_map/pallas_call | solution.py:642
  2.7 2.2 %collective-permute-start = (f32[576,128]{1,0:T(8,128)}, f32[576,128]{1,0:T(8,128)S(1)}, u32[]{:S(2)}, u32[]{:S(2)}) collective-permute-start(f32[576,128]{1,0:T(8,128)} %get-tuple-element.36), channel_id=1, source_target_pairs={{0,1},{1,0},{2,3},{3,2},{4,5},{5,4},{6,7},{7,6},{8,9},{9,8},{10,11... | collective-permute-start | bytes 884744 | tf_op jit(solution)/shard_map/ppermute | solution.py:677
  4.9 1.0 %collective-permute-start.1 = (f32[576,128]{1,0:T(8,128)}, f32[576,128]{1,0:T(8,128)S(1)}, u32[]{:S(2)}, u32[]{:S(2)}) collective-permute-start(f32[576,128]{1,0:T(8,128)} %get-tuple-element.37), channel_id=1, source_target_pairs={{0,16},{1,2},{2,1},{3,4},{4,3},{5,6},{6,5},{7,8},{8,7},{9,10},{10,... | collective-permute-start | bytes 884744 | tf_op jit(solution)/shard_map/ppermute | solution.py:677
  5.8 1.1 %collective-permute-start.2 = (f32[960,128]{1,0:T(8,128)}, f32[960,128]{1,0:T(8,128)S(1)}, u32[]{:S(2)}, u32[]{:S(2)}) collective-permute-start(f32[960,128]{1,0:T(8,128)} %get-tuple-element.39), channel_id=1, source_target_pairs={{0,16},{16,32},{32,48},{48,64},{64,80},{80,96},{96,112},{112,0},{1... | collective-permute-start | bytes 1474568 | tf_op jit(solution)/shard_map/ppermute | solution.py:657
  6.9 0.0 collective-permute-start.3
  6.9 4.5 %collective-permute-done.first.even = f32[576,128]{1,0:T(8,128)S(1)} collective-permute-done((f32[576,128]{1,0:T(8,128)}, f32[576,128]{1,0:T(8,128)S(1)}, u32[]{:S(2)}, u32[]{:S(2)}) %collective-permute-start) | collective-permute-done | bytes 294944 | tf_op jit(solution)/shard_map/ppermute | solution.py:677
  11.4 0.0 collective-permute-done.1.second.odd
  11.4 0.0 copy-done.2
  11.4 0.0 copy-done.3
  11.4 0.1 shard_map.47
  11.5 2.9 %collective-permute-start.4 = (f32[160,128]{1,0:T(8,128)S(1)}, f32[160,128]{1,0:T(8,128)S(1)}, u32[]{:S(2)}, u32[]{:S(2)}) collective-permute-start(f32[160,128]{1,0:T(8,128)S(1)} %get-tuple-element.42), channel_id=1, source_target_pairs={{0,16},{16,32},{32,48},{48,64},{64,80},{80,96},{96,112},{112,0},{1... | collective-permute-start | bytes 245768 | tf_op jit(solution)/shard_map/ppermute | solution.py:657
  14.4 0.0 collective-permute-start.5
  14.4 1.5 %collective-permute-done.4.kabove = f32[160,128]{1,0:T(8,128)S(1)} collective-permute-done((f32[160,128]{1,0:T(8,128)S(1)}, f32[160,128]{1,0:T(8,128)S(1)}, u32[]{:S(2)}, u32[]{:S(2)}) %collective-permute-start.4) | collective-permute-done | bytes 81952 | tf_op jit(solution)/shard_map/ppermute | solution.py:657
  15.9 2.4 %collective-permute-done.5.kbelow = f32[160,128]{1,0:T(8,128)S(1)} collective-permute-done((f32[160,128]{1,0:T(8,128)S(1)}, f32[160,128]{1,0:T(8,128)S(1)}, u32[]{:S(2)}, u32[]{:S(2)}) %collective-permute-start.5) | collective-permute-done | bytes 81952 | tf_op jit(solution)/shard_map/ppermute | solution.py:662
  18.3 0.0 collective-permute-start.7
  18.3 1.7 %collective-permute-start.6 = (f32[3,256,128]{2,1,0:T(8,128)S(1)}, f32[3,256,128]{2,1,0:T(8,128)S(1)}, u32[]{:S(2)}, u32[]{:S(2)}) collective-permute-start(f32[3,256,128]{2,1,0:T(8,128)S(1)} %get-tuple-element.51.kin), channel_id=1, source_target_pairs={{0,16},{16,32},{32,48},{48,64},{64,80},{80,96},{96,112},{112,0},{1... | collective-permute-start | bytes 1179656 | tf_op jit(solution)/shard_map/ppermute | solution.py:657
  20.0 0.0 collective-permute-done.2.above
  20.0 0.0 collective-permute-done.3.below
  20.0 0.0 copy-done.1
  20.0 0.0 copy-done
  20.0 6.6 %shard_map.48 = (f32[4,512,128]{2,1,0:T(8,128)S(1)}, f32[4,640,128]{2,1,0:T(8,128)S(1)}, f32[28,64,128]{2,1,0:T(8,128)S(1)}, f32[3,160,128]{2,1,0:T(8,128)S(1)},...) custom-call(f32[8,128]{1,0:T(8,128)S(1)} %get-tuple-element.38.reaction, ...), custom_call_target="tpu_custom_call" | custom-call | tf_op jit(solution)/shard_map/pallas_call | solution.py:642
  26.7 0.0 collective-permute-done.7.kin_below
  26.7 0.0 collective-permute-done.6.kin_above
  26.7 2.4 %collective-permute-start.10 = (f32[488,128]{1,0:T(8,128)S(1)}, f32[488,128]{1,0:T(8,128)S(1)}, u32[]{:S(2)}, u32[]{:S(2)}) collective-permute-start(f32[488,128]{1,0:T(8,128)S(1)} %get-tuple-element.54), channel_id=1, source_target_pairs={{0,1},{1,0},{2,3},{3,2},{4,5},{5,4},{6,7},{7,6},{8,9},{9,8},{10,11... | collective-permute-start | bytes 749576 | tf_op jit(solution)/shard_map/ppermute | solution.py:677
  29.2 3.1 %collective-permute-start.11 = (f32[488,128]{1,0:T(8,128)S(1)}, f32[488,128]{1,0:T(8,128)S(1)}, u32[]{:S(2)}, u32[]{:S(2)}) collective-permute-start(f32[488,128]{1,0:T(8,128)S(1)} %get-tuple-element.55), channel_id=1, source_target_pairs={{0,16},{1,2},{2,1},{3,4},{4,3},{5,6},{6,5},{7,8},{8,7},{9,10},{10,... | collective-permute-start | bytes 749576 | tf_op jit(solution)/shard_map/ppermute | solution.py:677
  32.2 0.0 collective-permute-start.8
  32.2 0.5 collective-permute-start.9
  32.7 0.1 collective-permute-done.10.first.even
  32.8 0.6 collective-permute-done.11.second.odd
  33.4 2.6 %collective-permute-start.12 = (f32[288,128]{1,0:T(8,128)S(1)}, f32[288,128]{1,0:T(8,128)S(1)}, u32[]{:S(2)}, u32[]{:S(2)}) collective-permute-start(f32[288,128]{1,0:T(8,128)S(1)} %get-tuple-element.56), channel_id=1, source_target_pairs={{0,16},{16,32},{32,48},{48,64},{64,80},{80,96},{96,112},{112,0},{1... | collective-permute-start | bytes 442376 | tf_op jit(solution)/shard_map/ppermute | solution.py:657
  36.0 0.5 collective-permute-start.13
  36.5 0.0 collective-permute-done.8.above
  36.5 2.0 %collective-permute-done.9.below = f32[560,128]{1,0:T(8,128)S(1)} collective-permute-done((f32[560,128]{1,0:T(8,128)S(1)}, f32[560,128]{1,0:T(8,128)S(1)}, u32[]{:S(2)}, u32[]{:S(2)}) %collective-permute-start.9) | collective-permute-done | bytes 286752 | tf_op jit(solution)/shard_map/ppermute | solution.py:662
  38.6 0.0 collective-permute-done.12.kabove
  38.6 2.3 %collective-permute-done.13.kbelow = f32[288,128]{1,0:T(8,128)S(1)} collective-permute-done((f32[288,128]{1,0:T(8,128)S(1)}, f32[288,128]{1,0:T(8,128)S(1)}, u32[]{:S(2)}, u32[]{:S(2)}) %collective-permute-start.13) | collective-permute-done | bytes 147488 | tf_op jit(solution)/shard_map/ppermute | solution.py:662
  40.9 2.4 %shard_map.50 = (f32[2,12,32,128]{3,2,1,0:T(8,128)S(1)}, f32[2,18,32,128]{3,2,1,0:T(8,128)S(1)}, f32[2,18,32,128]{3,2,1,0:T(8,128)S(1)}, f32[128,128]{1,0:T(8,128)S(1)}) custom-call(f32[8,128]{1,0:T(8,128)S(1)} %get-tuple-element.38.reaction, f32[3,160,128]{2,1,0:T(8,128)S(1)} %get-tuple-element.46.coarse, f32[560,128]{1,0:T(8,128)S(1)} %collective-permute-done.8.above, ...), custom_call_target="tpu_custom_call" | custom-call | tf_op jit(solution)/shard_map/pallas_call | solution.py:642
  43.3 24.9 %all_to_all.11 = f32[128,1,128]{2,1,0:T(1,128)S(1)} all-to-all(f32[128,1,128]{2,1,0:T(1,128)S(1)} %bitcast.13), channel_id=1, replica_groups=mesh['row'=8,'col'=16] {'row','col'}, dimensions={0} | all-to-all | bytes 131072 | tf_op jit(solution)/shard_map/all_to_all | solution.py:733
  68.2 7.4 %shard_map.51 = f32[4,512,128]{2,1,0:T(8,128)} custom-call(f32[8,128]{1,0:T(8,128)S(1)} %get-tuple-element.38.reaction, f32[128,128]{1,0:T(8,128)S(1)} %bitcast.12, f32[3,256,128]{2,1,0:T(8,128)S(1)} %get-tuple-element.51.kin, f32[3,256,128]{2,1,0:T(8,128)S(1)} %collective-permute-done.6.kin_above, f32[3,256,128]{2,1,0:T(8,128)S(1)} %collective-permute-done.7.kin_below, ...), custom_call_target="tpu_custom_call" | custom-call | tf_op jit(solution)/shard_map/pallas_call | solution.py:642
  (1 shorter events, 0.0 us)
Async XLA Ops:
  0.0 11.4 %copy-start.2 = (f32[4,8,1024]{2,1,0:T(8,128)S(1)}, f32[4,8,1024]{2,1,0:T(8,128)}, u32[]{:S(2)}) copy-start(f32[4,8,1024]{2,1,0:T(8,128)} %mine.1) | copy-start | bytes 393220
  0.0 20.0 %copy-start.1 = (s32[16,32,128]{2,1,0:T(8,128)S(1)}, s32[16,32,128]{2,1,0:T(8,128)}, u32[]{:S(2)}) copy-start(s32[16,32,128]{2,1,0:T(8,128)} %param.5) | copy-start | bytes 786436
  0.0 20.0 %copy-start = (f32[4,16,32,128]{3,2,1,0:T(8,128)S(1)}, f32[4,16,32,128]{3,2,1,0:T(8,128)}, u32[]{:S(2)}) copy-start(f32[4,16,32,128]{3,2,1,0:T(8,128)} %param.4) | copy-start | bytes 3145732
  0.0 11.4 %copy-start.3 = (f32[4,2]{0,1:T(2,128)S(1)}, f32[4,2]{0,1:T(2,128)}, u32[]{:S(2)}) copy-start(f32[4,2]{0,1:T(2,128)} %param.6) | copy-start | bytes 100
  2.7 8.7 %collective-permute-start = (f32[576,128]{1,0:T(8,128)}, f32[576,128]{1,0:T(8,128)S(1)}, u32[]{:S(2)}, u32[]{:S(2)}) collective-permute-start(f32[576,128]{1,0:T(8,128)} %get-tuple-element.36), channel_id=1, source_target_pairs={{0,1},{1,0},{2,3},{3,2},{4,5},{5,4},{6,7},{7,6},{8,9},{9,8},{10,11... | collective-permute-start | bytes 884744 | tf_op jit(solution)/shard_map/ppermute | solution.py:677
  4.9 6.5 %collective-permute-start.1 = (f32[576,128]{1,0:T(8,128)}, f32[576,128]{1,0:T(8,128)S(1)}, u32[]{:S(2)}, u32[]{:S(2)}) collective-permute-start(f32[576,128]{1,0:T(8,128)} %get-tuple-element.37), channel_id=1, source_target_pairs={{0,16},{1,2},{2,1},{3,4},{4,3},{5,6},{6,5},{7,8},{8,7},{9,10},{10,... | collective-permute-start | bytes 884744 | tf_op jit(solution)/shard_map/ppermute | solution.py:677
  5.8 14.2 %collective-permute-start.2 = (f32[960,128]{1,0:T(8,128)}, f32[960,128]{1,0:T(8,128)S(1)}, u32[]{:S(2)}, u32[]{:S(2)}) collective-permute-start(f32[960,128]{1,0:T(8,128)} %get-tuple-element.39), channel_id=1, source_target_pairs={{0,16},{16,32},{32,48},{48,64},{64,80},{80,96},{96,112},{112,0},{1... | collective-permute-start | bytes 1474568 | tf_op jit(solution)/shard_map/ppermute | solution.py:657
  6.9 13.1 %collective-permute-start.3 = (f32[960,128]{1,0:T(8,128)}, f32[960,128]{1,0:T(8,128)S(1)}, u32[]{:S(2)}, u32[]{:S(2)}) collective-permute-start(f32[960,128]{1,0:T(8,128)} %get-tuple-element.40), channel_id=1, source_target_pairs={{16,0},{32,16},{48,32},{64,48},{80,64},{96,80},{112,96},{0,112},{1... | collective-permute-start | bytes 1474568 | tf_op jit(solution)/shard_map/ppermute | solution.py:662
  11.5 4.4 %collective-permute-start.4 = (f32[160,128]{1,0:T(8,128)S(1)}, f32[160,128]{1,0:T(8,128)S(1)}, u32[]{:S(2)}, u32[]{:S(2)}) collective-permute-start(f32[160,128]{1,0:T(8,128)S(1)} %get-tuple-element.42), channel_id=1, source_target_pairs={{0,16},{16,32},{32,48},{48,64},{64,80},{80,96},{96,112},{112,0},{1... | collective-permute-start | bytes 245768 | tf_op jit(solution)/shard_map/ppermute | solution.py:657
  14.4 3.9 %collective-permute-start.5 = (f32[160,128]{1,0:T(8,128)S(1)}, f32[160,128]{1,0:T(8,128)S(1)}, u32[]{:S(2)}, u32[]{:S(2)}) collective-permute-start(f32[160,128]{1,0:T(8,128)S(1)} %get-tuple-element.43), channel_id=1, source_target_pairs={{16,0},{32,16},{48,32},{64,48},{80,64},{96,80},{112,96},{0,112},{1... | collective-permute-start | bytes 245768 | tf_op jit(solution)/shard_map/ppermute | solution.py:662
  18.3 8.4 %collective-permute-start.7 = (f32[3,256,128]{2,1,0:T(8,128)S(1)}, f32[3,256,128]{2,1,0:T(8,128)S(1)}, u32[]{:S(2)}, u32[]{:S(2)}) collective-permute-start(f32[3,256,128]{2,1,0:T(8,128)S(1)} %get-tuple-element.51.kin), channel_id=1, source_target_pairs={{16,0},{32,16},{48,32},{64,48},{80,64},{96,80},{112,96},{0,112},{1... | collective-permute-start | bytes 1179656 | tf_op jit(solution)/shard_map/ppermute | solution.py:662
  18.3 8.4 %collective-permute-start.6 = (f32[3,256,128]{2,1,0:T(8,128)S(1)}, f32[3,256,128]{2,1,0:T(8,128)S(1)}, u32[]{:S(2)}, u32[]{:S(2)}) collective-permute-start(f32[3,256,128]{2,1,0:T(8,128)S(1)} %get-tuple-element.51.kin), channel_id=1, source_target_pairs={{0,16},{16,32},{32,48},{48,64},{64,80},{80,96},{96,112},{112,0},{1... | collective-permute-start | bytes 1179656 | tf_op jit(solution)/shard_map/ppermute | solution.py:657
  26.7 6.1 %collective-permute-start.10 = (f32[488,128]{1,0:T(8,128)S(1)}, f32[488,128]{1,0:T(8,128)S(1)}, u32[]{:S(2)}, u32[]{:S(2)}) collective-permute-start(f32[488,128]{1,0:T(8,128)S(1)} %get-tuple-element.54), channel_id=1, source_target_pairs={{0,1},{1,0},{2,3},{3,2},{4,5},{5,4},{6,7},{7,6},{8,9},{9,8},{10,11... | collective-permute-start | bytes 749576 | tf_op jit(solution)/shard_map/ppermute | solution.py:677
  29.2 4.2 %collective-permute-start.11 = (f32[488,128]{1,0:T(8,128)S(1)}, f32[488,128]{1,0:T(8,128)S(1)}, u32[]{:S(2)}, u32[]{:S(2)}) collective-permute-start(f32[488,128]{1,0:T(8,128)S(1)} %get-tuple-element.55), channel_id=1, source_target_pairs={{0,16},{1,2},{2,1},{3,4},{4,3},{5,6},{6,5},{7,8},{8,7},{9,10},{10,... | collective-permute-start | bytes 749576 | tf_op jit(solution)/shard_map/ppermute | solution.py:677
  32.2 4.3 %collective-permute-start.8 = (f32[560,128]{1,0:T(8,128)S(1)}, f32[560,128]{1,0:T(8,128)S(1)}, u32[]{:S(2)}, u32[]{:S(2)}) collective-permute-start(f32[560,128]{1,0:T(8,128)S(1)} %get-tuple-element.52), channel_id=1, source_target_pairs={{0,16},{16,32},{32,48},{48,64},{64,80},{80,96},{96,112},{112,0},{1... | collective-permute-start | bytes 860168 | tf_op jit(solution)/shard_map/ppermute | solution.py:657
  32.2 6.4 %collective-permute-start.9 = (f32[560,128]{1,0:T(8,128)S(1)}, f32[560,128]{1,0:T(8,128)S(1)}, u32[]{:S(2)}, u32[]{:S(2)}) collective-permute-start(f32[560,128]{1,0:T(8,128)S(1)} %get-tuple-element.53), channel_id=1, source_target_pairs={{16,0},{32,16},{48,32},{64,48},{80,64},{96,80},{112,96},{0,112},{1... | collective-permute-start | bytes 860168 | tf_op jit(solution)/shard_map/ppermute | solution.py:662
  33.4 5.2 %collective-permute-start.12 = (f32[288,128]{1,0:T(8,128)S(1)}, f32[288,128]{1,0:T(8,128)S(1)}, u32[]{:S(2)}, u32[]{:S(2)}) collective-permute-start(f32[288,128]{1,0:T(8,128)S(1)} %get-tuple-element.56), channel_id=1, source_target_pairs={{0,16},{16,32},{32,48},{48,64},{64,80},{80,96},{96,112},{112,0},{1... | collective-permute-start | bytes 442376 | tf_op jit(solution)/shard_map/ppermute | solution.py:657
  36.0 4.9 %collective-permute-start.13 = (f32[288,128]{1,0:T(8,128)S(1)}, f32[288,128]{1,0:T(8,128)S(1)}, u32[]{:S(2)}, u32[]{:S(2)}) collective-permute-start(f32[288,128]{1,0:T(8,128)S(1)} %get-tuple-element.57), channel_id=1, source_target_pairs={{16,0},{32,16},{48,32},{64,48},{80,64},{96,80},{112,96},{0,112},{1... | collective-permute-start | bytes 442376 | tf_op jit(solution)/shard_map/ppermute | solution.py:662

commit v3 on v2

--- a/solution.py
+++ b/solution.py
@@ -18,20 +18,25 @@
 DELTA = (HIGH_BOUND - LOW_BOUND) / 2.0
 
 WX = CX + 4
-GX, FY, FO = CX + 12, CY + 32, 16
+GX, FY, FO, FN = CX + 12, CY + 24, 8, CY + 8
+OWN = slice(FO, FO + CY)
+ALL = slice(FO, FO + FN)
 FX = CX + 8
+MID = (4, CX - 4)
 VX = HX + 2
 QX, QY, QO = HX + 18, HY + 32, 16
 EX = HX + 12
 CORNER_AT = {1: 0, 2: 9, 3: 17, 4: 24, 5: 30, 6: 35, 7: 39, 8: 42, 9: 44}
 CORNER_LINES = 48
 FINE_CORNER_AT = {1: 0, 2: 5, 3: 9, 4: 12}
+FINE_CORNER_LINES = (FIELDS + 1) * 32
 
 LAYER_LINES = (FIELDS + 1) * 6 * CY
 BAND_LINES = (FIELDS + 1) * 4 * CX
 KIN_LINES = FIELDS * GROUPS * 8
 COARSE_LINES = 3 * (HX + 1) * HY
-FACE_LINES = COARSE_LINES + FIELDS * CY
+FACE_KIN = COARSE_LINES + FIELDS * CY
+FACE_LINES = FACE_KIN + 2 * KIN_LINES
 STRIP_LINES = 272
 STRIP_AT = {1: 0, 2: WX, 3: 2 * WX - 2}
 SIDE_LINES = STRIP_LINES + FIELDS * (3 * WX - 6)
@@ -126,20 +131,20 @@
             second[at : at + GROUPS, :] = value
 
 
-def pack_corners(mine, first, second, reaction, up, down, kin, constants):
+def pack_corners(first, second, reaction, inverse, up, down, constants):
+    for f in range(FIELDS):
+        for k in range(inverse.shape[2] // CZ):
+            at = FINE_CORNER_LINES + (f * GROUPS + k) * GROUPS
+            value = inverse[f, :, k * CZ : (k + 1) * CZ]
+            up[at : at + GROUPS, :] = value
+            down[at : at + GROUPS, :] = value
     for f in range(FIELDS):
         for i in range(2):
             constants[2 * f + i : 2 * f + i + 1, :] = jnp.broadcast_to(
                 reaction[i : i + 1, f : f + 1], (1, CZ)
             )
-    for f in range(FIELDS):
-        for k in range(mine.shape[2] // CZ):
-            at = (f * GROUPS + k) * GROUPS
-            kin[0, at : at + GROUPS, :] = mine[f, :, k * CZ : (k + 1) * CZ]
-
     def pack(low, high):
         for side, ref in enumerate((low, high)):
-            kin[1 + side] = ref[BAND_LINES : BAND_LINES + KIN_LINES, :]
             for f in range(FIELDS + 1):
                 for j, offset in FINE_CORNER_AT.items():
                     size = 6 - j
@@ -154,61 +159,179 @@
     by_parity(pack, first, second)
 
 
-def smooth_first(
+def halo_row(j, is_high):
+    return FO + CY - 1 + j if is_high else FO + FN - j
+
+
+def go_round(ref, f, x, value):
+    ref[f, x, ALL, :] = value
+    ref[f, x, FO - 1 : FO, :] = value[FN - 1 : FN]
+    ref[f, x, FO + FN : FO + FN + 1, :] = value[0:1]
+
+
+def fine_scale(x, reaction, code, s, inv, p0):
+    kind = code[x, ALL, :]
+    for f in range(FIELDS):
+        inverse = inverse_of(kind, reaction, f)
+        inv[f, x, ALL, :] = inverse
+        if p0 is not None:
+            value = inverse * s[f, x, ALL, :]
+            s[f, x, ALL, :] = value
+            go_round(p0, f, x, value * (1.0 / THETA))
+
+
+def fine_sweep(x, k, s, inv, parts):
+    keep, gain = coefficients()[k]
+    for f in range(FIELDS):
+        here, total = beside(parts[k], f, x, FO, FN, 1)
+        value = s[f, x, ALL, :] - here + inv[f, x, ALL, :] * total
+        s[f, x, ALL, :] = value
+        go_round(parts[k + 1], f, x, keep * here + gain * value)
+
+
+def fine_last(x, reaction, code, s, inv, p3, scaled, line):
+    residues = []
+    for f in range(FIELDS):
+        fluid, solid = diagonal_values(reaction, f)
+        here, total = beside(p3, f, x, FO, CY, 1)
+        value = s[f, x, OWN, :] - here + inv[f, x, OWN, :] * total
+        scaled[f, line : line + CY, :] = value
+        residues.append(jnp.where(code[x, OWN, :] == 1.0, solid, fluid) * value)
+    return residues
+
+
+def restrict(x, residues, code, pair, coarse, line):
+    parity = lanes() % 2 == 0
+    sums = [one + other for one, other in zip(*residues)]
+    sums.append(code[x, OWN, :] + code[x + 1, OWN, :])
+    halves = []
+    for f, value in enumerate(sums):
+        here = pair.at[x // 2 % 2, f]
+        here[...] = value
+        halves.append(here[pl.ds(0, HY, stride=2), :] + here[pl.ds(1, HY, stride=2), :])
+    halves.append(halves[4])
+    for plane in range(3):
+        even, odd = halves[2 * plane], halves[2 * plane + 1]
+        merged = jnp.where(
+            parity, even + pltpu.roll(even, CZ - 1, 1), odd + pltpu.roll(odd, 1, 1)
+        )
+        merged = merged * 0.5 if plane < 2 else jnp.where(merged > 8.5, -1.0, merged)
+        coarse[plane, line : line + HY, :] = merged
+
+
+def lay_own(x_at, xs, b, material, s, code):
+    zeros = jnp.zeros((8, CZ), jnp.float32)
+    for x in xs:
+        for f in range(FIELDS):
+            s[f, x + x_at, OWN, :] = b[f, x * CY : x * CY + CY, :]
+            s[f, x + x_at, FO + CY : FO + FN, :] = zeros
+        code[x + x_at, OWN, :] = material[x * CY : x * CY + CY, :].astype(jnp.float32)
+        code[x + x_at, FO + CY : FO + FN, :] = zeros + 2.0
+
+
+def putter(s, code):
+    sflat = s.reshape(FIELDS, s.shape[1] * FY, CZ)
+    cflat = code.reshape(s.shape[1] * FY, CZ)
+
+    def put(f, x, y_row, size, value):
+        to = pl.ds(x * FY + y_row, size, stride=FY)
+        if f < FIELDS:
+            sflat[f, to, :] = value
+        else:
+            cflat[to, :] = value
+
+    return put
+
+
+def lay_bands(x_at, spans, ncol, put, even, odd):
+    _, col = place()
+
+    def bands(ref, is_high):
+        for f in range(FIELDS + 1):
+            for i in range(4):
+                at = (f * 4 + i) * CX
+                row = halo_row(i + 1 if is_high else 4 - i, is_high)
+                for x, size in spans:
+                    put(f, x + x_at, row, size, ref[at + x : at + x + size, :])
+
+    def sides(low, high):
+        pl.when(col > 0)(functools.partial(bands, low, 0))
+        pl.when(col < ncol - 1)(functools.partial(bands, high, 1))
+
+    by_parity(sides, even, odd)
+
+
+def kept_lines():
+    for side in range(2):
+        for k in range(1, SWEEPS):
+            flip = lambda x: CX - 1 - x if side else x
+            yield side, k, (flip(k), flip(k + 1)), flip(k)
+
+
+def smooth_middle(
+    nrow, ncol, reaction, b, material, even, odd,
+    first, scaled, coarse, keep_p, keep_s, keep_sum,
+    s, inv, p0, p1, p2, p3, code, pair,
+):
+    parts = (p0, p1, p2, p3)
+    lay_own(0, range(CX), b, material, s, code)
+    lay_bands(0, ((0, CX),), ncol, putter(s, code), even, odd)
+    every(0, CX, lambda x: fine_scale(x, reaction, code, s, inv, p0))
+    for k in range(SWEEPS - 1):
+        every(k + 1, CX - k - 1, lambda x: fine_sweep(x, k, s, inv, parts))
+        for side, step, lines, line in kept_lines():
+            if step == k + 1:
+                for f in range(FIELDS):
+                    for i, x in enumerate(lines):
+                        keep_p[side, k, i, f] = parts[step][f, x]
+                    keep_s[side, k, f] = s[f, line, ALL, :]
+    for x in range(*MID, 2):
+        residues = []
+        for h in range(2):
+            line = (x + h - MID[0]) * CY
+            residues.append(fine_last(x + h, reaction, code, s, inv, p3, scaled, line))
+            for f in range(FIELDS):
+                first[f, line : line + CY, :] = sum(p[f, x + h, OWN, :] for p in parts)
+        restrict(x, residues, code, pair, coarse, (x - MID[0]) // 2 * HY)
+    for side in range(2):
+        for i in range(1, SWEEPS):
+            x = CX - 1 - i if side else i
+            for f in range(FIELDS):
+                keep_sum[side, i - 1, f] = sum(p[f, x, OWN, :] for p in parts[: i + 1])
+
+
+def smooth_outer(
     nrow, ncol, reaction, b, material, above, below, even, odd, kabove, kbelow,
+    mid_first, mid_scaled, mid_coarse, keep_p, keep_s, keep_sum,
     first, scaled, code, coarse, up, down, side_even, side_odd,
     s, inv, p0, p1, p2, p3, pair,
 ):
     row, col = place()
     parts = (p0, p1, p2, p3)
-    zeros = jnp.zeros((FY, CZ), jnp.float32)
+    at_x = 6
+    zeros = jnp.zeros((FN, CZ), jnp.float32)
     for x in (*range(6), *range(GX - 6, GX)):
         for f in range(FIELDS):
-            s[f, x, 8:56, :] = zeros[:48]
-        code[x] = zeros + 2.0
-
-    def own(i):
-        x = i + 6
-        for f in range(FIELDS):
-            s[f, x, 8:16, :] = zeros[:8]
-            s[f, x, 16:48, :] = b[f, i * CY : i * CY + CY, :]
-            s[f, x, 48:56, :] = zeros[:8]
-        code[x, 0:16, :] = zeros[:16] + 2.0
-        code[x, 16:48, :] = material[i * CY : i * CY + CY, :].astype(jnp.float32)
-        code[x, 48:64, :] = zeros[:16] + 2.0
-
-    every(0, CX, own)
-    sflat = s.reshape(FIELDS, GX * FY, CZ)
-    cflat = code.reshape(GX * FY, CZ)
-
-    def put(f, start, size, value):
-        if f < FIELDS:
-            sflat[f, pl.ds(start, size, stride=FY), :] = value
-        else:
-            cflat[pl.ds(start, size, stride=FY), :] = value
+            s[f, x, ALL, :] = zeros
+        code[x, ALL, :] = zeros + 2.0
+    outer = (*range(4), *range(CX - 4, CX))
+    lay_own(at_x, outer, b, material, s, code)
+    for x in range(4, CX - 4):
+        code[x + at_x, OWN, :] = material[x * CY : x * CY + CY, :].astype(jnp.float32)
+        code[x + at_x, FO + CY : FO + FN, :] = zeros[:8] + 2.0
+    put = putter(s, code)
 
     def rows(first_x, ref):
         for i in range(6):
             for f in range(FIELDS):
                 at = (f * 6 + i) * CY
-                s[f, first_x + i, 16:48, :] = ref[at : at + CY, :]
+                s[f, first_x + i, OWN, :] = ref[at : at + CY, :]
             at = (FIELDS * 6 + i) * CY
-            code[first_x + i, 16:48, :] = ref[at : at + CY, :]
+            code[first_x + i, OWN, :] = ref[at : at + CY, :]
 
     pl.when(row > 0)(functools.partial(rows, 0, above))
     pl.when(row < nrow - 1)(functools.partial(rows, GX - 6, below))
-
-    def bands(ref, first_y):
-        for f in range(FIELDS + 1):
-            for i in range(4):
-                at = (f * 4 + i) * CX
-                put(f, 6 * FY + first_y + i, CX, ref[at : at + CX, :])
-
-    def sides(low, high):
-        pl.when(col > 0)(functools.partial(bands, low, FO - 4))
-        pl.when(col < ncol - 1)(functools.partial(bands, high, FO + CY))
-
-    by_parity(sides, even, odd)
+    lay_bands(at_x, ((0, CX),), ncol, put, even, odd)
 
     def corners(ref, is_above, is_high):
         for f in range(FIELDS + 1):
@@ -216,75 +339,60 @@
                 size = 6 - j
                 at = (f * 2 + is_high) * 16 + offset
                 x = 6 - size if is_above else 6 + CX
-                y = FO + CY - 1 + j if is_high else FO - j
-                put(f, x * FY + y, size, ref[at : at + size, :])
+                put(f, x, halo_row(j, is_high), size, ref[at : at + size, :])
 
     for ref, is_above, in_x in ((kabove, 1, row > 0), (kbelow, 0, row < nrow - 1)):
         for is_high, in_y in ((0, col > 0), (1, col < ncol - 1)):
             pl.when(in_x & in_y)(functools.partial(corners, ref, is_above, is_high))
 
-    def scale(x):
-        kind = code[x, 8:56, :]
+    def both(low, high, step):
+        for x in range(low, high):
+            step(x + at_x)
+            step(CX - 1 - x + at_x)
+
+    both(-6, 2, lambda x: fine_scale(x, reaction, code, s, inv, p0))
+    both(2, 4, lambda x: fine_scale(x, reaction, code, s, inv, None))
+    for side, k, lines, line in kept_lines():
         for f in range(FIELDS):
-            inverse = inverse_of(kind, reaction, f)
-            value = inverse * s[f, x, 8:56, :]
-            inv[f, x, 8:56, :] = inverse
-            s[f, x, 8:56, :] = value
-            p0[f, x, 8:56, :] = value * (1.0 / THETA)
-
-    every(0, GX, scale)
-
-    for k, (keep, gain) in enumerate(coefficients()):
-        def sweep(x):
+            for i, x in enumerate(lines):
+                parts[k][f, x + at_x] = keep_p[side, k - 1, i, f]
+    for k in range(SWEEPS - 1):
+        if k > 0:
+            for side, step, lines, line in kept_lines():
+                if step == k:
+                    for f in range(FIELDS):
+                        s[f, line + at_x, ALL, :] = keep_s[side, k - 1, f]
+        both(k - 5, k + 1, lambda x: fine_sweep(x, k, s, inv, parts))
+    for side, step, lines, line in kept_lines():
+        if step == SWEEPS - 1:
             for f in range(FIELDS):
-                here, total = beside(parts[k], f, x, 8, 48, 1)
-                value = s[f, x, 8:56, :] - here + inv[f, x, 8:56, :] * total
-                s[f, x, 8:56, :] = value
-                parts[k + 1][f, x, 8:56, :] = keep * here + gain * value
-
-        every(k + 1, GX - k - 1, sweep)
-
-    parity = lanes() % 2 == 0
-
-    def finish(i):
-        at_y = i * 2 * CY
-        inside = 1 <= i <= HX
-        sums = []
-        for f in range(FIELDS):
-            fluid, solid = diagonal_values(reaction, f)
-            residue = jnp.zeros((CY, CZ), jnp.float32)
-            for h in range(2):
-                x = i * 2 + h + 4
-                row_at = (i * 2 + h - 2) * CY
-                here, total = beside(p3, f, x, 16, CY, 1)
-                value = s[f, x, 16:48, :] - here + inv[f, x, 16:48, :] * total
-                out = pl.ds(at_y + h * CY, CY)
-                scaled[f, out, :] = value
-                if inside:
-                    first[f, row_at : row_at + CY, :] = (
-                        p0[f, x, 16:48, :] + p1[f, x, 16:48, :] + p2[f, x, 16:48, :] + here
-                    )
-                residue = residue + jnp.where(code[x, 16:48, :] == 1.0, solid, fluid) * value
-            sums.append(residue)
-        sums.append(code[i * 2 + 4, 16:48, :] + code[i * 2 + 5, 16:48, :])
-        halves = []
-        for f, value in enumerate(sums):
-            here = pair.at[i % 2, f]
-            here[...] = value
-            halves.append(here[pl.ds(0, HY, stride=2), :] + here[pl.ds(1, HY, stride=2), :])
-        halves.append(halves[4])
-        out = pl.ds(i * HY, HY)
-        for plane in range(3):
-            even, odd = halves[2 * plane], halves[2 * plane + 1]
-            merged = jnp.where(
-                parity, even + pltpu.roll(even, CZ - 1, 1), odd + pltpu.roll(odd, 1, 1)
+                s[f, line + at_x, ALL, :] = keep_s[side, step - 1, f]
+    for x in (*range(-2, 4, 2), *range(CX - 4, CX + 2, 2)):
+        residues = []
+        for h in range(2):
+            line = (x + h + 2) * CY
+            residues.append(
+                fine_last(x + h + at_x, reaction, code, s, inv, p3, scaled, line)
             )
-            if plane < 2:
-                coarse[plane, out, :] = merged * 0.5
+        restrict(x + at_x, residues, code, pair, coarse, (x // 2 + 1) * HY)
+    for f in range(FIELDS):
+        for x in range(CX):
+            out = slice(x * CY, x * CY + CY)
+            side = x >= CX // 2
+            i = CX - 1 - x if side else x
+            if i < 4:
+                some = [p[f, x + at_x, OWN, :] for p in (parts if i == 0 else parts[i + 1 :])]
+                if i > 0:
+                    some.append(keep_sum[int(side), i - 1, f])
+                first[f, out, :] = sum(some)
             else:
-                coarse[plane, out, :] = jnp.where(merged > 8.5, -1.0, merged)
-
-    every(0, VX, finish)
+                mid = slice((x - MID[0]) * CY, (x - MID[0] + 1) * CY)
+                first[f, out, :] = mid_first[f, mid, :]
+                scaled[f, (x + 2) * CY : (x + 3) * CY, :] = mid_scaled[f, mid, :]
+    for plane in range(3):
+        size = (MID[1] - MID[0]) // 2 * HY
+        at = (MID[0] // 2 + 1) * HY
+        coarse[plane, at : at + size, :] = mid_coarse[plane]
 
     for f in range(FIELDS):
         at = COARSE_LINES + f * CY
@@ -294,6 +402,15 @@
         at, size = plane * (HX + 1) * HY, (HX + 1) * HY
         up[at : at + size, :] = coarse[plane, 0:size, :]
         down[at : at + size, :] = coarse[plane, HY : HY + size, :]
+
+    def kin(low, high):
+        for part, ref in enumerate((low, high)):
+            value = ref[BAND_LINES : BAND_LINES + KIN_LINES, :]
+            at = FACE_KIN + part * KIN_LINES
+            up[at : at + KIN_LINES, :] = value
+            down[at : at + KIN_LINES, :] = value
+
+    by_parity(kin, even, odd)
 
     def strips(left, right):
         for plane in range(3):
@@ -468,7 +585,7 @@
 
 
 def smooth_second(
-    nrow, ncol, reaction, gathered, kin, kin_above, kin_below,
+    nrow, ncol, reaction, gathered, kin_mine, kin_up, kin_down, mine,
     start, qscaled, qinverse, first, scaled, code, above, below, even, odd,
     out,
     wide, spread, e, q0, q1, q2, q3, qs, fs, inv, f0, p0, p1, p2,
@@ -511,15 +628,19 @@
     def slab(ref, part):
         def rows_of(f, k):
             at = (f * GROUPS + k) * GROUPS
-            return ref[part, at : at + GROUPS, :]
+            if part is None:
+                return ref[FINE_CORNER_LINES + at : FINE_CORNER_LINES + at + GROUPS, :]
+            at += FACE_KIN + part * KIN_LINES
+            return ref[at : at + GROUPS, :]
 
         return rows_of
 
     in_x = {-1: row > 0, 0: True, 1: row < nrow - 1}
     in_y = {-1: col > 0, 0: True, 1: col < ncol - 1}
-    for dx, ref in ((0, kin), (-1, kin_above), (1, kin_below)):
-        for part, dy in enumerate((0, -1, 1)):
-            step = functools.partial(neighbour, slab(ref, part), dx, dy)
+    for dx, row_ref, ref in ((0, kin_mine, mine), (-1, kin_up, above), (1, kin_down, below)):
+        for part, dy in ((None, 0), (0, -1), (1, 1)):
+            given = row_ref if part is None else ref
+            step = functools.partial(neighbour, slab(given, part), dx, dy)
             if dx == 0 and dy == 0:
                 step()
             else:
@@ -558,27 +679,30 @@
                 else:
                     value = jnp.where(parity, total, pltpu.roll(total, 1, 1))
                 spread[...] = value
-                some = spread[4:28, :]
+                high, low = spread[8:26, :], spread[6:8, :]
                 for h in range(2):
+                    to = f0.at[2 * plane + odd, i * 2 + h]
                     for y in range(2):
-                        f0[2 * plane + odd, i * 2 + h, pl.ds(8 + y, 24, stride=2), :] = some
+                        to[pl.ds(FO + y, 18, stride=2), :] = high
+                        to[pl.ds(FO + FN - 4 + y, 2, stride=2), :] = low
+                    to[FO - 1 : FO, :] = low[1:2]
+                    to[FO + FN : FO + FN + 1, :] = high[0:1]
 
     every(0, HX + 4, lift)
 
-    zeros = jnp.zeros((48, CZ), jnp.float32)
+    zeros = jnp.zeros((FN, CZ), jnp.float32)
     for f in range(FIELDS):
         for x in (1, FX - 2):
-            fs[f, x, 8:56, :] = zeros
+            fs[f, x, ALL, :] = zeros
         for x in range(2, FX - 2):
-            fs[f, x, 8:16, :] = zeros[:8]
-            fs[f, x, 16:48, :] = scaled[f, (x - 2) * CY : (x - 1) * CY, :]
-            fs[f, x, 48:56, :] = zeros[:8]
+            fs[f, x, OWN, :] = scaled[f, (x - 2) * CY : (x - 1) * CY, :]
+            fs[f, x, FO + CY : FO + FN, :] = zeros[:8]
     sflat = fs.reshape(FIELDS, FX * FY, CZ)
 
     def face(x, ref):
         for f in range(FIELDS):
             at = COARSE_LINES + f * CY
-            fs[f, x, 16:48, :] = ref[at : at + CY, :]
+            fs[f, x, OWN, :] = ref[at : at + CY, :]
 
     pl.when(in_x[-1])(functools.partial(face, 1, above))
     pl.when(in_x[1])(functools.partial(face, FX - 2, below))
@@ -588,8 +712,7 @@
             for j, offset in STRIP_AT.items():
                 size = WX + 2 - 2 * j
                 at = STRIP_LINES + f * (3 * WX - 6) + offset
-                y = FO + CY - 1 + j if is_high else FO - j
-                start = (1 + j) * FY + y
+                start = (1 + j) * FY + halo_row(j, is_high)
                 sflat[f, pl.ds(start, size, stride=FY), :] = ref[at : at + size, :]
 
     def sides(low, high):
@@ -601,25 +724,18 @@
     parts = (p0, p1, p2)
 
     def open_fine(x):
-        kind = code[x + 2, 8:56, :]
+        kind = code[x + 2, ALL, :]
         for f in range(FIELDS):
-            here, total = beside(f0, f, x, 8, 48, 1)
+            here, total = beside(f0, f, x, FO, FN, 1)
             inverse = inverse_of(kind, reaction, f)
-            inv[f, x, 8:56, :] = inverse
-            value = fs[f, x, 8:56, :] - here + inverse * total
-            fs[f, x, 8:56, :] = value
-            p0[f, x, 8:56, :] = value * (1.0 / THETA)
+            inv[f, x, ALL, :] = inverse
+            value = fs[f, x, ALL, :] - here + inverse * total
+            fs[f, x, ALL, :] = value
+            go_round(p0, f, x, value * (1.0 / THETA))
 
     every(1, FX - 1, open_fine)
-    for k, (keep, gain) in enumerate(coefficients()[:2]):
-        def sweep(x):
-            for f in range(FIELDS):
-                here, total = beside(parts[k], f, x, 8, 48, 1)
-                value = fs[f, x, 8:56, :] - here + inv[f, x, 8:56, :] * total
-                fs[f, x, 8:56, :] = value
-                parts[k + 1][f, x, 8:56, :] = keep * here + gain * value
-
-        every(k + 2, FX - k - 2, sweep)
+    for k in range(2):
+        every(k + 2, FX - k - 2, lambda x: fine_sweep(x, k, fs, inv, parts))
 
     keep, gain = coefficients()[2]
 
@@ -627,16 +743,16 @@
         x = i + 4
         at = pl.ds(i * CY, CY)
         for f in range(FIELDS):
-            here, total = beside(p2, f, x, 16, CY, 1)
-            value = fs[f, x, 16:48, :] - here + inv[f, x, 16:48, :] * total
-            result = first[f, at, :] + f0[f, x, 16:48, :] + p0[f, x, 16:48, :]
-            result = result + p1[f, x, 16:48, :] + here
+            here, total = beside(p2, f, x, FO, CY, 1)
+            value = fs[f, x, OWN, :] - here + inv[f, x, OWN, :] * total
+            result = first[f, at, :] + f0[f, x, OWN, :] + p0[f, x, OWN, :]
+            result = result + p1[f, x, OWN, :] + here
             out[f, at, :] = result + (keep * here + gain * value)
 
     every(0, CX, close)
 
 
-def call(kernel, out_shapes, scratch, *args, limit=16, in_hbm=False):
+def call(kernel, out_shapes, scratch, *args, limit=16, in_hbm=False, microseconds=0.1):
     vmem = pl.BlockSpec(memory_space=pltpu.VMEM)
     given = pl.BlockSpec(memory_space=pltpu.HBM) if in_hbm else vmem
     return pl.pallas_call(
@@ -648,6 +764,9 @@
             pltpu.VMEM(shape, jnp.float32) if isinstance(shape, tuple) else shape
             for shape in scratch
         ],
+        cost_estimate=pl.CostEstimate(
+            flops=int(microseconds * 1e6), bytes_accessed=int(microseconds * 3.5e6), transcendentals=0
+        ),
         compiler_params=pltpu.CompilerParams(vmem_limit_bytes=int(limit * 1024 * 1024)),
     )(*args)
 
@@ -693,29 +812,35 @@
     )
     odd, even = pairs(odd, True), pairs(even, False)
     above, below = ahead(up), back(down)
-    up, down, kin, reaction = call(
+    up, down, reaction = call(
         pack_corners,
-        [((FIELDS + 1) * 32, CZ)] * 2 + [(3, KIN_LINES, CZ), (2 * FIELDS, CZ)], [],
-        coarse_inverse, even, odd, reaction.T,
+        [(FINE_CORNER_LINES + KIN_LINES, CZ)] * 2 + [(2 * FIELDS, CZ)], [],
+        even, odd, reaction.T, coarse_inverse,
     )
+    mine = up
     kabove, kbelow = ahead(up), back(down)
-    kin, kabove, kbelow = lax.optimization_barrier((kin, kabove, kbelow))
-    kin_above, kin_below = ahead(kin), back(kin)
-
     wide = (FIELDS, WX * CY, CZ)
+    middle = MID[1] - MID[0]
+    padded = (FIELDS, CX, FY, CZ)
+    mids = call(
+        functools.partial(smooth_middle, nrow, ncol),
+        [(FIELDS, middle * CY, CZ)] * 2 + [(3, middle // 2 * HY, CZ),
+         (2, 3, 2, FIELDS, FY, CZ), (2, 3, FIELDS, FN, CZ), (2, 3, FIELDS, CY, CZ)],
+        [padded] * 6 + [padded[1:], (2, FIELDS + 1, CY, CZ)],
+        reaction, b, material, even, odd,
+        limit=16, microseconds=3,
+    )
     padded = (FIELDS, GX, FY, CZ)
     first, scaled, code, coarse, up, down, side_even, side_odd = call(
-        functools.partial(smooth_first, nrow, ncol),
+        functools.partial(smooth_outer, nrow, ncol),
         [fine, wide, padded[1:], (3, VX * HY, CZ)]
         + [(FACE_LINES, CZ)] * 2 + [(SIDE_LINES, CZ)] * 2,
         [padded] * 6 + [(2, FIELDS + 1, CY, CZ)],
-        reaction, b, material, above, below, even, odd, kabove, kbelow,
-        limit=30,
+        reaction, b, material, above, below, even, odd, kabove, kbelow, *mids,
+        limit=26, microseconds=3.5,
     )
-    up, down, side_even, side_odd, kin_above, kin_below = lax.optimization_barrier(
-        (up, down, side_even, side_odd, kin_above, kin_below)
-    )
-
+    kin_row = (mine, kabove, kbelow)
+    mine = up
     odd, even = pairs(side_odd, True), pairs(side_even, False)
     above, below = ahead(up), back(down)
     up, down = call(pack_knots, [(KNOT_LINES, CZ)] * 2, [], even, odd)
@@ -727,7 +852,7 @@
         [(2, HX + 4, 32, CZ), (2, HX + 10, 32, CZ), (2, HX + 10, 32, CZ), (nrow * ncol, CZ)],
         [qpadded, qpadded, qpadded[1:]] + [qpadded] * 4,
         reaction, coarse, above, below, even, odd, kabove, kbelow,
-        limit=14,
+        limit=14, microseconds=2.5,
     )
 
     gathered = lax.all_to_all(sums, ("row", "col"), 0, 0)
@@ -738,9 +863,9 @@
         functools.partial(smooth_second, nrow, ncol),
         [fine],
         [(FIELDS, nrow, CZ), (32, CZ)] + [epadded] * 5 + [(2, EX, 32, CZ)] + [padded] * 6,
-        reaction, gathered, kin, kin_above, kin_below,
+        reaction, gathered, *kin_row, mine,
         start, qscaled, qinverse, first, scaled, code, above, below, even, odd,
-        limit=32,
+        limit=32, microseconds=7,
     )
     return out.reshape(right_side.shape)
 

time: 75.7 us -> 72.1 us (0.952)
  starting transfers between devices: 18 us -> 14.4 us
  waiting for transfers between devices: 13.3 us -> 14.2 us
    ppermute x5 -> x4, starting transfers between devices: 8.35 us -> 2.4 us  [ahead(): lax.ppermute(value, 'row', [(i, (i + 1) % count) for i in range(count)])]
    ppermute x5 -> x4, starting transfers between devices: 1.02 us -> 5.84 us  [back(): lax.ppermute(value, 'row', [((i + 1) % count, i) for i in range(count)])]
    ppermute x4, waiting for transfers between devices: 5.12 us -> 9.65 us  [pairs(): return lax.ppermute(value, ('row', 'col'), moves)]
    ppermute x5 -> x4, waiting for transfers between devices: 6.73 us -> 3.46 us  [back(): lax.ppermute(value, 'row', [((i + 1) % count, i) for i in range(count)])]
    ppermute x4, starting transfers between devices: 8.67 us -> 6.15 us  [pairs(): return lax.ppermute(value, ('row', 'col'), moves)]
    pallas_call x6 -> x7, Pallas kernels: 19.2 us -> 18.5 us  [call(): pl.pallas_call(kernel, out_shape=[jax.ShapeDtypeStruct(shape, jnp.float32...]
  transfers between devices with their start and end apart: 14 -> 12, of which waited for: 7 -> 5; matrix products, arithmetic and copies ran while one was open for 0% -> 0% of each run, Pallas kernels for 9% -> 4%
where the time goes in v3:
time: 72.1 us; the launch traced here: 71.9 us
  blocking collectives  24.8 us (34%)
  Pallas kernels  18.5 us (26%)
  starting transfers between devices  14.4 us (20%)
  waiting for transfers between devices  14.2 us (20%)
    all_to_all x1, blocking collectives, body(): gathered = lax.all_to_all(sums, ('row', 'col'), 0, 0)  24.8 us
    pallas_call x7, Pallas kernels, call(): pl.pallas_call(kernel, out_shape=[jax.ShapeDtypeStruct(shape, jnp.float32...  18.5 us
    ppermute x4, waiting for transfers between devices, pairs(): return lax.ppermute(value, ('row', 'col'), moves)  9.65 us
    ppermute x4, starting transfers between devices, pairs(): return lax.ppermute(value, ('row', 'col'), moves)  6.15 us
    ppermute x4, starting transfers between devices, back(): lax.ppermute(value, 'row', [((i + 1) % count, i) for i in range(count)])  5.84 us
    ppermute x4, waiting for transfers between devices, back(): lax.ppermute(value, 'row', [((i + 1) % count, i) for i in range(count)])  3.46 us
    ppermute x4, starting transfers between devices, ahead(): lax.ppermute(value, 'row', [(i, (i + 1) % count) for i in range(count)])  2.4 us
  transfers between devices with their start and end apart: 12, of which 5 were waited for; matrix products, arithmetic and copies ran while one was open for 0% of the time, Pallas kernels for 4%

profile of v3, /device:TPU:1, one launch (start us, length us, event | category | flops | bytes accessed | tf_op | source)
XLA Modules:
  0.0 71.9 jit_solution(1832946923640430871)
XLA Ops:
  0.0 0.0 copy-start.2
  0.0 0.0 copy-start.1
  0.0 0.0 copy-start
  0.0 0.0 copy-start.3
  0.0 2.6 %shard_map.46 = (f32[960,128]{1,0:T(8,128)}, f32[960,128]{1,0:T(8,128)}, f32[576,128]{1,0:T(8,128)}, f32[576,128]{1,0:T(8,128)}) custom-call(f32[4,512,128]{2,1,0:T(8,128)} %bitcast.8, s32[512,128]{1,0:T(8,128)} %bitcast.11, f32[4,8,1024]{2,1,0:T(8,128)} %inverse.3), custom_call_target="tpu_custom_call" | custom-call | flops 100000 | bytes 350000 | tf_op jit(solution)/shard_map/pallas_call | solution.py:758
  2.6 2.2 %collective-permute-start = (f32[576,128]{1,0:T(8,128)}, f32[576,128]{1,0:T(8,128)S(1)}, u32[]{:S(2)}, u32[]{:S(2)}) collective-permute-start(f32[576,128]{1,0:T(8,128)} %get-tuple-element.32), channel_id=1, source_target_pairs={{0,1},{1,0},{2,3},{3,2},{4,5},{5,4},{6,7},{7,6},{8,9},{9,8},{10,11... | collective-permute-start | bytes 884744 | tf_op jit(solution)/shard_map/ppermute | solution.py:796
  4.9 1.0 %collective-permute-start.1 = (f32[576,128]{1,0:T(8,128)}, f32[576,128]{1,0:T(8,128)S(1)}, u32[]{:S(2)}, u32[]{:S(2)}) collective-permute-start(f32[576,128]{1,0:T(8,128)} %get-tuple-element.33), channel_id=1, source_target_pairs={{0,16},{1,2},{2,1},{3,4},{4,3},{5,6},{6,5},{7,8},{8,7},{9,10},{10,... | collective-permute-start | bytes 884744 | tf_op jit(solution)/shard_map/ppermute | solution.py:796
  5.8 1.1 %collective-permute-start.2 = (f32[960,128]{1,0:T(8,128)}, f32[960,128]{1,0:T(8,128)S(1)}, u32[]{:S(2)}, u32[]{:S(2)}) collective-permute-start(f32[960,128]{1,0:T(8,128)} %get-tuple-element.35), channel_id=1, source_target_pairs={{0,16},{16,32},{32,48},{48,64},{64,80},{80,96},{96,112},{112,0},{1... | collective-permute-start | bytes 1474568 | tf_op jit(solution)/shard_map/ppermute | solution.py:776
  6.9 0.0 collective-permute-start.3
  6.9 4.5 %collective-permute-done.first.even = f32[576,128]{1,0:T(8,128)S(1)} collective-permute-done((f32[576,128]{1,0:T(8,128)}, f32[576,128]{1,0:T(8,128)S(1)}, u32[]{:S(2)}, u32[]{:S(2)}) %collective-permute-start) | collective-permute-done | bytes 294944 | tf_op jit(solution)/shard_map/ppermute | solution.py:796
  11.4 0.0 collective-permute-done.1.second.odd
  11.4 0.0 copy-done.2
  11.4 0.0 copy-done.3
  11.4 0.1 shard_map.47
  11.5 1.6 %collective-permute-start.5 = (f32[416,128]{1,0:T(8,128)S(1)}, f32[416,128]{1,0:T(8,128)S(1)}, u32[]{:S(2)}, u32[]{:S(2)}) collective-permute-start(f32[416,128]{1,0:T(8,128)S(1)} %get-tuple-element.38), channel_id=1, source_target_pairs={{16,0},{32,16},{48,32},{64,48},{80,64},{96,80},{112,96},{0,112},{1... | collective-permute-start | bytes 638984 | tf_op jit(solution)/shard_map/ppermute | solution.py:781
  13.1 1.3 %collective-permute-start.4 = (f32[416,128]{1,0:T(8,128)S(1)}, f32[416,128]{1,0:T(8,128)S(1)}, u32[]{:S(2)}, u32[]{:S(2)}) collective-permute-start(f32[416,128]{1,0:T(8,128)S(1)} %get-tuple-element.37.kin_mine), channel_id=1, source_target_pairs={{0,16},{16,32},{32,48},{48,64},{64,80},{80,96},{96,112},{112,0},{1... | collective-permute-start | bytes 638984 | tf_op jit(solution)/shard_map/ppermute | solution.py:776
  14.4 0.0 copy-done.1
  14.4 0.0 copy-done
  14.4 2.8 %shard_map.48 = (f32[4,256,128]{2,1,0:T(8,128)S(1)}, f32[4,256,128]{2,1,0:T(8,128)S(1)}, f32[3,64,128]{2,1,0:T(8,128)S(1)}, f32[2,3,2,4,56,128]{5,4,3,2,1,0:T(8,...) custom-call(f32[8,128]{1,0:T(8,128)S(1)} %get-tuple-element.34.reaction, ...), custom_call_target="tpu_custom_call" | custom-call | flops 3000000 | bytes 10500000 | tf_op jit(solution)/shard_map/pallas_call | solution.py:758
  17.2 0.0 collective-permute-done.2.above
  17.2 0.0 collective-permute-done.3.below
  17.2 0.7 collective-permute-done.5.kbelow.kin_down
  17.9 0.0 collective-permute-done.4.kabove.kin_up
  17.9 3.5 %shard_map.49 = (f32[4,512,128]{2,1,0:T(8,128)S(1)}, f32[4,640,128]{2,1,0:T(8,128)S(1)}, f32[28,56,128]{2,1,0:T(8,128)S(1)}, f32[3,160,128]{2,1,0:T(8,128)S(1)},...) custom-call(f32[8,128]{1,0:T(8,128)S(1)} %get-tuple-element.34.reaction, ...), custom_call_target="tpu_custom_call" | custom-call | flops 3500000 | bytes 12250000 | tf_op jit(solution)/shard_map/pallas_call | solution.py:758
  21.4 3.1 %collective-permute-start.7 = (f32[1072,128]{1,0:T(8,128)S(1)}, f32[1072,128]{1,0:T(8,128)S(1)}, u32[]{:S(2)}, u32[]{:S(2)}) collective-permute-start(f32[1072,128]{1,0:T(8,128)S(1)} %get-tuple-element.47), channel_id=1, source_target_pairs={{16,0},{32,16},{48,32},{64,48},{80,64},{96,80},{112,96},{0,112},{1... | collective-permute-start | bytes 1646600 | tf_op jit(solution)/shard_map/ppermute | solution.py:781
  24.5 0.0 collective-permute-start.6
  24.6 2.2 %collective-permute-start.8 = (f32[488,128]{1,0:T(8,128)S(1)}, f32[488,128]{1,0:T(8,128)S(1)}, u32[]{:S(2)}, u32[]{:S(2)}) collective-permute-start(f32[488,128]{1,0:T(8,128)S(1)} %get-tuple-element.48), channel_id=1, source_target_pairs={{0,1},{1,0},{2,3},{3,2},{4,5},{5,4},{6,7},{7,6},{8,9},{9,8},{10,11... | collective-permute-start | bytes 749576 | tf_op jit(solution)/shard_map/ppermute | solution.py:796
  26.8 0.8 %collective-permute-start.9 = (f32[488,128]{1,0:T(8,128)S(1)}, f32[488,128]{1,0:T(8,128)S(1)}, u32[]{:S(2)}, u32[]{:S(2)}) collective-permute-start(f32[488,128]{1,0:T(8,128)S(1)} %get-tuple-element.49), channel_id=1, source_target_pairs={{0,16},{1,2},{2,1},{3,4},{4,3},{5,6},{6,5},{7,8},{8,7},{9,10},{10,... | collective-permute-start | bytes 749576 | tf_op jit(solution)/shard_map/ppermute | solution.py:796
  27.5 5.2 %collective-permute-done.8.first.even = f32[488,128]{1,0:T(8,128)S(1)} collective-permute-done((f32[488,128]{1,0:T(8,128)S(1)}, f32[488,128]{1,0:T(8,128)S(1)}, u32[]{:S(2)}, u32[]{:S(2)}) %collective-permute-start.8) | collective-permute-done | bytes 249888 | tf_op jit(solution)/shard_map/ppermute | solution.py:796
  32.7 0.0 collective-permute-done.9.second.odd
  32.8 0.0 collective-permute-start.10
  32.8 1.1 %collective-permute-start.11 = (f32[288,128]{1,0:T(8,128)S(1)}, f32[288,128]{1,0:T(8,128)S(1)}, u32[]{:S(2)}, u32[]{:S(2)}) collective-permute-start(f32[288,128]{1,0:T(8,128)S(1)} %get-tuple-element.51), channel_id=1, source_target_pairs={{16,0},{32,16},{48,32},{64,48},{80,64},{96,80},{112,96},{0,112},{1... | collective-permute-start | bytes 442376 | tf_op jit(solution)/shard_map/ppermute | solution.py:781
  33.8 1.0 %collective-permute-done.10.kabove = f32[288,128]{1,0:T(8,128)S(1)} collective-permute-done((f32[288,128]{1,0:T(8,128)S(1)}, f32[288,128]{1,0:T(8,128)S(1)}, u32[]{:S(2)}, u32[]{:S(2)}) %collective-permute-start.10) | collective-permute-done | bytes 147488 | tf_op jit(solution)/shard_map/ppermute | solution.py:776
  34.9 2.8 %collective-permute-done.11.kbelow = f32[288,128]{1,0:T(8,128)S(1)} collective-permute-done((f32[288,128]{1,0:T(8,128)S(1)}, f32[288,128]{1,0:T(8,128)S(1)}, u32[]{:S(2)}, u32[]{:S(2)}) %collective-permute-start.11) | collective-permute-done | bytes 147488 | tf_op jit(solution)/shard_map/ppermute | solution.py:781
  37.7 0.0 collective-permute-done.7.below
  37.7 0.0 collective-permute-done.6.above
  37.7 2.5 %shard_map.51 = (f32[2,12,32,128]{3,2,1,0:T(8,128)S(1)}, f32[2,18,32,128]{3,2,1,0:T(8,128)S(1)}, f32[2,18,32,128]{3,2,1,0:T(8,128)S(1)}, f32[128,128]{1,0:T(8,128)S(1)}) custom-call(f32[8,128]{1,0:T(8,128)S(1)} %get-tuple-element.34.reaction, f32[3,160,128]{2,1,0:T(8,128)S(1)} %get-tuple-element.45.coarse, f32[1072,128]{1,0:T(8,128)S(1)} %collective-permute-done.6.above, ...), custom_call_target="tpu_custom_call" | custom-call | flops 2500000 | bytes 8750000 | tf_op jit(solution)/shard_map/pallas_call | solution.py:758
  40.1 24.8 %all_to_all.11 = f32[128,1,128]{2,1,0:T(1,128)S(1)} all-to-all(f32[128,1,128]{2,1,0:T(1,128)S(1)} %bitcast.15), channel_id=1, replica_groups=mesh['row'=8,'col'=16] {'row','col'}, dimensions={0} | all-to-all | bytes 131072 | tf_op jit(solution)/shard_map/all_to_all | solution.py:858
  64.9 7.0 %shard_map.52 = f32[4,512,128]{2,1,0:T(8,128)} custom-call(f32[8,128]{1,0:T(8,128)S(1)} %get-tuple-element.34.reaction, f32[128,128]{1,0:T(8,128)S(1)} %bitcast.14, f32[416,128]{1,0:T(8,128)S(1)} %get-tuple-element.37.kin_mine, f32[416,128]{1,0:T(8,128)S(1)} %collective-permute-done.4.kabove.kin_up, f32[416,128]{1,0:T(8,128)S(1)} %collective-permute-done.5.kbelow.kin_down, ...), custom_call_target="tpu_custom_call" | custom-call | flops 7000000 | bytes 24500000 | tf_op jit(solution)/shard_map/pallas_call | solution.py:758
  (1 shorter events, 0.0 us)
Async XLA Ops:
  0.0 11.4 %copy-start.2 = (f32[4,8,1024]{2,1,0:T(8,128)S(1)}, f32[4,8,1024]{2,1,0:T(8,128)}, u32[]{:S(2)}) copy-start(f32[4,8,1024]{2,1,0:T(8,128)} %inverse.3) | copy-start | bytes 393220
  0.0 14.4 %copy-start.1 = (s32[16,32,128]{2,1,0:T(8,128)S(1)}, s32[16,32,128]{2,1,0:T(8,128)}, u32[]{:S(2)}) copy-start(s32[16,32,128]{2,1,0:T(8,128)} %param.5) | copy-start | bytes 786436
  0.0 14.4 %copy-start = (f32[4,16,32,128]{3,2,1,0:T(8,128)S(1)}, f32[4,16,32,128]{3,2,1,0:T(8,128)}, u32[]{:S(2)}) copy-start(f32[4,16,32,128]{3,2,1,0:T(8,128)} %param.4) | copy-start | bytes 3145732
  0.0 11.4 %copy-start.3 = (f32[4,2]{0,1:T(2,128)S(1)}, f32[4,2]{0,1:T(2,128)}, u32[]{:S(2)}) copy-start(f32[4,2]{0,1:T(2,128)} %param.6) | copy-start | bytes 100
  2.6 8.7 %collective-permute-start = (f32[576,128]{1,0:T(8,128)}, f32[576,128]{1,0:T(8,128)S(1)}, u32[]{:S(2)}, u32[]{:S(2)}) collective-permute-start(f32[576,128]{1,0:T(8,128)} %get-tuple-element.32), channel_id=1, source_target_pairs={{0,1},{1,0},{2,3},{3,2},{4,5},{5,4},{6,7},{7,6},{8,9},{9,8},{10,11... | collective-permute-start | bytes 884744 | tf_op jit(solution)/shard_map/ppermute | solution.py:796
  4.9 6.5 %collective-permute-start.1 = (f32[576,128]{1,0:T(8,128)}, f32[576,128]{1,0:T(8,128)S(1)}, u32[]{:S(2)}, u32[]{:S(2)}) collective-permute-start(f32[576,128]{1,0:T(8,128)} %get-tuple-element.33), channel_id=1, source_target_pairs={{0,16},{1,2},{2,1},{3,4},{4,3},{5,6},{6,5},{7,8},{8,7},{9,10},{10,... | collective-permute-start | bytes 884744 | tf_op jit(solution)/shard_map/ppermute | solution.py:796
  5.8 11.4 %collective-permute-start.2 = (f32[960,128]{1,0:T(8,128)}, f32[960,128]{1,0:T(8,128)S(1)}, u32[]{:S(2)}, u32[]{:S(2)}) collective-permute-start(f32[960,128]{1,0:T(8,128)} %get-tuple-element.35), channel_id=1, source_target_pairs={{0,16},{16,32},{32,48},{48,64},{64,80},{80,96},{96,112},{112,0},{1... | collective-permute-start | bytes 1474568 | tf_op jit(solution)/shard_map/ppermute | solution.py:776
  6.9 10.3 %collective-permute-start.3 = (f32[960,128]{1,0:T(8,128)}, f32[960,128]{1,0:T(8,128)S(1)}, u32[]{:S(2)}, u32[]{:S(2)}) collective-permute-start(f32[960,128]{1,0:T(8,128)} %get-tuple-element.36), channel_id=1, source_target_pairs={{16,0},{32,16},{48,32},{64,48},{80,64},{96,80},{112,96},{0,112},{1... | collective-permute-start | bytes 1474568 | tf_op jit(solution)/shard_map/ppermute | solution.py:781
  11.5 6.4 %collective-permute-start.5 = (f32[416,128]{1,0:T(8,128)S(1)}, f32[416,128]{1,0:T(8,128)S(1)}, u32[]{:S(2)}, u32[]{:S(2)}) collective-permute-start(f32[416,128]{1,0:T(8,128)S(1)} %get-tuple-element.38), channel_id=1, source_target_pairs={{16,0},{32,16},{48,32},{64,48},{80,64},{96,80},{112,96},{0,112},{1... | collective-permute-start | bytes 638984 | tf_op jit(solution)/shard_map/ppermute | solution.py:781
  13.1 4.8 %collective-permute-start.4 = (f32[416,128]{1,0:T(8,128)S(1)}, f32[416,128]{1,0:T(8,128)S(1)}, u32[]{:S(2)}, u32[]{:S(2)}) collective-permute-start(f32[416,128]{1,0:T(8,128)S(1)} %get-tuple-element.37.kin_mine), channel_id=1, source_target_pairs={{0,16},{16,32},{32,48},{48,64},{64,80},{80,96},{96,112},{112,0},{1... | collective-permute-start | bytes 638984 | tf_op jit(solution)/shard_map/ppermute | solution.py:776
  21.4 16.3 %collective-permute-start.7 = (f32[1072,128]{1,0:T(8,128)S(1)}, f32[1072,128]{1,0:T(8,128)S(1)}, u32[]{:S(2)}, u32[]{:S(2)}) collective-permute-start(f32[1072,128]{1,0:T(8,128)S(1)} %get-tuple-element.47), channel_id=1, source_target_pairs={{16,0},{32,16},{48,32},{64,48},{80,64},{96,80},{112,96},{0,112},{1... | collective-permute-start | bytes 1646600 | tf_op jit(solution)/shard_map/ppermute | solution.py:781
  24.5 13.1 %collective-permute-start.6 = (f32[1072,128]{1,0:T(8,128)S(1)}, f32[1072,128]{1,0:T(8,128)S(1)}, u32[]{:S(2)}, u32[]{:S(2)}) collective-permute-start(f32[1072,128]{1,0:T(8,128)S(1)} %get-tuple-element.46.mine), channel_id=1, source_target_pairs={{0,16},{16,32},{32,48},{48,64},{64,80},{80,96},{96,112},{112,0},{1... | collective-permute-start | bytes 1646600 | tf_op jit(solution)/shard_map/ppermute | solution.py:776
  24.6 8.2 %collective-permute-start.8 = (f32[488,128]{1,0:T(8,128)S(1)}, f32[488,128]{1,0:T(8,128)S(1)}, u32[]{:S(2)}, u32[]{:S(2)}) collective-permute-start(f32[488,128]{1,0:T(8,128)S(1)} %get-tuple-element.48), channel_id=1, source_target_pairs={{0,1},{1,0},{2,3},{3,2},{4,5},{5,4},{6,7},{7,6},{8,9},{9,8},{10,11... | collective-permute-start | bytes 749576 | tf_op jit(solution)/shard_map/ppermute | solution.py:796
  26.8 6.0 %collective-permute-start.9 = (f32[488,128]{1,0:T(8,128)S(1)}, f32[488,128]{1,0:T(8,128)S(1)}, u32[]{:S(2)}, u32[]{:S(2)}) collective-permute-start(f32[488,128]{1,0:T(8,128)S(1)} %get-tuple-element.49), channel_id=1, source_target_pairs={{0,16},{1,2},{2,1},{3,4},{4,3},{5,6},{6,5},{7,8},{8,7},{9,10},{10,... | collective-permute-start | bytes 749576 | tf_op jit(solution)/shard_map/ppermute | solution.py:796
  32.8 2.1 %collective-permute-start.10 = (f32[288,128]{1,0:T(8,128)S(1)}, f32[288,128]{1,0:T(8,128)S(1)}, u32[]{:S(2)}, u32[]{:S(2)}) collective-permute-start(f32[288,128]{1,0:T(8,128)S(1)} %get-tuple-element.50), channel_id=1, source_target_pairs={{0,16},{16,32},{32,48},{48,64},{64,80},{80,96},{96,112},{112,0},{1... | collective-permute-start | bytes 442376 | tf_op jit(solution)/shard_map/ppermute | solution.py:776
  32.8 4.9 %collective-permute-start.11 = (f32[288,128]{1,0:T(8,128)S(1)}, f32[288,128]{1,0:T(8,128)S(1)}, u32[]{:S(2)}, u32[]{:S(2)}) collective-permute-start(f32[288,128]{1,0:T(8,128)S(1)} %get-tuple-element.51), channel_id=1, source_target_pairs={{16,0},{32,16},{48,32},{64,48},{80,64},{96,80},{112,96},{0,112},{1... | collective-permute-start | bytes 442376 | tf_op jit(solution)/shard_map/ppermute | solution.py:781

commit v4 on v3

--- a/solution.py
+++ b/solution.py
@@ -35,8 +35,7 @@
 BAND_LINES = (FIELDS + 1) * 4 * CX
 KIN_LINES = FIELDS * GROUPS * 8
 COARSE_LINES = 3 * (HX + 1) * HY
-FACE_KIN = COARSE_LINES + FIELDS * CY
-FACE_LINES = FACE_KIN + 2 * KIN_LINES
+FACE_LINES = COARSE_LINES + FIELDS * CY
 STRIP_LINES = 272
 STRIP_AT = {1: 0, 2: WX, 3: 2 * WX - 2}
 SIDE_LINES = STRIP_LINES + FIELDS * (3 * WX - 6)
@@ -96,53 +95,62 @@
 
 
 def pack_layers(
-    b, material, inverse, up, down, first, second, b_here, material_here, inverse_here, sems,
+    b, material, inverse, up, down, first, second, own,
+    b_here, material_here, inverse_here, solid, first_here, second_here, own_here, sems, out_sems,
 ):
     copies = [pltpu.make_async_copy(b.at[f], b_here.at[f], sems.at[f]) for f in range(FIELDS)]
     copies.append(pltpu.make_async_copy(material, material_here, sems.at[FIELDS]))
     copies.append(pltpu.make_async_copy(inverse, inverse_here, sems.at[FIELDS + 1]))
     for copy in copies:
         copy.start()
+    sent = []
+
+    def send(source, target):
+        sent.append(pltpu.make_async_copy(source, target, out_sems.at[len(sent)]))
+        sent[-1].start()
+
     for f in range(FIELDS + 1):
         copies[f].wait()
+        layer, band = 6 * CY, 4 * CX
         if f < FIELDS:
             take = lambda start, size, step: b_here[f, pl.ds(start, size, stride=step), :]
+            ends = (b_here.at[f, pl.ds((CX - 6) * CY, layer)], b_here.at[f, pl.ds(0, layer)])
         else:
             take = lambda start, size, step: material_here[
                 pl.ds(start, size, stride=step), :
             ].astype(jnp.float32)
-        at = f * 6 * CY
-        up[at : at + 6 * CY, :] = take((CX - 6) * CY, 6 * CY, 1)
-        down[at : at + 6 * CY, :] = take(0, 6 * CY, 1)
+            solid[0] = take((CX - 6) * CY, layer, 1)
+            solid[1] = take(0, layer, 1)
+            ends = (solid.at[0], solid.at[1])
+        for source, target in zip(ends, (up, down)):
+            send(source, target.at[pl.ds(f * layer, layer)])
 
         def bands(left, right):
             for i in range(4):
-                at = (f * 4 + i) * CX
+                at = f * band + i * CX
                 right[at : at + CX, :] = take(CY - 4 + i, CX, CY)
                 left[at : at + CX, :] = take(i, CX, CY)
 
-        by_parity(bands, first, second)
+        by_parity(bands, first_here, second_here)
+        for source, target in ((first_here, first), (second_here, second)):
+            send(source.at[pl.ds(f * band, band)], target.at[pl.ds(f * band, band)])
     copies[FIELDS + 1].wait()
     for f in range(FIELDS):
         for k in range(inverse.shape[2] // CZ):
-            at = BAND_LINES + (f * GROUPS + k) * GROUPS
-            value = inverse_here[f, :, k * CZ : (k + 1) * CZ]
-            first[at : at + GROUPS, :] = value
-            second[at : at + GROUPS, :] = value
-
-
-def pack_corners(first, second, reaction, inverse, up, down, constants):
-    for f in range(FIELDS):
-        for k in range(inverse.shape[2] // CZ):
-            at = FINE_CORNER_LINES + (f * GROUPS + k) * GROUPS
-            value = inverse[f, :, k * CZ : (k + 1) * CZ]
-            up[at : at + GROUPS, :] = value
-            down[at : at + GROUPS, :] = value
+            at = (f * GROUPS + k) * GROUPS
+            own_here[at : at + GROUPS, :] = inverse_here[f, :, k * CZ : (k + 1) * CZ]
+    send(own_here, own)
+    for copy in sent:
+        copy.wait()
+
+
+def pack_corners(first, second, reaction, up, down, constants):
     for f in range(FIELDS):
         for i in range(2):
             constants[2 * f + i : 2 * f + i + 1, :] = jnp.broadcast_to(
                 reaction[i : i + 1, f : f + 1], (1, CZ)
             )
+
     def pack(low, high):
         for side, ref in enumerate((low, high)):
             for f in range(FIELDS + 1):
@@ -302,8 +310,8 @@
 
 def smooth_outer(
     nrow, ncol, reaction, b, material, above, below, even, odd, kabove, kbelow,
-    mid_first, mid_scaled, mid_coarse, keep_p, keep_s, keep_sum,
-    first, scaled, code, coarse, up, down, side_even, side_odd,
+    own, kin_even, kin_odd, mid_first, mid_scaled, mid_coarse, keep_p, keep_s, keep_sum,
+    first, scaled, code, coarse, up, down, side_even, side_odd, kin,
     s, inv, p0, p1, p2, p3, pair,
 ):
     row, col = place()
@@ -403,14 +411,13 @@
         up[at : at + size, :] = coarse[plane, 0:size, :]
         down[at : at + size, :] = coarse[plane, HY : HY + size, :]
 
-    def kin(low, high):
-        for part, ref in enumerate((low, high)):
-            value = ref[BAND_LINES : BAND_LINES + KIN_LINES, :]
-            at = FACE_KIN + part * KIN_LINES
-            up[at : at + KIN_LINES, :] = value
-            down[at : at + KIN_LINES, :] = value
-
-    by_parity(kin, even, odd)
+    kin[0] = own[...]
+
+    def gather(low, high):
+        kin[1] = low[...]
+        kin[2] = high[...]
+
+    by_parity(gather, kin_even, kin_odd)
 
     def strips(left, right):
         for plane in range(3):
@@ -585,7 +592,7 @@
 
 
 def smooth_second(
-    nrow, ncol, reaction, gathered, kin_mine, kin_up, kin_down, mine,
+    nrow, ncol, reaction, gathered, kin, kin_above, kin_below,
     start, qscaled, qinverse, first, scaled, code, above, below, even, odd,
     out,
     wide, spread, e, q0, q1, q2, q3, qs, fs, inv, f0, p0, p1, p2,
@@ -614,12 +621,14 @@
             total = total + rows_of(f, k) * wide[f, k : k + 1, 0:width]
         return jnp.sum(total, axis=1, keepdims=True)
 
-    def neighbour(rows_of, dx, dy):
+    def neighbour(rows_of, dx, dy, inside):
         for plane in range(2):
             even = product(rows_of, 2 * plane)
             odd = product(rows_of, 2 * plane + 1)
             full = jnp.where(mask[0], even, jnp.where(mask[1], odd, 0.0))
             line = jnp.sum(full, axis=0, keepdims=True)
+            if inside is not None:
+                line = jnp.where(inside, line, 0.0)
             x_from, x_to = {-1: (0, 6), 0: (6, 6 + HX), 1: (6 + HX, EX)}[dx]
             y_from, y_to = {-1: (8, QO), 0: (QO, QO + HY), 1: (QO + HY, QO + HY + 8)}[dy]
             for x in range(x_from, x_to):
@@ -628,23 +637,16 @@
     def slab(ref, part):
         def rows_of(f, k):
             at = (f * GROUPS + k) * GROUPS
-            if part is None:
-                return ref[FINE_CORNER_LINES + at : FINE_CORNER_LINES + at + GROUPS, :]
-            at += FACE_KIN + part * KIN_LINES
-            return ref[at : at + GROUPS, :]
+            return ref[part, at : at + GROUPS, :]
 
         return rows_of
 
     in_x = {-1: row > 0, 0: True, 1: row < nrow - 1}
     in_y = {-1: col > 0, 0: True, 1: col < ncol - 1}
-    for dx, row_ref, ref in ((0, kin_mine, mine), (-1, kin_up, above), (1, kin_down, below)):
-        for part, dy in ((None, 0), (0, -1), (1, 1)):
-            given = row_ref if part is None else ref
-            step = functools.partial(neighbour, slab(given, part), dx, dy)
-            if dx == 0 and dy == 0:
-                step()
-            else:
-                pl.when(in_x[dx] & in_y[dy])(step)
+    for dx, ref in ((0, kin), (-1, kin_above), (1, kin_below)):
+        for part, dy in enumerate((0, -1, 1)):
+            inside = in_x[dx] & in_y[dy] if (dx, dy) != (0, 0) else None
+            neighbour(slab(ref, part), dx, dy, inside)
 
     parts = (q0, q1, q2, q3)
 
@@ -759,7 +761,7 @@
         kernel,
         out_shape=[jax.ShapeDtypeStruct(shape, jnp.float32) for shape in out_shapes],
         in_specs=[given] * len(args),
-        out_specs=[vmem] * len(out_shapes),
+        out_specs=[given] * len(out_shapes),
         scratch_shapes=[
             pltpu.VMEM(shape, jnp.float32) if isinstance(shape, tuple) else shape
             for shape in scratch
@@ -802,23 +804,25 @@
     material = material.reshape(CX * CY, CZ)
 
     fine = (FIELDS, CX * CY, CZ)
-    up, down, even, odd = call(
+    up, down, even, odd, own = call(
         pack_layers,
-        [(LAYER_LINES, CZ)] * 2 + [(BAND_LINES + KIN_LINES, CZ)] * 2,
+        [(LAYER_LINES, CZ)] * 2 + [(BAND_LINES, CZ)] * 2 + [(KIN_LINES, CZ)],
         [fine, pltpu.VMEM(fine[1:], jnp.int32), coarse_inverse.shape,
-         pltpu.SemaphoreType.DMA((FIELDS + 2,))],
+         (2, 6 * CY, CZ), (BAND_LINES, CZ), (BAND_LINES, CZ), (KIN_LINES, CZ),
+         pltpu.SemaphoreType.DMA((FIELDS + 2,)), pltpu.SemaphoreType.DMA((4 * FIELDS + 5,))],
         b, material, coarse_inverse,
         in_hbm=True, limit=59.27,
     )
     odd, even = pairs(odd, True), pairs(even, False)
     above, below = ahead(up), back(down)
+    even, odd, above, below = lax.optimization_barrier((even, odd, above, below))
     up, down, reaction = call(
-        pack_corners,
-        [(FINE_CORNER_LINES + KIN_LINES, CZ)] * 2 + [(2 * FIELDS, CZ)], [],
-        even, odd, reaction.T, coarse_inverse,
+        pack_corners, [(FINE_CORNER_LINES, CZ)] * 2 + [(2 * FIELDS, CZ)], [],
+        even, odd, reaction.T,
     )
-    mine = up
     kabove, kbelow = ahead(up), back(down)
+    kin_odd, kin_even = pairs(own, True), pairs(own, False)
+
     wide = (FIELDS, WX * CY, CZ)
     middle = MID[1] - MID[0]
     padded = (FIELDS, CX, FY, CZ)
@@ -828,22 +832,21 @@
          (2, 3, 2, FIELDS, FY, CZ), (2, 3, FIELDS, FN, CZ), (2, 3, FIELDS, CY, CZ)],
         [padded] * 6 + [padded[1:], (2, FIELDS + 1, CY, CZ)],
         reaction, b, material, even, odd,
-        limit=16, microseconds=3,
+        limit=16, microseconds=100,
     )
     padded = (FIELDS, GX, FY, CZ)
-    first, scaled, code, coarse, up, down, side_even, side_odd = call(
+    first, scaled, code, coarse, up, down, side_even, side_odd, kin = call(
         functools.partial(smooth_outer, nrow, ncol),
         [fine, wide, padded[1:], (3, VX * HY, CZ)]
-        + [(FACE_LINES, CZ)] * 2 + [(SIDE_LINES, CZ)] * 2,
+        + [(FACE_LINES, CZ)] * 2 + [(SIDE_LINES, CZ)] * 2 + [(3, KIN_LINES, CZ)],
         [padded] * 6 + [(2, FIELDS + 1, CY, CZ)],
-        reaction, b, material, above, below, even, odd, kabove, kbelow, *mids,
-        limit=26, microseconds=3.5,
+        reaction, b, material, above, below, even, odd, kabove, kbelow, own, kin_even, kin_odd, *mids,
+        limit=26,
     )
-    kin_row = (mine, kabove, kbelow)
-    mine = up
     odd, even = pairs(side_odd, True), pairs(side_even, False)
     above, below = ahead(up), back(down)
-    up, down = call(pack_knots, [(KNOT_LINES, CZ)] * 2, [], even, odd)
+    kin_above, kin_below = ahead(kin), back(kin)
+    up, down = call(pack_knots, [(KNOT_LINES, CZ)] * 2, [], even, odd, microseconds=100)
     kabove, kbelow = ahead(up), back(down)
 
     qpadded = (2, QX, QY, CZ)
@@ -855,6 +858,7 @@
         limit=14, microseconds=2.5,
     )
 
+    sums, kin_above, kin_below = lax.optimization_barrier((sums, kin_above, kin_below))
     gathered = lax.all_to_all(sums, ("row", "col"), 0, 0)
 
     epadded = (2, EX, QY, CZ)
@@ -863,7 +867,7 @@
         functools.partial(smooth_second, nrow, ncol),
         [fine],
         [(FIELDS, nrow, CZ), (32, CZ)] + [epadded] * 5 + [(2, EX, 32, CZ)] + [padded] * 6,
-        reaction, gathered, *kin_row, mine,
+        reaction, gathered, kin, kin_above, kin_below,
         start, qscaled, qinverse, first, scaled, code, above, below, even, odd,
         limit=32, microseconds=7,
     )

time: 72.1 us -> 69.8 us (0.968)
  starting transfers between devices: 14.4 us -> 16.8 us
  waiting for transfers between devices: 14.2 us -> 12.1 us
  blocking collectives: 24.8 us -> 23.2 us
  Pallas kernels: 18.5 us -> 17.5 us
    ppermute x4 -> x6, waiting for transfers between devices: 9.65 us -> 3.08 us  [pairs(): return lax.ppermute(value, ('row', 'col'), moves)]
    ppermute x4 -> x5, waiting for transfers between devices: 3.46 us -> 8.9 us  [back(): lax.ppermute(value, 'row', [((i + 1) % count, i) for i in range(count)])]
    ppermute x4 -> x5, starting transfers between devices: 2.4 us -> 7.13 us  [ahead(): lax.ppermute(value, 'row', [(i, (i + 1) % count) for i in range(count)])]
    ppermute x4 -> x5, starting transfers between devices: 5.84 us -> 3.06 us  [back(): lax.ppermute(value, 'row', [((i + 1) % count, i) for i in range(count)])]
    all_to_all x1, blocking collectives: 24.8 us -> 23.2 us  [body(): gathered = lax.all_to_all(sums, ('row', 'col'), 0, 0)]
    pallas_call x7, Pallas kernels: 18.5 us -> 17.5 us  [call(): pl.pallas_call(kernel, out_shape=[jax.ShapeDtypeStruct(shape, jnp.float32...]
    ppermute x4 -> x5, waiting for transfers between devices: 1.05 us -> 0.12 us  [ahead(): lax.ppermute(value, 'row', [(i, (i + 1) % count) for i in range(count)])]
    ppermute x4 -> x6, starting transfers between devices: 6.15 us -> 6.64 us  [pairs(): return lax.ppermute(value, ('row', 'col'), moves)]
  transfers between devices with their start and end apart: 12 -> 16, of which waited for: 5 -> 7; matrix products, arithmetic and copies ran while one was open for 0% -> 0% of each run, Pallas kernels for 4% -> 8%
where the time goes in v4:
time: 69.8 us; the launch traced here: 69.7 us
  blocking collectives  23.2 us (33%)
  Pallas kernels  17.5 us (25%)
  starting transfers between devices  16.8 us (24%)
  waiting for transfers between devices  12.1 us (17%)
    all_to_all x1, blocking collectives, body(): gathered = lax.all_to_all(sums, ('row', 'col'), 0, 0)  23.2 us
    pallas_call x7, Pallas kernels, call(): pl.pallas_call(kernel, out_shape=[jax.ShapeDtypeStruct(shape, jnp.float32...  17.5 us
    ppermute x5, waiting for transfers between devices, back(): lax.ppermute(value, 'row', [((i + 1) % count, i) for i in range(count)])  8.9 us
    ppermute x5, starting transfers between devices, ahead(): lax.ppermute(value, 'row', [(i, (i + 1) % count) for i in range(count)])  7.13 us
    ppermute x6, starting transfers between devices, pairs(): return lax.ppermute(value, ('row', 'col'), moves)  6.64 us
    ppermute x6, waiting for transfers between devices, pairs(): return lax.ppermute(value, ('row', 'col'), moves)  3.08 us
    ppermute x5, starting transfers between devices, back(): lax.ppermute(value, 'row', [((i + 1) % count, i) for i in range(count)])  3.06 us
  transfers between devices with their start and end apart: 16, of which 7 were waited for; matrix products, arithmetic and copies ran while one was open for 0% of the time, Pallas kernels for 8%

profile of v4, /device:TPU:1, one launch (start us, length us, event | category | flops | bytes accessed | tf_op | source)
XLA Modules:
  0.0 69.7 jit_solution(15122678014665734442)
XLA Ops:
  0.0 0.0 copy-start.1
  0.0 0.0 copy-start
  0.0 0.0 copy-start.3
  0.0 2.4 %shard_map.46 = (f32[960,128]{1,0:T(8,128)}, f32[960,128]{1,0:T(8,128)}, f32[320,128]{1,0:T(8,128)}, f32[320,128]{1,0:T(8,128)}, f32[256,128]{1,0:T(8,128)}) custom-call(f32[4,512,128]{2,1,0:T(8,128)} %bitcast.8, s32[512,128]{1,0:T(8,128)} %bitcast.11, f32[4,8,1024]{2,1,0:T(8,128)} %inverse.1), custom_call_target="tpu_custom_call" | custom-call | flops 100000 | bytes 350000 | tf_op jit(solution)/shard_map/pallas_call | solution.py:760
  2.4 0.0 copy-start.2
  2.4 2.6 %collective-permute-start.2 = (f32[960,128]{1,0:T(8,128)}, f32[960,128]{1,0:T(8,128)S(1)}, u32[]{:S(2)}, u32[]{:S(2)}) collective-permute-start(f32[960,128]{1,0:T(8,128)} %get-tuple-element.43), channel_id=1, source_target_pairs={{0,16},{16,32},{32,48},{48,64},{64,80},{80,96},{96,112},{112,0},{1... | collective-permute-start | bytes 1474568 | tf_op jit(solution)/shard_map/ppermute | solution.py:778
  5.0 0.0 collective-permute-start.3
  5.0 1.3 %collective-permute-start = (f32[320,128]{1,0:T(8,128)}, f32[320,128]{1,0:T(8,128)S(1)}, u32[]{:S(2)}, u32[]{:S(2)}) collective-permute-start(f32[320,128]{1,0:T(8,128)} %get-tuple-element.41), channel_id=1, source_target_pairs={{0,1},{1,0},{2,3},{3,2},{4,5},{5,4},{6,7},{7,6},{8,9},{9,8},{10,11... | collective-permute-start | bytes 491528 | tf_op jit(solution)/shard_map/ppermute | solution.py:798
  6.3 2.1 %collective-permute-start.1 = (f32[320,128]{1,0:T(8,128)}, f32[320,128]{1,0:T(8,128)S(1)}, u32[]{:S(2)}, u32[]{:S(2)}) collective-permute-start(f32[320,128]{1,0:T(8,128)} %get-tuple-element.42), channel_id=1, source_target_pairs={{0,16},{1,2},{2,1},{3,4},{4,3},{5,6},{6,5},{7,8},{8,7},{9,10},{10,... | collective-permute-start | bytes 491528 | tf_op jit(solution)/shard_map/ppermute | solution.py:798
  8.4 0.0 collective-permute-start.7
  8.4 1.2 %collective-permute-done.first.even = f32[320,128]{1,0:T(8,128)S(1)} collective-permute-done((f32[320,128]{1,0:T(8,128)}, f32[320,128]{1,0:T(8,128)S(1)}, u32[]{:S(2)}, u32[]{:S(2)}) %collective-permute-start) | collective-permute-done | bytes 163872 | tf_op jit(solution)/shard_map/ppermute | solution.py:798
  9.7 1.3 %collective-permute-start.6 = (f32[256,128]{1,0:T(8,128)}, f32[256,128]{1,0:T(8,128)S(1)}, u32[]{:S(2)}, u32[]{:S(2)}) collective-permute-start(f32[256,128]{1,0:T(8,128)} %get-tuple-element.52.own), channel_id=1, source_target_pairs={{0,1},{1,0},{2,3},{3,2},{4,5},{5,4},{6,7},{7,6},{8,9},{9,8},{10,11... | collective-permute-start | bytes 393224 | tf_op jit(solution)/shard_map/ppermute | solution.py:798
  11.0 0.0 collective-permute-done.1.second.odd
  11.0 0.1 collective-permute-done.2.above
  11.1 2.4 %collective-permute-done.3.below = f32[960,128]{1,0:T(8,128)S(1)} collective-permute-done((f32[960,128]{1,0:T(8,128)}, f32[960,128]{1,0:T(8,128)S(1)}, u32[]{:S(2)}, u32[]{:S(2)}) %collective-permute-start.3) | collective-permute-done | bytes 491552 | tf_op jit(solution)/shard_map/ppermute | solution.py:783
  13.5 0.0 copy-done.3
  13.5 0.1 shard_map.47
  13.5 1.1 %collective-permute-start.4 = (f32[160,128]{1,0:T(8,128)S(1)}, f32[160,128]{1,0:T(8,128)S(1)}, u32[]{:S(2)}, u32[]{:S(2)}) collective-permute-start(f32[160,128]{1,0:T(8,128)S(1)} %get-tuple-element.50), channel_id=1, source_target_pairs={{0,16},{16,32},{32,48},{48,64},{64,80},{80,96},{96,112},{112,0},{1... | collective-permute-start | bytes 245768 | tf_op jit(solution)/shard_map/ppermute | solution.py:778
  14.6 0.0 collective-permute-start.5
  14.6 0.0 copy-done.1
  14.6 0.0 copy-done
  14.6 2.8 %shard_map.48 = (f32[4,256,128]{2,1,0:T(8,128)S(1)}, f32[4,256,128]{2,1,0:T(8,128)S(1)}, f32[3,64,128]{2,1,0:T(8,128)S(1)}, f32[2,3,2,4,56,128]{5,4,3,2,1,0:T(8,...) custom-call(f32[8,128]{1,0:T(8,128)S(1)} %get-tuple-element.47.reaction, ...), custom_call_target="tpu_custom_call" | custom-call | flops 100000000 | bytes 350000000 | tf_op jit(solution)/shard_map/pallas_call | solution.py:760
  17.4 0.0 collective-permute-done.7.kin_odd
  17.4 0.0 collective-permute-done.6.kin_even
  17.5 0.0 collective-permute-done.4.kabove
  17.5 1.3 %collective-permute-done.5.kbelow = f32[160,128]{1,0:T(8,128)S(1)} collective-permute-done((f32[160,128]{1,0:T(8,128)S(1)}, f32[160,128]{1,0:T(8,128)S(1)}, u32[]{:S(2)}, u32[]{:S(2)}) %collective-permute-start.5) | collective-permute-done | bytes 81952 | tf_op jit(solution)/shard_map/ppermute | solution.py:783
  18.8 0.0 copy-done.2
  18.8 3.5 %shard_map.49 = (f32[4,512,128]{2,1,0:T(8,128)S(1)}, f32[4,640,128]{2,1,0:T(8,128)S(1)}, f32[28,56,128]{2,1,0:T(8,128)S(1)}, f32[3,160,128]{2,1,0:T(8,128)S(1)},...) custom-call(f32[8,128]{1,0:T(8,128)S(1)} %get-tuple-element.47.react, ...), custom_call_target="tpu_custom_call" | custom-call | flops 100000 | bytes 350000 | tf_op jit(solution)/shard_map/pallas_call | solution.py:760
  22.2 1.5 %collective-permute-start.10 = (f32[488,128]{1,0:T(8,128)S(1)}, f32[488,128]{1,0:T(8,128)S(1)}, u32[]{:S(2)}, u32[]{:S(2)}) collective-permute-start(f32[488,128]{1,0:T(8,128)S(1)} %get-tuple-element.62), channel_id=1, source_target_pairs={{0,1},{1,0},{2,3},{3,2},{4,5},{5,4},{6,7},{7,6},{8,9},{9,8},{10,11... | collective-permute-start | bytes 749576 | tf_op jit(solution)/shard_map/ppermute | solution.py:798
  23.8 1.0 %collective-permute-start.8 = (f32[560,128]{1,0:T(8,128)S(1)}, f32[560,128]{1,0:T(8,128)S(1)}, u32[]{:S(2)}, u32[]{:S(2)}) collective-permute-start(f32[560,128]{1,0:T(8,128)S(1)} %get-tuple-element.60), channel_id=1, source_target_pairs={{0,16},{16,32},{32,48},{48,64},{64,80},{80,96},{96,112},{112,0},{1... | collective-permute-start | bytes 860168 | tf_op jit(solution)/shard_map/ppermute | solution.py:778
  24.8 0.4 collective-permute-start.11
  25.2 0.2 collective-permute-start.15
  25.3 1.6 %collective-permute-start.14 = (f32[3,256,128]{2,1,0:T(8,128)S(1)}, f32[3,256,128]{2,1,0:T(8,128)S(1)}, u32[]{:S(2)}, u32[]{:S(2)}) collective-permute-start(f32[3,256,128]{2,1,0:T(8,128)S(1)} %get-tuple-element.67.kin), channel_id=1, source_target_pairs={{0,16},{16,32},{32,48},{48,64},{64,80},{80,96},{96,112},{112,0},{1... | collective-permute-start | bytes 1179656 | tf_op jit(solution)/shard_map/ppermute | solution.py:778
  26.9 1.8 %collective-permute-done.10.first.even = f32[488,128]{1,0:T(8,128)S(1)} collective-permute-done((f32[488,128]{1,0:T(8,128)S(1)}, f32[488,128]{1,0:T(8,128)S(1)}, u32[]{:S(2)}, u32[]{:S(2)}) %collective-permute-start.10) | collective-permute-done | bytes 249888 | tf_op jit(solution)/shard_map/ppermute | solution.py:798
  28.8 2.0 %collective-permute-start.9 = (f32[560,128]{1,0:T(8,128)S(1)}, f32[560,128]{1,0:T(8,128)S(1)}, u32[]{:S(2)}, u32[]{:S(2)}) collective-permute-start(f32[560,128]{1,0:T(8,128)S(1)} %get-tuple-element.61), channel_id=1, source_target_pairs={{16,0},{32,16},{48,32},{64,48},{80,64},{96,80},{112,96},{0,112},{1... | collective-permute-start | bytes 860168 | tf_op jit(solution)/shard_map/ppermute | solution.py:783
  30.8 0.0 collective-permute-done.11.second.odd
  30.8 0.8 %collective-permute-start.12 = (f32[288,128]{1,0:T(8,128)S(1)}, f32[288,128]{1,0:T(8,128)S(1)}, u32[]{:S(2)}, u32[]{:S(2)}) collective-permute-start(f32[288,128]{1,0:T(8,128)S(1)} %get-tuple-element.64), channel_id=1, source_target_pairs={{0,16},{16,32},{32,48},{48,64},{64,80},{80,96},{96,112},{112,0},{1... | collective-permute-start | bytes 442376 | tf_op jit(solution)/shard_map/ppermute | solution.py:778
  31.7 0.0 collective-permute-done.8.above
  31.7 0.9 %collective-permute-start.13 = (f32[288,128]{1,0:T(8,128)S(1)}, f32[288,128]{1,0:T(8,128)S(1)}, u32[]{:S(2)}, u32[]{:S(2)}) collective-permute-start(f32[288,128]{1,0:T(8,128)S(1)} %get-tuple-element.65), channel_id=1, source_target_pairs={{16,0},{32,16},{48,32},{64,48},{80,64},{96,80},{112,96},{0,112},{1... | collective-permute-start | bytes 442376 | tf_op jit(solution)/shard_map/ppermute | solution.py:783
  32.5 3.7 %collective-permute-done.9.below = f32[560,128]{1,0:T(8,128)S(1)} collective-permute-done((f32[560,128]{1,0:T(8,128)S(1)}, f32[560,128]{1,0:T(8,128)S(1)}, u32[]{:S(2)}, u32[]{:S(2)}) %collective-permute-start.9) | collective-permute-done | bytes 286752 | tf_op jit(solution)/shard_map/ppermute | solution.py:783
  36.2 0.0 collective-permute-done.12.kabove
  36.2 1.6 %collective-permute-done.13.kbelow = f32[288,128]{1,0:T(8,128)S(1)} collective-permute-done((f32[288,128]{1,0:T(8,128)S(1)}, f32[288,128]{1,0:T(8,128)S(1)}, u32[]{:S(2)}, u32[]{:S(2)}) %collective-permute-start.13) | collective-permute-done | bytes 147488 | tf_op jit(solution)/shard_map/ppermute | solution.py:783
  37.8 2.4 %shard_map.51 = (f32[2,12,32,128]{3,2,1,0:T(8,128)S(1)}, f32[2,18,32,128]{3,2,1,0:T(8,128)S(1)}, f32[2,18,32,128]{3,2,1,0:T(8,128)S(1)}, f32[128,128]{1,0:T(8,128)S(1)}) custom-call(f32[8,128]{1,0:T(8,128)S(1)} %get-tuple-element.47.reaction, f32[3,160,128]{2,1,0:T(8,128)S(1)} %get-tuple-element.59.coarse, f32[560,128]{1,0:T(8,128)S(1)} %collective-permute-done.8.above, ...), custom_call_target="tpu_custom_call" | custom-call | flops 2500000 | bytes 8750000 | tf_op jit(solution)/shard_map/pallas_call | solution.py:760
  40.2 0.0 collective-permute-done.15.kin_below
  40.2 0.0 collective-permute-done.14.kin_above
  40.3 23.2 %all_to_all.11 = f32[128,1,128]{2,1,0:T(1,128)S(1)} all-to-all(f32[128,1,128]{2,1,0:T(1,128)S(1)} %bitcast.15), channel_id=1, replica_groups=mesh['row'=8,'col'=16] {'row','col'}, dimensions={0} | all-to-all | bytes 131072 | tf_op jit(solution)/shard_map/all_to_all | solution.py:862
  63.4 6.3 %shard_map.52 = f32[4,512,128]{2,1,0:T(8,128)} custom-call(f32[8,128]{1,0:T(8,128)S(1)} %get-tuple-element.47.reaction, f32[128,128]{1,0:T(8,128)S(1)} %bitcast.14, f32[3,256,128]{2,1,0:T(8,128)S(1)} %get-tuple-element.67.kin, f32[3,256,128]{2,1,0:T(8,128)S(1)} %collective-permute-done.14.kin_above, f32[3,256,128]{2,1,0:T(8,128)S(1)} %collective-permute-done.15.kin_below, ...), custom_call_target="tpu_custom_call" | custom-call | flops 7000000 | bytes 24500000 | tf_op jit(solution)/shard_map/pallas_call | solution.py:760
  (1 shorter events, 0.0 us)
Async XLA Ops:
  0.0 14.6 %copy-start.1 = (s32[16,32,128]{2,1,0:T(8,128)S(1)}, s32[16,32,128]{2,1,0:T(8,128)}, u32[]{:S(2)}) copy-start(s32[16,32,128]{2,1,0:T(8,128)} %param.5) | copy-start | bytes 786436
  0.0 14.6 %copy-start = (f32[4,16,32,128]{3,2,1,0:T(8,128)S(1)}, f32[4,16,32,128]{3,2,1,0:T(8,128)}, u32[]{:S(2)}) copy-start(f32[4,16,32,128]{3,2,1,0:T(8,128)} %param.4) | copy-start | bytes 3145732
  0.0 13.5 %copy-start.3 = (f32[4,2]{0,1:T(2,128)S(1)}, f32[4,2]{0,1:T(2,128)}, u32[]{:S(2)}) copy-start(f32[4,2]{0,1:T(2,128)} %param.6) | copy-start | bytes 100
  2.4 16.4 %copy-start.2 = (f32[256,128]{1,0:T(8,128)S(1)}, f32[256,128]{1,0:T(8,128)}, u32[]{:S(2)}) copy-start(f32[256,128]{1,0:T(8,128)} %get-tuple-element.52.own) | copy-start | bytes 393220
  2.4 8.7 %collective-permute-start.2 = (f32[960,128]{1,0:T(8,128)}, f32[960,128]{1,0:T(8,128)S(1)}, u32[]{:S(2)}, u32[]{:S(2)}) collective-permute-start(f32[960,128]{1,0:T(8,128)} %get-tuple-element.43), channel_id=1, source_target_pairs={{0,16},{16,32},{32,48},{48,64},{64,80},{80,96},{96,112},{112,0},{1... | collective-permute-start | bytes 1474568 | tf_op jit(solution)/shard_map/ppermute | solution.py:778
  5.0 8.5 %collective-permute-start.3 = (f32[960,128]{1,0:T(8,128)}, f32[960,128]{1,0:T(8,128)S(1)}, u32[]{:S(2)}, u32[]{:S(2)}) collective-permute-start(f32[960,128]{1,0:T(8,128)} %get-tuple-element.44), channel_id=1, source_target_pairs={{16,0},{32,16},{48,32},{64,48},{80,64},{96,80},{112,96},{0,112},{1... | collective-permute-start | bytes 1474568 | tf_op jit(solution)/shard_map/ppermute | solution.py:783
  5.0 4.7 %collective-permute-start = (f32[320,128]{1,0:T(8,128)}, f32[320,128]{1,0:T(8,128)S(1)}, u32[]{:S(2)}, u32[]{:S(2)}) collective-permute-start(f32[320,128]{1,0:T(8,128)} %get-tuple-element.41), channel_id=1, source_target_pairs={{0,1},{1,0},{2,3},{3,2},{4,5},{5,4},{6,7},{7,6},{8,9},{9,8},{10,11... | collective-permute-start | bytes 491528 | tf_op jit(solution)/shard_map/ppermute | solution.py:798
  6.3 4.7 %collective-permute-start.1 = (f32[320,128]{1,0:T(8,128)}, f32[320,128]{1,0:T(8,128)S(1)}, u32[]{:S(2)}, u32[]{:S(2)}) collective-permute-start(f32[320,128]{1,0:T(8,128)} %get-tuple-element.42), channel_id=1, source_target_pairs={{0,16},{1,2},{2,1},{3,4},{4,3},{5,6},{6,5},{7,8},{8,7},{9,10},{10,... | collective-permute-start | bytes 491528 | tf_op jit(solution)/shard_map/ppermute | solution.py:798
  8.4 9.0 %collective-permute-start.7 = (f32[256,128]{1,0:T(8,128)}, f32[256,128]{1,0:T(8,128)S(1)}, u32[]{:S(2)}, u32[]{:S(2)}) collective-permute-start(f32[256,128]{1,0:T(8,128)} %get-tuple-element.52.own), channel_id=1, source_target_pairs={{0,16},{1,2},{2,1},{3,4},{4,3},{5,6},{6,5},{7,8},{8,7},{9,10},{10,... | collective-permute-start | bytes 393224 | tf_op jit(solution)/shard_map/ppermute | solution.py:798
  9.7 7.8 %collective-permute-start.6 = (f32[256,128]{1,0:T(8,128)}, f32[256,128]{1,0:T(8,128)S(1)}, u32[]{:S(2)}, u32[]{:S(2)}) collective-permute-start(f32[256,128]{1,0:T(8,128)} %get-tuple-element.52.own), channel_id=1, source_target_pairs={{0,1},{1,0},{2,3},{3,2},{4,5},{5,4},{6,7},{7,6},{8,9},{9,8},{10,11... | collective-permute-start | bytes 393224 | tf_op jit(solution)/shard_map/ppermute | solution.py:798
  13.5 3.9 %collective-permute-start.4 = (f32[160,128]{1,0:T(8,128)S(1)}, f32[160,128]{1,0:T(8,128)S(1)}, u32[]{:S(2)}, u32[]{:S(2)}) collective-permute-start(f32[160,128]{1,0:T(8,128)S(1)} %get-tuple-element.50), channel_id=1, source_target_pairs={{0,16},{16,32},{32,48},{48,64},{64,80},{80,96},{96,112},{112,0},{1... | collective-permute-start | bytes 245768 | tf_op jit(solution)/shard_map/ppermute | solution.py:778
  14.6 4.1 %collective-permute-start.5 = (f32[160,128]{1,0:T(8,128)S(1)}, f32[160,128]{1,0:T(8,128)S(1)}, u32[]{:S(2)}, u32[]{:S(2)}) collective-permute-start(f32[160,128]{1,0:T(8,128)S(1)} %get-tuple-element.51), channel_id=1, source_target_pairs={{16,0},{32,16},{48,32},{64,48},{80,64},{96,80},{112,96},{0,112},{1... | collective-permute-start | bytes 245768 | tf_op jit(solution)/shard_map/ppermute | solution.py:783
  22.2 6.5 %collective-permute-start.10 = (f32[488,128]{1,0:T(8,128)S(1)}, f32[488,128]{1,0:T(8,128)S(1)}, u32[]{:S(2)}, u32[]{:S(2)}) collective-permute-start(f32[488,128]{1,0:T(8,128)S(1)} %get-tuple-element.62), channel_id=1, source_target_pairs={{0,1},{1,0},{2,3},{3,2},{4,5},{5,4},{6,7},{7,6},{8,9},{9,8},{10,11... | collective-permute-start | bytes 749576 | tf_op jit(solution)/shard_map/ppermute | solution.py:798
  23.8 7.9 %collective-permute-start.8 = (f32[560,128]{1,0:T(8,128)S(1)}, f32[560,128]{1,0:T(8,128)S(1)}, u32[]{:S(2)}, u32[]{:S(2)}) collective-permute-start(f32[560,128]{1,0:T(8,128)S(1)} %get-tuple-element.60), channel_id=1, source_target_pairs={{0,16},{16,32},{32,48},{48,64},{64,80},{80,96},{96,112},{112,0},{1... | collective-permute-start | bytes 860168 | tf_op jit(solution)/shard_map/ppermute | solution.py:778
  24.8 6.0 %collective-permute-start.11 = (f32[488,128]{1,0:T(8,128)S(1)}, f32[488,128]{1,0:T(8,128)S(1)}, u32[]{:S(2)}, u32[]{:S(2)}) collective-permute-start(f32[488,128]{1,0:T(8,128)S(1)} %get-tuple-element.63), channel_id=1, source_target_pairs={{0,16},{1,2},{2,1},{3,4},{4,3},{5,6},{6,5},{7,8},{8,7},{9,10},{10,... | collective-permute-start | bytes 749576 | tf_op jit(solution)/shard_map/ppermute | solution.py:798
  25.2 15.0 %collective-permute-start.15 = (f32[3,256,128]{2,1,0:T(8,128)S(1)}, f32[3,256,128]{2,1,0:T(8,128)S(1)}, u32[]{:S(2)}, u32[]{:S(2)}) collective-permute-start(f32[3,256,128]{2,1,0:T(8,128)S(1)} %get-tuple-element.67.kin), channel_id=1, source_target_pairs={{16,0},{32,16},{48,32},{64,48},{80,64},{96,80},{112,96},{0,112},{1... | collective-permute-start | bytes 1179656 | tf_op jit(solution)/shard_map/ppermute | solution.py:783
  25.3 14.9 %collective-permute-start.14 = (f32[3,256,128]{2,1,0:T(8,128)S(1)}, f32[3,256,128]{2,1,0:T(8,128)S(1)}, u32[]{:S(2)}, u32[]{:S(2)}) collective-permute-start(f32[3,256,128]{2,1,0:T(8,128)S(1)} %get-tuple-element.67.kin), channel_id=1, source_target_pairs={{0,16},{16,32},{32,48},{48,64},{64,80},{80,96},{96,112},{112,0},{1... | collective-permute-start | bytes 1179656 | tf_op jit(solution)/shard_map/ppermute | solution.py:778
  28.8 7.4 %collective-permute-start.9 = (f32[560,128]{1,0:T(8,128)S(1)}, f32[560,128]{1,0:T(8,128)S(1)}, u32[]{:S(2)}, u32[]{:S(2)}) collective-permute-start(f32[560,128]{1,0:T(8,128)S(1)} %get-tuple-element.61), channel_id=1, source_target_pairs={{16,0},{32,16},{48,32},{64,48},{80,64},{96,80},{112,96},{0,112},{1... | collective-permute-start | bytes 860168 | tf_op jit(solution)/shard_map/ppermute | solution.py:783
  30.8 5.4 %collective-permute-start.12 = (f32[288,128]{1,0:T(8,128)S(1)}, f32[288,128]{1,0:T(8,128)S(1)}, u32[]{:S(2)}, u32[]{:S(2)}) collective-permute-start(f32[288,128]{1,0:T(8,128)S(1)} %get-tuple-element.64), channel_id=1, source_target_pairs={{0,16},{16,32},{32,48},{48,64},{64,80},{80,96},{96,112},{112,0},{1... | collective-permute-start | bytes 442376 | tf_op jit(solution)/shard_map/ppermute | solution.py:778
  31.7 6.1 %collective-permute-start.13 = (f32[288,128]{1,0:T(8,128)S(1)}, f32[288,128]{1,0:T(8,128)S(1)}, u32[]{:S(2)}, u32[]{:S(2)}) collective-permute-start(f32[288,128]{1,0:T(8,128)S(1)} %get-tuple-element.65), channel_id=1, source_target_pairs={{16,0},{32,16},{48,32},{64,48},{80,64},{96,80},{112,96},{0,112},{1... | collective-permute-start | bytes 442376 | tf_op jit(solution)/shard_map/ppermute | solution.py:783

commit v5 on v4

--- a/solution.py
+++ b/solution.py
@@ -61,10 +61,11 @@
     return lax.broadcasted_iota(jnp.int32, (1, CZ), 1)
 
 
-def beside(ref, f, x, low, count, width):
+def beside(ref, f, x, low, count, width, share=1):
+    after, before, x = (x + 1) // share, (x - 1) // share, x // share
     here = ref[f, x, low : low + count, :]
     lane = lanes()
-    total = ref[f, x + 1, low : low + count, :] + ref[f, x - 1, low : low + count, :]
+    total = ref[f, after, low : low + count, :] + ref[f, before, low : low + count, :]
     total = total + ref[f, x, low + 1 : low + 1 + count, :]
     total = total + ref[f, x, low - 1 : low - 1 + count, :]
     total = total + jnp.where(lane < CZ - width, pltpu.roll(here, CZ - width, 1), 0.0)
@@ -595,7 +596,7 @@
     nrow, ncol, reaction, gathered, kin, kin_above, kin_below,
     start, qscaled, qinverse, first, scaled, code, above, below, even, odd,
     out,
-    wide, spread, e, q0, q1, q2, q3, qs, fs, inv, f0, p0, p1, p2,
+    wide, spread, e, q0, q1, q2, q3, qs, fs, inv, f0, p0, p1, p2, out_here, sems,
 ):
     row, col = place()
     lane = lanes()
@@ -680,15 +681,15 @@
                     value = jnp.where(parity, pltpu.roll(total, CZ - 1, 1), total)
                 else:
                     value = jnp.where(parity, total, pltpu.roll(total, 1, 1))
-                spread[...] = value
-                high, low = spread[8:26, :], spread[6:8, :]
-                for h in range(2):
-                    to = f0.at[2 * plane + odd, i * 2 + h]
-                    for y in range(2):
-                        to[pl.ds(FO + y, 18, stride=2), :] = high
-                        to[pl.ds(FO + FN - 4 + y, 2, stride=2), :] = low
-                    to[FO - 1 : FO, :] = low[1:2]
-                    to[FO + FN : FO + FN + 1, :] = high[0:1]
+                some = spread.at[i % 2, 2 * plane + odd]
+                some[...] = value
+                high, low = some[8:26, :], some[6:8, :]
+                to = f0.at[2 * plane + odd, i]
+                for y in range(2):
+                    to[pl.ds(FO + y, 18, stride=2), :] = high
+                    to[pl.ds(FO + FN - 4 + y, 2, stride=2), :] = low
+                to[FO - 1 : FO, :] = low[1:2]
+                to[FO + FN : FO + FN + 1, :] = high[0:1]
 
     every(0, HX + 4, lift)
 
@@ -728,7 +729,7 @@
     def open_fine(x):
         kind = code[x + 2, ALL, :]
         for f in range(FIELDS):
-            here, total = beside(f0, f, x, FO, FN, 1)
+            here, total = beside(f0, f, x, FO, FN, 1, 2)
             inverse = inverse_of(kind, reaction, f)
             inv[f, x, ALL, :] = inverse
             value = fs[f, x, ALL, :] - here + inverse * total
@@ -741,27 +742,37 @@
 
     keep, gain = coefficients()[2]
 
-    def close(i):
-        x = i + 4
-        at = pl.ds(i * CY, CY)
-        for f in range(FIELDS):
+    sent = []
+    part = CX // 2
+    for f in range(FIELDS):
+        for i in range(CX):
+            x = i + 4
+            at = slice(i * CY, i * CY + CY)
             here, total = beside(p2, f, x, FO, CY, 1)
             value = fs[f, x, OWN, :] - here + inv[f, x, OWN, :] * total
-            result = first[f, at, :] + f0[f, x, OWN, :] + p0[f, x, OWN, :]
+            result = first[f, at, :] + f0[f, x // 2, OWN, :] + p0[f, x, OWN, :]
             result = result + p1[f, x, OWN, :] + here
-            out[f, at, :] = result + (keep * here + gain * value)
-
-    every(0, CX, close)
-
-
-def call(kernel, out_shapes, scratch, *args, limit=16, in_hbm=False, microseconds=0.1):
+            out_here[f, at, :] = result + (keep * here + gain * value)
+            if i % part == part - 1:
+                lines = pl.ds((i + 1 - part) * CY, part * CY)
+                copy = pltpu.make_async_copy(
+                    out_here.at[f, lines], out.at[f, lines], sems.at[len(sent)]
+                )
+                copy.start()
+                sent.append(copy)
+    for copy in sent:
+        copy.wait()
+
+
+def call(kernel, out_shapes, scratch, *args, limit=16, in_hbm=False, out_hbm=False, microseconds=0.1):
     vmem = pl.BlockSpec(memory_space=pltpu.VMEM)
-    given = pl.BlockSpec(memory_space=pltpu.HBM) if in_hbm else vmem
+    hbm = pl.BlockSpec(memory_space=pltpu.HBM)
+    given, taken = hbm if in_hbm else vmem, hbm if out_hbm else vmem
     return pl.pallas_call(
         kernel,
         out_shape=[jax.ShapeDtypeStruct(shape, jnp.float32) for shape in out_shapes],
         in_specs=[given] * len(args),
-        out_specs=[given] * len(out_shapes),
+        out_specs=[taken] * len(out_shapes),
         scratch_shapes=[
             pltpu.VMEM(shape, jnp.float32) if isinstance(shape, tuple) else shape
             for shape in scratch
@@ -811,7 +822,7 @@
          (2, 6 * CY, CZ), (BAND_LINES, CZ), (BAND_LINES, CZ), (KIN_LINES, CZ),
          pltpu.SemaphoreType.DMA((FIELDS + 2,)), pltpu.SemaphoreType.DMA((4 * FIELDS + 5,))],
         b, material, coarse_inverse,
-        in_hbm=True, limit=59.27,
+        in_hbm=True, out_hbm=True, limit=59.27,
     )
     odd, even = pairs(odd, True), pairs(even, False)
     above, below = ahead(up), back(down)
@@ -866,10 +877,11 @@
     (out,) = call(
         functools.partial(smooth_second, nrow, ncol),
         [fine],
-        [(FIELDS, nrow, CZ), (32, CZ)] + [epadded] * 5 + [(2, EX, 32, CZ)] + [padded] * 6,
+        [(FIELDS, nrow, CZ), (2, FIELDS, 32, CZ)] + [epadded] * 5 + [(2, EX, 32, CZ)] + [padded] * 2
+        + [(FIELDS, FX // 2, FY, CZ)] + [padded] * 3 + [fine, pltpu.SemaphoreType.DMA((2 * FIELDS,))],
         reaction, gathered, kin, kin_above, kin_below,
         start, qscaled, qinverse, first, scaled, code, above, below, even, odd,
-        limit=32, microseconds=7,
+        limit=30, microseconds=7, out_hbm=True,
     )
     return out.reshape(right_side.shape)
 

time: 69.8 us -> 69.6 us (level)
  no operation moved by 1% of the time
where the time goes in v5:
time: 69.6 us; the launch traced here: 69.5 us
  blocking collectives  23.2 us (33%)
  Pallas kernels  17.1 us (25%)
  starting transfers between devices  16.8 us (24%)
  waiting for transfers between devices  12.1 us (17%)
    all_to_all x1, blocking collectives, body(): gathered = lax.all_to_all(sums, ('row', 'col'), 0, 0)  23.2 us
    pallas_call x7, Pallas kernels, call(): pl.pallas_call(kernel, out_shape=[jax.ShapeDtypeStruct(shape, jnp.float32...  17.1 us
    ppermute x5, waiting for transfers between devices, back(): lax.ppermute(value, 'row', [((i + 1) % count, i) for i in range(count)])  8.9 us
    ppermute x5, starting transfers between devices, ahead(): lax.ppermute(value, 'row', [(i, (i + 1) % count) for i in range(count)])  7.08 us
    ppermute x6, starting transfers between devices, pairs(): return lax.ppermute(value, ('row', 'col'), moves)  6.64 us
    ppermute x6, waiting for transfers between devices, pairs(): return lax.ppermute(value, ('row', 'col'), moves)  3.11 us
    ppermute x5, starting transfers between devices, back(): lax.ppermute(value, 'row', [((i + 1) % count, i) for i in range(count)])  3.06 us
  transfers between devices with their start and end apart: 16, of which 7 were waited for; matrix products, arithmetic and copies ran while one was open for 0% of the time, Pallas kernels for 8%

profile of v5, /device:TPU:1, one launch (start us, length us, event | category | flops | bytes accessed | tf_op | source)
XLA Modules:
  0.0 69.5 jit_solution(13545610703657933565)
XLA Ops:
  0.0 0.0 copy-start.1
  0.0 0.0 copy-start
  0.0 0.0 copy-start.3
  0.0 2.4 %shard_map.46 = (f32[960,128]{1,0:T(8,128)}, f32[960,128]{1,0:T(8,128)}, f32[320,128]{1,0:T(8,128)}, f32[320,128]{1,0:T(8,128)}, f32[256,128]{1,0:T(8,128)}) custom-call(f32[4,512,128]{2,1,0:T(8,128)} %bitcast.8, s32[512,128]{1,0:T(8,128)} %bitcast.11, f32[4,8,1024]{2,1,0:T(8,128)} %inverse.1), custom_call_target="tpu_custom_call" | custom-call | flops 100000 | bytes 350000 | tf_op jit(solution)/shard_map/pallas_call | solution.py:771
  2.4 0.0 copy-start.2
  2.4 2.6 %collective-permute-start.2 = (f32[960,128]{1,0:T(8,128)}, f32[960,128]{1,0:T(8,128)S(1)}, u32[]{:S(2)}, u32[]{:S(2)}) collective-permute-start(f32[960,128]{1,0:T(8,128)} %get-tuple-element.43), channel_id=1, source_target_pairs={{0,16},{16,32},{32,48},{48,64},{64,80},{80,96},{96,112},{112,0},{1... | collective-permute-start | bytes 1474568 | tf_op jit(solution)/shard_map/ppermute | solution.py:789
  5.0 0.0 collective-permute-start.3
  5.0 1.3 %collective-permute-start = (f32[320,128]{1,0:T(8,128)}, f32[320,128]{1,0:T(8,128)S(1)}, u32[]{:S(2)}, u32[]{:S(2)}) collective-permute-start(f32[320,128]{1,0:T(8,128)} %get-tuple-element.41), channel_id=1, source_target_pairs={{0,1},{1,0},{2,3},{3,2},{4,5},{5,4},{6,7},{7,6},{8,9},{9,8},{10,11... | collective-permute-start | bytes 491528 | tf_op jit(solution)/shard_map/ppermute | solution.py:809
  6.3 2.1 %collective-permute-start.1 = (f32[320,128]{1,0:T(8,128)}, f32[320,128]{1,0:T(8,128)S(1)}, u32[]{:S(2)}, u32[]{:S(2)}) collective-permute-start(f32[320,128]{1,0:T(8,128)} %get-tuple-element.42), channel_id=1, source_target_pairs={{0,16},{1,2},{2,1},{3,4},{4,3},{5,6},{6,5},{7,8},{8,7},{9,10},{10,... | collective-permute-start | bytes 491528 | tf_op jit(solution)/shard_map/ppermute | solution.py:809
  8.4 0.0 collective-permute-start.7
  8.4 1.2 %collective-permute-done.first.even = f32[320,128]{1,0:T(8,128)S(1)} collective-permute-done((f32[320,128]{1,0:T(8,128)}, f32[320,128]{1,0:T(8,128)S(1)}, u32[]{:S(2)}, u32[]{:S(2)}) %collective-permute-start) | collective-permute-done | bytes 163872 | tf_op jit(solution)/shard_map/ppermute | solution.py:809
  9.7 1.3 %collective-permute-start.6 = (f32[256,128]{1,0:T(8,128)}, f32[256,128]{1,0:T(8,128)S(1)}, u32[]{:S(2)}, u32[]{:S(2)}) collective-permute-start(f32[256,128]{1,0:T(8,128)} %get-tuple-element.52.own), channel_id=1, source_target_pairs={{0,1},{1,0},{2,3},{3,2},{4,5},{5,4},{6,7},{7,6},{8,9},{9,8},{10,11... | collective-permute-start | bytes 393224 | tf_op jit(solution)/shard_map/ppermute | solution.py:809
  11.0 0.0 collective-permute-done.1.second.odd
  11.0 0.1 collective-permute-done.2.above
  11.1 2.4 %collective-permute-done.3.below = f32[960,128]{1,0:T(8,128)S(1)} collective-permute-done((f32[960,128]{1,0:T(8,128)}, f32[960,128]{1,0:T(8,128)S(1)}, u32[]{:S(2)}, u32[]{:S(2)}) %collective-permute-start.3) | collective-permute-done | bytes 491552 | tf_op jit(solution)/shard_map/ppermute | solution.py:794
  13.5 0.0 copy-done.3
  13.5 0.1 shard_map.47
  13.5 1.1 %collective-permute-start.4 = (f32[160,128]{1,0:T(8,128)S(1)}, f32[160,128]{1,0:T(8,128)S(1)}, u32[]{:S(2)}, u32[]{:S(2)}) collective-permute-start(f32[160,128]{1,0:T(8,128)S(1)} %get-tuple-element.50), channel_id=1, source_target_pairs={{0,16},{16,32},{32,48},{48,64},{64,80},{80,96},{96,112},{112,0},{1... | collective-permute-start | bytes 245768 | tf_op jit(solution)/shard_map/ppermute | solution.py:789
  14.6 0.0 collective-permute-start.5
  14.6 0.0 copy-done.1
  14.6 0.0 copy-done
  14.6 2.8 %shard_map.48 = (f32[4,256,128]{2,1,0:T(8,128)S(1)}, f32[4,256,128]{2,1,0:T(8,128)S(1)}, f32[3,64,128]{2,1,0:T(8,128)S(1)}, f32[2,3,2,4,56,128]{5,4,3,2,1,0:T(8,...) custom-call(f32[8,128]{1,0:T(8,128)S(1)} %get-tuple-element.47.reaction, ...), custom_call_target="tpu_custom_call" | custom-call | flops 100000000 | bytes 350000000 | tf_op jit(solution)/shard_map/pallas_call | solution.py:771
  17.4 0.0 collective-permute-done.7.kin_odd
  17.4 0.0 collective-permute-done.6.kin_even
  17.4 0.0 collective-permute-done.4.kabove
  17.4 1.3 %collective-permute-done.5.kbelow = f32[160,128]{1,0:T(8,128)S(1)} collective-permute-done((f32[160,128]{1,0:T(8,128)S(1)}, f32[160,128]{1,0:T(8,128)S(1)}, u32[]{:S(2)}, u32[]{:S(2)}) %collective-permute-start.5) | collective-permute-done | bytes 81952 | tf_op jit(solution)/shard_map/ppermute | solution.py:794
  18.8 0.0 copy-done.2
  18.8 3.4 %shard_map.49 = (f32[4,512,128]{2,1,0:T(8,128)S(1)}, f32[4,640,128]{2,1,0:T(8,128)S(1)}, f32[28,56,128]{2,1,0:T(8,128)S(1)}, f32[3,160,128]{2,1,0:T(8,128)S(1)},...) custom-call(f32[8,128]{1,0:T(8,128)S(1)} %get-tuple-element.47.react, ...), custom_call_target="tpu_custom_call" | custom-call | flops 100000 | bytes 350000 | tf_op jit(solution)/shard_map/pallas_call | solution.py:771
  22.2 1.5 %collective-permute-start.10 = (f32[488,128]{1,0:T(8,128)S(1)}, f32[488,128]{1,0:T(8,128)S(1)}, u32[]{:S(2)}, u32[]{:S(2)}) collective-permute-start(f32[488,128]{1,0:T(8,128)S(1)} %get-tuple-element.62), channel_id=1, source_target_pairs={{0,1},{1,0},{2,3},{3,2},{4,5},{5,4},{6,7},{7,6},{8,9},{9,8},{10,11... | collective-permute-start | bytes 749576 | tf_op jit(solution)/shard_map/ppermute | solution.py:809
  23.8 1.0 %collective-permute-start.8 = (f32[560,128]{1,0:T(8,128)S(1)}, f32[560,128]{1,0:T(8,128)S(1)}, u32[]{:S(2)}, u32[]{:S(2)}) collective-permute-start(f32[560,128]{1,0:T(8,128)S(1)} %get-tuple-element.60), channel_id=1, source_target_pairs={{0,16},{16,32},{32,48},{48,64},{64,80},{80,96},{96,112},{112,0},{1... | collective-permute-start | bytes 860168 | tf_op jit(solution)/shard_map/ppermute | solution.py:789
  24.8 0.4 collective-permute-start.11
  25.1 0.2 collective-permute-start.15
  25.3 1.6 %collective-permute-start.14 = (f32[3,256,128]{2,1,0:T(8,128)S(1)}, f32[3,256,128]{2,1,0:T(8,128)S(1)}, u32[]{:S(2)}, u32[]{:S(2)}) collective-permute-start(f32[3,256,128]{2,1,0:T(8,128)S(1)} %get-tuple-element.67.kin), channel_id=1, source_target_pairs={{0,16},{16,32},{32,48},{48,64},{64,80},{80,96},{96,112},{112,0},{1... | collective-permute-start | bytes 1179656 | tf_op jit(solution)/shard_map/ppermute | solution.py:789
  26.9 1.9 %collective-permute-done.10.first.even = f32[488,128]{1,0:T(8,128)S(1)} collective-permute-done((f32[488,128]{1,0:T(8,128)S(1)}, f32[488,128]{1,0:T(8,128)S(1)}, u32[]{:S(2)}, u32[]{:S(2)}) %collective-permute-start.10) | collective-permute-done | bytes 249888 | tf_op jit(solution)/shard_map/ppermute | solution.py:809
  28.8 2.0 %collective-permute-start.9 = (f32[560,128]{1,0:T(8,128)S(1)}, f32[560,128]{1,0:T(8,128)S(1)}, u32[]{:S(2)}, u32[]{:S(2)}) collective-permute-start(f32[560,128]{1,0:T(8,128)S(1)} %get-tuple-element.61), channel_id=1, source_target_pairs={{16,0},{32,16},{48,32},{64,48},{80,64},{96,80},{112,96},{0,112},{1... | collective-permute-start | bytes 860168 | tf_op jit(solution)/shard_map/ppermute | solution.py:794
  30.8 0.0 collective-permute-done.11.second.odd
  30.8 0.8 %collective-permute-start.12 = (f32[288,128]{1,0:T(8,128)S(1)}, f32[288,128]{1,0:T(8,128)S(1)}, u32[]{:S(2)}, u32[]{:S(2)}) collective-permute-start(f32[288,128]{1,0:T(8,128)S(1)} %get-tuple-element.64), channel_id=1, source_target_pairs={{0,16},{16,32},{32,48},{48,64},{64,80},{80,96},{96,112},{112,0},{1... | collective-permute-start | bytes 442376 | tf_op jit(solution)/shard_map/ppermute | solution.py:789
  31.6 0.0 collective-permute-done.8.above
  31.6 0.9 %collective-permute-start.13 = (f32[288,128]{1,0:T(8,128)S(1)}, f32[288,128]{1,0:T(8,128)S(1)}, u32[]{:S(2)}, u32[]{:S(2)}) collective-permute-start(f32[288,128]{1,0:T(8,128)S(1)} %get-tuple-element.65), channel_id=1, source_target_pairs={{16,0},{32,16},{48,32},{64,48},{80,64},{96,80},{112,96},{0,112},{1... | collective-permute-start | bytes 442376 | tf_op jit(solution)/shard_map/ppermute | solution.py:794
  32.5 3.6 %collective-permute-done.9.below = f32[560,128]{1,0:T(8,128)S(1)} collective-permute-done((f32[560,128]{1,0:T(8,128)S(1)}, f32[560,128]{1,0:T(8,128)S(1)}, u32[]{:S(2)}, u32[]{:S(2)}) %collective-permute-start.9) | collective-permute-done | bytes 286752 | tf_op jit(solution)/shard_map/ppermute | solution.py:794
  36.1 0.0 collective-permute-done.12.kabove
  36.1 1.6 %collective-permute-done.13.kbelow = f32[288,128]{1,0:T(8,128)S(1)} collective-permute-done((f32[288,128]{1,0:T(8,128)S(1)}, f32[288,128]{1,0:T(8,128)S(1)}, u32[]{:S(2)}, u32[]{:S(2)}) %collective-permute-start.13) | collective-permute-done | bytes 147488 | tf_op jit(solution)/shard_map/ppermute | solution.py:794
  37.7 2.4 %shard_map.51 = (f32[2,12,32,128]{3,2,1,0:T(8,128)S(1)}, f32[2,18,32,128]{3,2,1,0:T(8,128)S(1)}, f32[2,18,32,128]{3,2,1,0:T(8,128)S(1)}, f32[128,128]{1,0:T(8,128)S(1)}) custom-call(f32[8,128]{1,0:T(8,128)S(1)} %get-tuple-element.47.reaction, f32[3,160,128]{2,1,0:T(8,128)S(1)} %get-tuple-element.59.coarse, f32[560,128]{1,0:T(8,128)S(1)} %collective-permute-done.8.above, ...), custom_call_target="tpu_custom_call" | custom-call | flops 2500000 | bytes 8750000 | tf_op jit(solution)/shard_map/pallas_call | solution.py:771
  40.2 0.0 collective-permute-done.15.kin_below
  40.2 0.0 collective-permute-done.14.kin_above
  40.2 23.2 %all_to_all.11 = f32[128,1,128]{2,1,0:T(1,128)S(1)} all-to-all(f32[128,1,128]{2,1,0:T(1,128)S(1)} %bitcast.15), channel_id=1, replica_groups=mesh['row'=8,'col'=16] {'row','col'}, dimensions={0} | all-to-all | bytes 131072 | tf_op jit(solution)/shard_map/all_to_all | solution.py:873
  63.4 5.9 %shard_map.52 = f32[4,512,128]{2,1,0:T(8,128)} custom-call(f32[8,128]{1,0:T(8,128)S(1)} %get-tuple-element.47.reaction, f32[128,128]{1,0:T(8,128)S(1)} %bitcast.14, f32[3,256,128]{2,1,0:T(8,128)S(1)} %get-tuple-element.67.kin, f32[3,256,128]{2,1,0:T(8,128)S(1)} %collective-permute-done.14.kin_above, f32[3,256,128]{2,1,0:T(8,128)S(1)} %collective-permute-done.15.kin_below, ...), custom_call_target="tpu_custom_call" | custom-call | flops 7000000 | bytes 24500000 | tf_op jit(solution)/shard_map/pallas_call | solution.py:771
  (1 shorter events, 0.0 us)
Async XLA Ops:
  0.0 14.6 %copy-start.1 = (s32[16,32,128]{2,1,0:T(8,128)S(1)}, s32[16,32,128]{2,1,0:T(8,128)}, u32[]{:S(2)}) copy-start(s32[16,32,128]{2,1,0:T(8,128)} %param.5) | copy-start | bytes 786436
  0.0 14.6 %copy-start = (f32[4,16,32,128]{3,2,1,0:T(8,128)S(1)}, f32[4,16,32,128]{3,2,1,0:T(8,128)}, u32[]{:S(2)}) copy-start(f32[4,16,32,128]{3,2,1,0:T(8,128)} %param.4) | copy-start | bytes 3145732
  0.0 13.5 %copy-start.3 = (f32[4,2]{0,1:T(2,128)S(1)}, f32[4,2]{0,1:T(2,128)}, u32[]{:S(2)}) copy-start(f32[4,2]{0,1:T(2,128)} %param.6) | copy-start | bytes 100
  2.4 16.4 %copy-start.2 = (f32[256,128]{1,0:T(8,128)S(1)}, f32[256,128]{1,0:T(8,128)}, u32[]{:S(2)}) copy-start(f32[256,128]{1,0:T(8,128)} %get-tuple-element.52.own) | copy-start | bytes 393220
  2.4 8.7 %collective-permute-start.2 = (f32[960,128]{1,0:T(8,128)}, f32[960,128]{1,0:T(8,128)S(1)}, u32[]{:S(2)}, u32[]{:S(2)}) collective-permute-start(f32[960,128]{1,0:T(8,128)} %get-tuple-element.43), channel_id=1, source_target_pairs={{0,16},{16,32},{32,48},{48,64},{64,80},{80,96},{96,112},{112,0},{1... | collective-permute-start | bytes 1474568 | tf_op jit(solution)/shard_map/ppermute | solution.py:789
  5.0 8.5 %collective-permute-start.3 = (f32[960,128]{1,0:T(8,128)}, f32[960,128]{1,0:T(8,128)S(1)}, u32[]{:S(2)}, u32[]{:S(2)}) collective-permute-start(f32[960,128]{1,0:T(8,128)} %get-tuple-element.44), channel_id=1, source_target_pairs={{16,0},{32,16},{48,32},{64,48},{80,64},{96,80},{112,96},{0,112},{1... | collective-permute-start | bytes 1474568 | tf_op jit(solution)/shard_map/ppermute | solution.py:794
  5.0 4.7 %collective-permute-start = (f32[320,128]{1,0:T(8,128)}, f32[320,128]{1,0:T(8,128)S(1)}, u32[]{:S(2)}, u32[]{:S(2)}) collective-permute-start(f32[320,128]{1,0:T(8,128)} %get-tuple-element.41), channel_id=1, source_target_pairs={{0,1},{1,0},{2,3},{3,2},{4,5},{5,4},{6,7},{7,6},{8,9},{9,8},{10,11... | collective-permute-start | bytes 491528 | tf_op jit(solution)/shard_map/ppermute | solution.py:809
  6.3 4.7 %collective-permute-start.1 = (f32[320,128]{1,0:T(8,128)}, f32[320,128]{1,0:T(8,128)S(1)}, u32[]{:S(2)}, u32[]{:S(2)}) collective-permute-start(f32[320,128]{1,0:T(8,128)} %get-tuple-element.42), channel_id=1, source_target_pairs={{0,16},{1,2},{2,1},{3,4},{4,3},{5,6},{6,5},{7,8},{8,7},{9,10},{10,... | collective-permute-start | bytes 491528 | tf_op jit(solution)/shard_map/ppermute | solution.py:809
  8.4 9.0 %collective-permute-start.7 = (f32[256,128]{1,0:T(8,128)}, f32[256,128]{1,0:T(8,128)S(1)}, u32[]{:S(2)}, u32[]{:S(2)}) collective-permute-start(f32[256,128]{1,0:T(8,128)} %get-tuple-element.52.own), channel_id=1, source_target_pairs={{0,16},{1,2},{2,1},{3,4},{4,3},{5,6},{6,5},{7,8},{8,7},{9,10},{10,... | collective-permute-start | bytes 393224 | tf_op jit(solution)/shard_map/ppermute | solution.py:809
  9.7 7.7 %collective-permute-start.6 = (f32[256,128]{1,0:T(8,128)}, f32[256,128]{1,0:T(8,128)S(1)}, u32[]{:S(2)}, u32[]{:S(2)}) collective-permute-start(f32[256,128]{1,0:T(8,128)} %get-tuple-element.52.own), channel_id=1, source_target_pairs={{0,1},{1,0},{2,3},{3,2},{4,5},{5,4},{6,7},{7,6},{8,9},{9,8},{10,11... | collective-permute-start | bytes 393224 | tf_op jit(solution)/shard_map/ppermute | solution.py:809
  13.5 3.9 %collective-permute-start.4 = (f32[160,128]{1,0:T(8,128)S(1)}, f32[160,128]{1,0:T(8,128)S(1)}, u32[]{:S(2)}, u32[]{:S(2)}) collective-permute-start(f32[160,128]{1,0:T(8,128)S(1)} %get-tuple-element.50), channel_id=1, source_target_pairs={{0,16},{16,32},{32,48},{48,64},{64,80},{80,96},{96,112},{112,0},{1... | collective-permute-start | bytes 245768 | tf_op jit(solution)/shard_map/ppermute | solution.py:789
  14.6 4.1 %collective-permute-start.5 = (f32[160,128]{1,0:T(8,128)S(1)}, f32[160,128]{1,0:T(8,128)S(1)}, u32[]{:S(2)}, u32[]{:S(2)}) collective-permute-start(f32[160,128]{1,0:T(8,128)S(1)} %get-tuple-element.51), channel_id=1, source_target_pairs={{16,0},{32,16},{48,32},{64,48},{80,64},{96,80},{112,96},{0,112},{1... | collective-permute-start | bytes 245768 | tf_op jit(solution)/shard_map/ppermute | solution.py:794
  22.2 6.5 %collective-permute-start.10 = (f32[488,128]{1,0:T(8,128)S(1)}, f32[488,128]{1,0:T(8,128)S(1)}, u32[]{:S(2)}, u32[]{:S(2)}) collective-permute-start(f32[488,128]{1,0:T(8,128)S(1)} %get-tuple-element.62), channel_id=1, source_target_pairs={{0,1},{1,0},{2,3},{3,2},{4,5},{5,4},{6,7},{7,6},{8,9},{9,8},{10,11... | collective-permute-start | bytes 749576 | tf_op jit(solution)/shard_map/ppermute | solution.py:809
  23.8 7.8 %collective-permute-start.8 = (f32[560,128]{1,0:T(8,128)S(1)}, f32[560,128]{1,0:T(8,128)S(1)}, u32[]{:S(2)}, u32[]{:S(2)}) collective-permute-start(f32[560,128]{1,0:T(8,128)S(1)} %get-tuple-element.60), channel_id=1, source_target_pairs={{0,16},{16,32},{32,48},{48,64},{64,80},{80,96},{96,112},{112,0},{1... | collective-permute-start | bytes 860168 | tf_op jit(solution)/shard_map/ppermute | solution.py:789
  24.8 6.0 %collective-permute-start.11 = (f32[488,128]{1,0:T(8,128)S(1)}, f32[488,128]{1,0:T(8,128)S(1)}, u32[]{:S(2)}, u32[]{:S(2)}) collective-permute-start(f32[488,128]{1,0:T(8,128)S(1)} %get-tuple-element.63), channel_id=1, source_target_pairs={{0,16},{1,2},{2,1},{3,4},{4,3},{5,6},{6,5},{7,8},{8,7},{9,10},{10,... | collective-permute-start | bytes 749576 | tf_op jit(solution)/shard_map/ppermute | solution.py:809
  25.1 15.0 %collective-permute-start.15 = (f32[3,256,128]{2,1,0:T(8,128)S(1)}, f32[3,256,128]{2,1,0:T(8,128)S(1)}, u32[]{:S(2)}, u32[]{:S(2)}) collective-permute-start(f32[3,256,128]{2,1,0:T(8,128)S(1)} %get-tuple-element.67.kin), channel_id=1, source_target_pairs={{16,0},{32,16},{48,32},{64,48},{80,64},{96,80},{112,96},{0,112},{1... | collective-permute-start | bytes 1179656 | tf_op jit(solution)/shard_map/ppermute | solution.py:794
  25.3 14.9 %collective-permute-start.14 = (f32[3,256,128]{2,1,0:T(8,128)S(1)}, f32[3,256,128]{2,1,0:T(8,128)S(1)}, u32[]{:S(2)}, u32[]{:S(2)}) collective-permute-start(f32[3,256,128]{2,1,0:T(8,128)S(1)} %get-tuple-element.67.kin), channel_id=1, source_target_pairs={{0,16},{16,32},{32,48},{48,64},{64,80},{80,96},{96,112},{112,0},{1... | collective-permute-start | bytes 1179656 | tf_op jit(solution)/shard_map/ppermute | solution.py:789
  28.8 7.4 %collective-permute-start.9 = (f32[560,128]{1,0:T(8,128)S(1)}, f32[560,128]{1,0:T(8,128)S(1)}, u32[]{:S(2)}, u32[]{:S(2)}) collective-permute-start(f32[560,128]{1,0:T(8,128)S(1)} %get-tuple-element.61), channel_id=1, source_target_pairs={{16,0},{32,16},{48,32},{64,48},{80,64},{96,80},{112,96},{0,112},{1... | collective-permute-start | bytes 860168 | tf_op jit(solution)/shard_map/ppermute | solution.py:794
  30.8 5.3 %collective-permute-start.12 = (f32[288,128]{1,0:T(8,128)S(1)}, f32[288,128]{1,0:T(8,128)S(1)}, u32[]{:S(2)}, u32[]{:S(2)}) collective-permute-start(f32[288,128]{1,0:T(8,128)S(1)} %get-tuple-element.64), channel_id=1, source_target_pairs={{0,16},{16,32},{32,48},{48,64},{64,80},{80,96},{96,112},{112,0},{1... | collective-permute-start | bytes 442376 | tf_op jit(solution)/shard_map/ppermute | solution.py:789
  31.6 6.1 %collective-permute-start.13 = (f32[288,128]{1,0:T(8,128)S(1)}, f32[288,128]{1,0:T(8,128)S(1)}, u32[]{:S(2)}, u32[]{:S(2)}) collective-permute-start(f32[288,128]{1,0:T(8,128)S(1)} %get-tuple-element.65), channel_id=1, source_target_pairs={{16,0},{32,16},{48,32},{64,48},{80,64},{96,80},{112,96},{0,112},{1... | collective-permute-start | bytes 442376 | tf_op jit(solution)/shard_map/ppermute | solution.py:794

commit v6 on v5

--- a/solution.py
+++ b/solution.py
@@ -260,7 +260,7 @@
             for i in range(4):
                 at = (f * 4 + i) * CX
                 row = halo_row(i + 1 if is_high else 4 - i, is_high)
-                for x, size in spans:
+                for x, size in spans if f < FIELDS else ((0, CX),):
                     put(f, x + x_at, row, size, ref[at + x : at + x + size, :])
 
     def sides(low, high):
@@ -340,7 +340,7 @@
 
     pl.when(row > 0)(functools.partial(rows, 0, above))
     pl.when(row < nrow - 1)(functools.partial(rows, GX - 6, below))
-    lay_bands(at_x, ((0, CX),), ncol, put, even, odd)
+    lay_bands(at_x, ((0, 4), (CX - 4, 4)), ncol, put, even, odd)
 
     def corners(ref, is_above, is_high):
         for f in range(FIELDS + 1):

time: 69.6 us -> 69.6 us (level)
  no operation moved by 1% of the time
where the time goes in v6:
time: 69.6 us; the launch traced here: 69.5 us
  blocking collectives  23.2 us (33%)
  Pallas kernels  17.1 us (25%)
  starting transfers between devices  16.8 us (24%)
  waiting for transfers between devices  12.1 us (17%)
    all_to_all x1, blocking collectives, body(): gathered = lax.all_to_all(sums, ('row', 'col'), 0, 0)  23.2 us
    pallas_call x7, Pallas kernels, call(): pl.pallas_call(kernel, out_shape=[jax.ShapeDtypeStruct(shape, jnp.float32...  17.1 us
    ppermute x5, waiting for transfers between devices, back(): lax.ppermute(value, 'row', [((i + 1) % count, i) for i in range(count)])  8.91 us
    ppermute x5, starting transfers between devices, ahead(): lax.ppermute(value, 'row', [(i, (i + 1) % count) for i in range(count)])  7.08 us
    ppermute x6, starting transfers between devices, pairs(): return lax.ppermute(value, ('row', 'col'), moves)  6.64 us
    ppermute x6, waiting for transfers between devices, pairs(): return lax.ppermute(value, ('row', 'col'), moves)  3.11 us
    ppermute x5, starting transfers between devices, back(): lax.ppermute(value, 'row', [((i + 1) % count, i) for i in range(count)])  3.05 us
  transfers between devices with their start and end apart: 16, of which 7 were waited for; matrix products, arithmetic and copies ran while one was open for 0% of the time, Pallas kernels for 8%

profile of v6, /device:TPU:1, one launch (start us, length us, event | category | flops | bytes accessed | tf_op | source)
XLA Modules:
  0.0 69.5 jit_solution(15570161448561964786)
XLA Ops:
  0.0 0.0 copy-start.1
  0.0 0.0 copy-start
  0.0 0.0 copy-start.3
  0.0 2.4 %shard_map.46 = (f32[960,128]{1,0:T(8,128)}, f32[960,128]{1,0:T(8,128)}, f32[320,128]{1,0:T(8,128)}, f32[320,128]{1,0:T(8,128)}, f32[256,128]{1,0:T(8,128)}) custom-call(f32[4,512,128]{2,1,0:T(8,128)} %bitcast.8, s32[512,128]{1,0:T(8,128)} %bitcast.11, f32[4,8,1024]{2,1,0:T(8,128)} %inverse.1), custom_call_target="tpu_custom_call" | custom-call | flops 100000 | bytes 350000 | tf_op jit(solution)/shard_map/pallas_call | solution.py:771
  2.4 0.0 copy-start.2
  2.4 2.6 %collective-permute-start.2 = (f32[960,128]{1,0:T(8,128)}, f32[960,128]{1,0:T(8,128)S(1)}, u32[]{:S(2)}, u32[]{:S(2)}) collective-permute-start(f32[960,128]{1,0:T(8,128)} %get-tuple-element.43), channel_id=1, source_target_pairs={{0,16},{16,32},{32,48},{48,64},{64,80},{80,96},{96,112},{112,0},{1... | collective-permute-start | bytes 1474568 | tf_op jit(solution)/shard_map/ppermute | solution.py:789
  5.0 0.0 collective-permute-start.3
  5.0 1.3 %collective-permute-start = (f32[320,128]{1,0:T(8,128)}, f32[320,128]{1,0:T(8,128)S(1)}, u32[]{:S(2)}, u32[]{:S(2)}) collective-permute-start(f32[320,128]{1,0:T(8,128)} %get-tuple-element.41), channel_id=1, source_target_pairs={{0,1},{1,0},{2,3},{3,2},{4,5},{5,4},{6,7},{7,6},{8,9},{9,8},{10,11... | collective-permute-start | bytes 491528 | tf_op jit(solution)/shard_map/ppermute | solution.py:809
  6.3 2.1 %collective-permute-start.1 = (f32[320,128]{1,0:T(8,128)}, f32[320,128]{1,0:T(8,128)S(1)}, u32[]{:S(2)}, u32[]{:S(2)}) collective-permute-start(f32[320,128]{1,0:T(8,128)} %get-tuple-element.42), channel_id=1, source_target_pairs={{0,16},{1,2},{2,1},{3,4},{4,3},{5,6},{6,5},{7,8},{8,7},{9,10},{10,... | collective-permute-start | bytes 491528 | tf_op jit(solution)/shard_map/ppermute | solution.py:809
  8.4 0.0 collective-permute-start.7
  8.4 1.2 %collective-permute-done.first.even = f32[320,128]{1,0:T(8,128)S(1)} collective-permute-done((f32[320,128]{1,0:T(8,128)}, f32[320,128]{1,0:T(8,128)S(1)}, u32[]{:S(2)}, u32[]{:S(2)}) %collective-permute-start) | collective-permute-done | bytes 163872 | tf_op jit(solution)/shard_map/ppermute | solution.py:809
  9.7 1.3 %collective-permute-start.6 = (f32[256,128]{1,0:T(8,128)}, f32[256,128]{1,0:T(8,128)S(1)}, u32[]{:S(2)}, u32[]{:S(2)}) collective-permute-start(f32[256,128]{1,0:T(8,128)} %get-tuple-element.52.own), channel_id=1, source_target_pairs={{0,1},{1,0},{2,3},{3,2},{4,5},{5,4},{6,7},{7,6},{8,9},{9,8},{10,11... | collective-permute-start | bytes 393224 | tf_op jit(solution)/shard_map/ppermute | solution.py:809
  11.0 0.0 collective-permute-done.1.second.odd
  11.0 0.1 collective-permute-done.2.above
  11.1 2.4 %collective-permute-done.3.below = f32[960,128]{1,0:T(8,128)S(1)} collective-permute-done((f32[960,128]{1,0:T(8,128)}, f32[960,128]{1,0:T(8,128)S(1)}, u32[]{:S(2)}, u32[]{:S(2)}) %collective-permute-start.3) | collective-permute-done | bytes 491552 | tf_op jit(solution)/shard_map/ppermute | solution.py:794
  13.5 0.0 copy-done.3
  13.5 0.1 shard_map.47
  13.5 1.1 %collective-permute-start.4 = (f32[160,128]{1,0:T(8,128)S(1)}, f32[160,128]{1,0:T(8,128)S(1)}, u32[]{:S(2)}, u32[]{:S(2)}) collective-permute-start(f32[160,128]{1,0:T(8,128)S(1)} %get-tuple-element.50), channel_id=1, source_target_pairs={{0,16},{16,32},{32,48},{48,64},{64,80},{80,96},{96,112},{112,0},{1... | collective-permute-start | bytes 245768 | tf_op jit(solution)/shard_map/ppermute | solution.py:789
  14.6 0.0 collective-permute-start.5
  14.6 0.0 copy-done.1
  14.6 0.0 copy-done
  14.6 2.8 %shard_map.48 = (f32[4,256,128]{2,1,0:T(8,128)S(1)}, f32[4,256,128]{2,1,0:T(8,128)S(1)}, f32[3,64,128]{2,1,0:T(8,128)S(1)}, f32[2,3,2,4,56,128]{5,4,3,2,1,0:T(8,...) custom-call(f32[8,128]{1,0:T(8,128)S(1)} %get-tuple-element.47.reaction, ...), custom_call_target="tpu_custom_call" | custom-call | flops 100000000 | bytes 350000000 | tf_op jit(solution)/shard_map/pallas_call | solution.py:771
  17.4 0.0 collective-permute-done.7.kin_odd
  17.4 0.0 collective-permute-done.6.kin_even
  17.4 0.0 collective-permute-done.4.kabove
  17.4 1.3 %collective-permute-done.5.kbelow = f32[160,128]{1,0:T(8,128)S(1)} collective-permute-done((f32[160,128]{1,0:T(8,128)S(1)}, f32[160,128]{1,0:T(8,128)S(1)}, u32[]{:S(2)}, u32[]{:S(2)}) %collective-permute-start.5) | collective-permute-done | bytes 81952 | tf_op jit(solution)/shard_map/ppermute | solution.py:794
  18.8 0.0 copy-done.2
  18.8 3.4 %shard_map.49 = (f32[4,512,128]{2,1,0:T(8,128)S(1)}, f32[4,640,128]{2,1,0:T(8,128)S(1)}, f32[28,56,128]{2,1,0:T(8,128)S(1)}, f32[3,160,128]{2,1,0:T(8,128)S(1)},...) custom-call(f32[8,128]{1,0:T(8,128)S(1)} %get-tuple-element.47.react, ...), custom_call_target="tpu_custom_call" | custom-call | flops 100000 | bytes 350000 | tf_op jit(solution)/shard_map/pallas_call | solution.py:771
  22.2 1.6 %collective-permute-start.10 = (f32[488,128]{1,0:T(8,128)S(1)}, f32[488,128]{1,0:T(8,128)S(1)}, u32[]{:S(2)}, u32[]{:S(2)}) collective-permute-start(f32[488,128]{1,0:T(8,128)S(1)} %get-tuple-element.62), channel_id=1, source_target_pairs={{0,1},{1,0},{2,3},{3,2},{4,5},{5,4},{6,7},{7,6},{8,9},{9,8},{10,11... | collective-permute-start | bytes 749576 | tf_op jit(solution)/shard_map/ppermute | solution.py:809
  23.8 1.0 %collective-permute-start.8 = (f32[560,128]{1,0:T(8,128)S(1)}, f32[560,128]{1,0:T(8,128)S(1)}, u32[]{:S(2)}, u32[]{:S(2)}) collective-permute-start(f32[560,128]{1,0:T(8,128)S(1)} %get-tuple-element.60), channel_id=1, source_target_pairs={{0,16},{16,32},{32,48},{48,64},{64,80},{80,96},{96,112},{112,0},{1... | collective-permute-start | bytes 860168 | tf_op jit(solution)/shard_map/ppermute | solution.py:789
  24.8 0.4 collective-permute-start.11
  25.1 0.2 collective-permute-start.15
  25.3 1.6 %collective-permute-start.14 = (f32[3,256,128]{2,1,0:T(8,128)S(1)}, f32[3,256,128]{2,1,0:T(8,128)S(1)}, u32[]{:S(2)}, u32[]{:S(2)}) collective-permute-start(f32[3,256,128]{2,1,0:T(8,128)S(1)} %get-tuple-element.67.kin), channel_id=1, source_target_pairs={{0,16},{16,32},{32,48},{48,64},{64,80},{80,96},{96,112},{112,0},{1... | collective-permute-start | bytes 1179656 | tf_op jit(solution)/shard_map/ppermute | solution.py:789
  26.9 1.9 %collective-permute-done.10.first.even = f32[488,128]{1,0:T(8,128)S(1)} collective-permute-done((f32[488,128]{1,0:T(8,128)S(1)}, f32[488,128]{1,0:T(8,128)S(1)}, u32[]{:S(2)}, u32[]{:S(2)}) %collective-permute-start.10) | collective-permute-done | bytes 249888 | tf_op jit(solution)/shard_map/ppermute | solution.py:809
  28.8 2.0 %collective-permute-start.9 = (f32[560,128]{1,0:T(8,128)S(1)}, f32[560,128]{1,0:T(8,128)S(1)}, u32[]{:S(2)}, u32[]{:S(2)}) collective-permute-start(f32[560,128]{1,0:T(8,128)S(1)} %get-tuple-element.61), channel_id=1, source_target_pairs={{16,0},{32,16},{48,32},{64,48},{80,64},{96,80},{112,96},{0,112},{1... | collective-permute-start | bytes 860168 | tf_op jit(solution)/shard_map/ppermute | solution.py:794
  30.8 0.0 collective-permute-done.11.second.odd
  30.8 0.8 %collective-permute-start.12 = (f32[288,128]{1,0:T(8,128)S(1)}, f32[288,128]{1,0:T(8,128)S(1)}, u32[]{:S(2)}, u32[]{:S(2)}) collective-permute-start(f32[288,128]{1,0:T(8,128)S(1)} %get-tuple-element.64), channel_id=1, source_target_pairs={{0,16},{16,32},{32,48},{48,64},{64,80},{80,96},{96,112},{112,0},{1... | collective-permute-start | bytes 442376 | tf_op jit(solution)/shard_map/ppermute | solution.py:789
  31.6 0.0 collective-permute-done.8.above
  31.6 0.9 %collective-permute-start.13 = (f32[288,128]{1,0:T(8,128)S(1)}, f32[288,128]{1,0:T(8,128)S(1)}, u32[]{:S(2)}, u32[]{:S(2)}) collective-permute-start(f32[288,128]{1,0:T(8,128)S(1)} %get-tuple-element.65), channel_id=1, source_target_pairs={{16,0},{32,16},{48,32},{64,48},{80,64},{96,80},{112,96},{0,112},{1... | collective-permute-start | bytes 442376 | tf_op jit(solution)/shard_map/ppermute | solution.py:794
  32.5 3.6 %collective-permute-done.9.below = f32[560,128]{1,0:T(8,128)S(1)} collective-permute-done((f32[560,128]{1,0:T(8,128)S(1)}, f32[560,128]{1,0:T(8,128)S(1)}, u32[]{:S(2)}, u32[]{:S(2)}) %collective-permute-start.9) | collective-permute-done | bytes 286752 | tf_op jit(solution)/shard_map/ppermute | solution.py:794
  36.1 0.0 collective-permute-done.12.kabove
  36.1 1.6 %collective-permute-done.13.kbelow = f32[288,128]{1,0:T(8,128)S(1)} collective-permute-done((f32[288,128]{1,0:T(8,128)S(1)}, f32[288,128]{1,0:T(8,128)S(1)}, u32[]{:S(2)}, u32[]{:S(2)}) %collective-permute-start.13) | collective-permute-done | bytes 147488 | tf_op jit(solution)/shard_map/ppermute | solution.py:794
  37.7 2.4 %shard_map.51 = (f32[2,12,32,128]{3,2,1,0:T(8,128)S(1)}, f32[2,18,32,128]{3,2,1,0:T(8,128)S(1)}, f32[2,18,32,128]{3,2,1,0:T(8,128)S(1)}, f32[128,128]{1,0:T(8,128)S(1)}) custom-call(f32[8,128]{1,0:T(8,128)S(1)} %get-tuple-element.47.reaction, f32[3,160,128]{2,1,0:T(8,128)S(1)} %get-tuple-element.59.coarse, f32[560,128]{1,0:T(8,128)S(1)} %collective-permute-done.8.above, ...), custom_call_target="tpu_custom_call" | custom-call | flops 2500000 | bytes 8750000 | tf_op jit(solution)/shard_map/pallas_call | solution.py:771
  40.2 0.0 collective-permute-done.15.kin_below
  40.2 0.0 collective-permute-done.14.kin_above
  40.2 23.2 %all_to_all.11 = f32[128,1,128]{2,1,0:T(1,128)S(1)} all-to-all(f32[128,1,128]{2,1,0:T(1,128)S(1)} %bitcast.15), channel_id=1, replica_groups=mesh['row'=8,'col'=16] {'row','col'}, dimensions={0} | all-to-all | bytes 131072 | tf_op jit(solution)/shard_map/all_to_all | solution.py:873
  63.4 5.9 %shard_map.52 = f32[4,512,128]{2,1,0:T(8,128)} custom-call(f32[8,128]{1,0:T(8,128)S(1)} %get-tuple-element.47.reaction, f32[128,128]{1,0:T(8,128)S(1)} %bitcast.14, f32[3,256,128]{2,1,0:T(8,128)S(1)} %get-tuple-element.67.kin, f32[3,256,128]{2,1,0:T(8,128)S(1)} %collective-permute-done.14.kin_above, f32[3,256,128]{2,1,0:T(8,128)S(1)} %collective-permute-done.15.kin_below, ...), custom_call_target="tpu_custom_call" | custom-call | flops 7000000 | bytes 24500000 | tf_op jit(solution)/shard_map/pallas_call | solution.py:771
  (1 shorter events, 0.0 us)
Async XLA Ops:
  0.0 14.6 %copy-start.1 = (s32[16,32,128]{2,1,0:T(8,128)S(1)}, s32[16,32,128]{2,1,0:T(8,128)}, u32[]{:S(2)}) copy-start(s32[16,32,128]{2,1,0:T(8,128)} %param.5) | copy-start | bytes 786436
  0.0 14.6 %copy-start = (f32[4,16,32,128]{3,2,1,0:T(8,128)S(1)}, f32[4,16,32,128]{3,2,1,0:T(8,128)}, u32[]{:S(2)}) copy-start(f32[4,16,32,128]{3,2,1,0:T(8,128)} %param.4) | copy-start | bytes 3145732
  0.0 13.5 %copy-start.3 = (f32[4,2]{0,1:T(2,128)S(1)}, f32[4,2]{0,1:T(2,128)}, u32[]{:S(2)}) copy-start(f32[4,2]{0,1:T(2,128)} %param.6) | copy-start | bytes 100
  2.4 16.4 %copy-start.2 = (f32[256,128]{1,0:T(8,128)S(1)}, f32[256,128]{1,0:T(8,128)}, u32[]{:S(2)}) copy-start(f32[256,128]{1,0:T(8,128)} %get-tuple-element.52.own) | copy-start | bytes 393220
  2.4 8.7 %collective-permute-start.2 = (f32[960,128]{1,0:T(8,128)}, f32[960,128]{1,0:T(8,128)S(1)}, u32[]{:S(2)}, u32[]{:S(2)}) collective-permute-start(f32[960,128]{1,0:T(8,128)} %get-tuple-element.43), channel_id=1, source_target_pairs={{0,16},{16,32},{32,48},{48,64},{64,80},{80,96},{96,112},{112,0},{1... | collective-permute-start | bytes 1474568 | tf_op jit(solution)/shard_map/ppermute | solution.py:789
  5.0 8.5 %collective-permute-start.3 = (f32[960,128]{1,0:T(8,128)}, f32[960,128]{1,0:T(8,128)S(1)}, u32[]{:S(2)}, u32[]{:S(2)}) collective-permute-start(f32[960,128]{1,0:T(8,128)} %get-tuple-element.44), channel_id=1, source_target_pairs={{16,0},{32,16},{48,32},{64,48},{80,64},{96,80},{112,96},{0,112},{1... | collective-permute-start | bytes 1474568 | tf_op jit(solution)/shard_map/ppermute | solution.py:794
  5.0 4.7 %collective-permute-start = (f32[320,128]{1,0:T(8,128)}, f32[320,128]{1,0:T(8,128)S(1)}, u32[]{:S(2)}, u32[]{:S(2)}) collective-permute-start(f32[320,128]{1,0:T(8,128)} %get-tuple-element.41), channel_id=1, source_target_pairs={{0,1},{1,0},{2,3},{3,2},{4,5},{5,4},{6,7},{7,6},{8,9},{9,8},{10,11... | collective-permute-start | bytes 491528 | tf_op jit(solution)/shard_map/ppermute | solution.py:809
  6.3 4.7 %collective-permute-start.1 = (f32[320,128]{1,0:T(8,128)}, f32[320,128]{1,0:T(8,128)S(1)}, u32[]{:S(2)}, u32[]{:S(2)}) collective-permute-start(f32[320,128]{1,0:T(8,128)} %get-tuple-element.42), channel_id=1, source_target_pairs={{0,16},{1,2},{2,1},{3,4},{4,3},{5,6},{6,5},{7,8},{8,7},{9,10},{10,... | collective-permute-start | bytes 491528 | tf_op jit(solution)/shard_map/ppermute | solution.py:809
  8.4 9.0 %collective-permute-start.7 = (f32[256,128]{1,0:T(8,128)}, f32[256,128]{1,0:T(8,128)S(1)}, u32[]{:S(2)}, u32[]{:S(2)}) collective-permute-start(f32[256,128]{1,0:T(8,128)} %get-tuple-element.52.own), channel_id=1, source_target_pairs={{0,16},{1,2},{2,1},{3,4},{4,3},{5,6},{6,5},{7,8},{8,7},{9,10},{10,... | collective-permute-start | bytes 393224 | tf_op jit(solution)/shard_map/ppermute | solution.py:809
  9.7 7.7 %collective-permute-start.6 = (f32[256,128]{1,0:T(8,128)}, f32[256,128]{1,0:T(8,128)S(1)}, u32[]{:S(2)}, u32[]{:S(2)}) collective-permute-start(f32[256,128]{1,0:T(8,128)} %get-tuple-element.52.own), channel_id=1, source_target_pairs={{0,1},{1,0},{2,3},{3,2},{4,5},{5,4},{6,7},{7,6},{8,9},{9,8},{10,11... | collective-permute-start | bytes 393224 | tf_op jit(solution)/shard_map/ppermute | solution.py:809
  13.5 3.9 %collective-permute-start.4 = (f32[160,128]{1,0:T(8,128)S(1)}, f32[160,128]{1,0:T(8,128)S(1)}, u32[]{:S(2)}, u32[]{:S(2)}) collective-permute-start(f32[160,128]{1,0:T(8,128)S(1)} %get-tuple-element.50), channel_id=1, source_target_pairs={{0,16},{16,32},{32,48},{48,64},{64,80},{80,96},{96,112},{112,0},{1... | collective-permute-start | bytes 245768 | tf_op jit(solution)/shard_map/ppermute | solution.py:789
  14.6 4.1 %collective-permute-start.5 = (f32[160,128]{1,0:T(8,128)S(1)}, f32[160,128]{1,0:T(8,128)S(1)}, u32[]{:S(2)}, u32[]{:S(2)}) collective-permute-start(f32[160,128]{1,0:T(8,128)S(1)} %get-tuple-element.51), channel_id=1, source_target_pairs={{16,0},{32,16},{48,32},{64,48},{80,64},{96,80},{112,96},{0,112},{1... | collective-permute-start | bytes 245768 | tf_op jit(solution)/shard_map/ppermute | solution.py:794
  22.2 6.5 %collective-permute-start.10 = (f32[488,128]{1,0:T(8,128)S(1)}, f32[488,128]{1,0:T(8,128)S(1)}, u32[]{:S(2)}, u32[]{:S(2)}) collective-permute-start(f32[488,128]{1,0:T(8,128)S(1)} %get-tuple-element.62), channel_id=1, source_target_pairs={{0,1},{1,0},{2,3},{3,2},{4,5},{5,4},{6,7},{7,6},{8,9},{9,8},{10,11... | collective-permute-start | bytes 749576 | tf_op jit(solution)/shard_map/ppermute | solution.py:809
  23.8 7.8 %collective-permute-start.8 = (f32[560,128]{1,0:T(8,128)S(1)}, f32[560,128]{1,0:T(8,128)S(1)}, u32[]{:S(2)}, u32[]{:S(2)}) collective-permute-start(f32[560,128]{1,0:T(8,128)S(1)} %get-tuple-element.60), channel_id=1, source_target_pairs={{0,16},{16,32},{32,48},{48,64},{64,80},{80,96},{96,112},{112,0},{1... | collective-permute-start | bytes 860168 | tf_op jit(solution)/shard_map/ppermute | solution.py:789
  24.8 6.0 %collective-permute-start.11 = (f32[488,128]{1,0:T(8,128)S(1)}, f32[488,128]{1,0:T(8,128)S(1)}, u32[]{:S(2)}, u32[]{:S(2)}) collective-permute-start(f32[488,128]{1,0:T(8,128)S(1)} %get-tuple-element.63), channel_id=1, source_target_pairs={{0,16},{1,2},{2,1},{3,4},{4,3},{5,6},{6,5},{7,8},{8,7},{9,10},{10,... | collective-permute-start | bytes 749576 | tf_op jit(solution)/shard_map/ppermute | solution.py:809
  25.1 15.0 %collective-permute-start.15 = (f32[3,256,128]{2,1,0:T(8,128)S(1)}, f32[3,256,128]{2,1,0:T(8,128)S(1)}, u32[]{:S(2)}, u32[]{:S(2)}) collective-permute-start(f32[3,256,128]{2,1,0:T(8,128)S(1)} %get-tuple-element.67.kin), channel_id=1, source_target_pairs={{16,0},{32,16},{48,32},{64,48},{80,64},{96,80},{112,96},{0,112},{1... | collective-permute-start | bytes 1179656 | tf_op jit(solution)/shard_map/ppermute | solution.py:794
  25.3 14.9 %collective-permute-start.14 = (f32[3,256,128]{2,1,0:T(8,128)S(1)}, f32[3,256,128]{2,1,0:T(8,128)S(1)}, u32[]{:S(2)}, u32[]{:S(2)}) collective-permute-start(f32[3,256,128]{2,1,0:T(8,128)S(1)} %get-tuple-element.67.kin), channel_id=1, source_target_pairs={{0,16},{16,32},{32,48},{48,64},{64,80},{80,96},{96,112},{112,0},{1... | collective-permute-start | bytes 1179656 | tf_op jit(solution)/shard_map/ppermute | solution.py:789
  28.8 7.4 %collective-permute-start.9 = (f32[560,128]{1,0:T(8,128)S(1)}, f32[560,128]{1,0:T(8,128)S(1)}, u32[]{:S(2)}, u32[]{:S(2)}) collective-permute-start(f32[560,128]{1,0:T(8,128)S(1)} %get-tuple-element.61), channel_id=1, source_target_pairs={{16,0},{32,16},{48,32},{64,48},{80,64},{96,80},{112,96},{0,112},{1... | collective-permute-start | bytes 860168 | tf_op jit(solution)/shard_map/ppermute | solution.py:794
  30.8 5.3 %collective-permute-start.12 = (f32[288,128]{1,0:T(8,128)S(1)}, f32[288,128]{1,0:T(8,128)S(1)}, u32[]{:S(2)}, u32[]{:S(2)}) collective-permute-start(f32[288,128]{1,0:T(8,128)S(1)} %get-tuple-element.64), channel_id=1, source_target_pairs={{0,16},{16,32},{32,48},{48,64},{64,80},{80,96},{96,112},{112,0},{1... | collective-permute-start | bytes 442376 | tf_op jit(solution)/shard_map/ppermute | solution.py:789
  31.6 6.1 %collective-permute-start.13 = (f32[288,128]{1,0:T(8,128)S(1)}, f32[288,128]{1,0:T(8,128)S(1)}, u32[]{:S(2)}, u32[]{:S(2)}) collective-permute-start(f32[288,128]{1,0:T(8,128)S(1)} %get-tuple-element.65), channel_id=1, source_target_pairs={{16,0},{32,16},{48,32},{64,48},{80,64},{96,80},{112,96},{0,112},{1... | collective-permute-start | bytes 442376 | tf_op jit(solution)/shard_map/ppermute | solution.py:794

commit v7 on v6

--- a/solution.py
+++ b/solution.py
@@ -614,7 +614,6 @@
     group = lax.broadcasted_iota(jnp.int32, (GROUPS, CZ), 0)
     spot = lax.broadcasted_iota(jnp.int32, (GROUPS, CZ), 1)
     mask = [(spot // 16 == group) & (spot % 2 == odd) for odd in range(2)]
-    e[...] = jnp.zeros_like(e)
 
     def product(rows_of, f):
         total = jnp.zeros((GROUPS, width), jnp.float32)
@@ -826,7 +825,7 @@
     )
     odd, even = pairs(odd, True), pairs(even, False)
     above, below = ahead(up), back(down)
-    even, odd, above, below = lax.optimization_barrier((even, odd, above, below))
+    even, odd, above = lax.optimization_barrier((even, odd, above))
     up, down, reaction = call(
         pack_corners, [(FINE_CORNER_LINES, CZ)] * 2 + [(2 * FIELDS, CZ)], [],
         even, odd, reaction.T,

time: 69.6 us -> 69.6 us (level)
  starting transfers between devices: 16.8 us -> 19.2 us
  waiting for transfers between devices: 12.1 us -> 9.75 us
    ppermute x5, starting transfers between devices: 7.08 us -> 9.47 us  [ahead(): lax.ppermute(value, 'row', [(i, (i + 1) % count) for i in range(count)])]
    ppermute x5, waiting for transfers between devices: 8.91 us -> 6.54 us  [back(): lax.ppermute(value, 'row', [((i + 1) % count, i) for i in range(count)])]
  transfers between devices with their start and end apart: 16 -> 16, of which waited for: 7 -> 6; matrix products, arithmetic and copies ran while one was open for 0% -> 0% of each run, Pallas kernels for 8% -> 8%
where the time goes in v7:
time: 69.6 us; the launch traced here: 69.5 us
  blocking collectives  23.2 us (33%)
  starting transfers between devices  19.2 us (28%)
  Pallas kernels  17.1 us (25%)
  waiting for transfers between devices  9.75 us (14%)
    all_to_all x1, blocking collectives, body(): gathered = lax.all_to_all(sums, ('row', 'col'), 0, 0)  23.2 us
    pallas_call x7, Pallas kernels, call(): pl.pallas_call(kernel, out_shape=[jax.ShapeDtypeStruct(shape, jnp.float32...  17.1 us
    ppermute x5, starting transfers between devices, ahead(): lax.ppermute(value, 'row', [(i, (i + 1) % count) for i in range(count)])  9.47 us
    ppermute x6, starting transfers between devices, pairs(): return lax.ppermute(value, ('row', 'col'), moves)  6.65 us
    ppermute x5, waiting for transfers between devices, back(): lax.ppermute(value, 'row', [((i + 1) % count, i) for i in range(count)])  6.54 us
    ppermute x6, waiting for transfers between devices, pairs(): return lax.ppermute(value, ('row', 'col'), moves)  3.09 us
    ppermute x5, starting transfers between devices, back(): lax.ppermute(value, 'row', [((i + 1) % count, i) for i in range(count)])  3.04 us
  transfers between devices with their start and end apart: 16, of which 6 were waited for; matrix products, arithmetic and copies ran while one was open for 0% of the time, Pallas kernels for 8%

profile of v7, /device:TPU:1, one launch (start us, length us, event | category | flops | bytes accessed | tf_op | source)
XLA Modules:
  0.0 69.5 jit_solution(4403994527928275182)
XLA Ops:
  0.0 0.0 copy-start.1
  0.0 0.0 copy-start
  0.0 0.0 copy-start.3
  0.0 2.4 %shard_map.46 = (f32[960,128]{1,0:T(8,128)}, f32[960,128]{1,0:T(8,128)}, f32[320,128]{1,0:T(8,128)}, f32[320,128]{1,0:T(8,128)}, f32[256,128]{1,0:T(8,128)}) custom-call(f32[4,512,128]{2,1,0:T(8,128)} %bitcast.8, s32[512,128]{1,0:T(8,128)} %bitcast.11, f32[4,8,1024]{2,1,0:T(8,128)} %inverse.1), custom_call_target="tpu_custom_call" | custom-call | flops 100000 | bytes 350000 | tf_op jit(solution)/shard_map/pallas_call | solution.py:770
  2.4 0.0 copy-start.2
  2.4 2.6 %collective-permute-start.2 = (f32[960,128]{1,0:T(8,128)}, f32[960,128]{1,0:T(8,128)S(1)}, u32[]{:S(2)}, u32[]{:S(2)}) collective-permute-start(f32[960,128]{1,0:T(8,128)} %get-tuple-element.42), channel_id=1, source_target_pairs={{0,16},{16,32},{32,48},{48,64},{64,80},{80,96},{96,112},{112,0},{1... | collective-permute-start | bytes 1474568 | tf_op jit(solution)/shard_map/ppermute | solution.py:788
  5.0 0.0 collective-permute-start.3
  5.0 1.3 %collective-permute-start = (f32[320,128]{1,0:T(8,128)}, f32[320,128]{1,0:T(8,128)S(1)}, u32[]{:S(2)}, u32[]{:S(2)}) collective-permute-start(f32[320,128]{1,0:T(8,128)} %get-tuple-element.40), channel_id=1, source_target_pairs={{0,1},{1,0},{2,3},{3,2},{4,5},{5,4},{6,7},{7,6},{8,9},{9,8},{10,11... | collective-permute-start | bytes 491528 | tf_op jit(solution)/shard_map/ppermute | solution.py:808
  6.3 2.1 %collective-permute-start.1 = (f32[320,128]{1,0:T(8,128)}, f32[320,128]{1,0:T(8,128)S(1)}, u32[]{:S(2)}, u32[]{:S(2)}) collective-permute-start(f32[320,128]{1,0:T(8,128)} %get-tuple-element.41), channel_id=1, source_target_pairs={{0,16},{1,2},{2,1},{3,4},{4,3},{5,6},{6,5},{7,8},{8,7},{9,10},{10,... | collective-permute-start | bytes 491528 | tf_op jit(solution)/shard_map/ppermute | solution.py:808
  8.4 0.0 collective-permute-start.7
  8.4 1.2 %collective-permute-done.first.even = f32[320,128]{1,0:T(8,128)S(1)} collective-permute-done((f32[320,128]{1,0:T(8,128)}, f32[320,128]{1,0:T(8,128)S(1)}, u32[]{:S(2)}, u32[]{:S(2)}) %collective-permute-start) | collective-permute-done | bytes 163872 | tf_op jit(solution)/shard_map/ppermute | solution.py:808
  9.7 1.3 %collective-permute-start.6 = (f32[256,128]{1,0:T(8,128)}, f32[256,128]{1,0:T(8,128)S(1)}, u32[]{:S(2)}, u32[]{:S(2)}) collective-permute-start(f32[256,128]{1,0:T(8,128)} %get-tuple-element.50.own), channel_id=1, source_target_pairs={{0,1},{1,0},{2,3},{3,2},{4,5},{5,4},{6,7},{7,6},{8,9},{9,8},{10,11... | collective-permute-start | bytes 393224 | tf_op jit(solution)/shard_map/ppermute | solution.py:808
  11.0 0.0 collective-permute-done.1.second.odd
  11.0 0.1 collective-permute-done.2.above
  11.1 0.0 copy-done.3
  11.1 0.1 shard_map.47
  11.2 3.4 %collective-permute-start.4 = (f32[160,128]{1,0:T(8,128)S(1)}, f32[160,128]{1,0:T(8,128)S(1)}, u32[]{:S(2)}, u32[]{:S(2)}) collective-permute-start(f32[160,128]{1,0:T(8,128)S(1)} %get-tuple-element.48), channel_id=1, source_target_pairs={{0,16},{16,32},{32,48},{48,64},{64,80},{80,96},{96,112},{112,0},{1... | collective-permute-start | bytes 245768 | tf_op jit(solution)/shard_map/ppermute | solution.py:788
  14.6 0.0 collective-permute-start.5
  14.6 0.0 copy-done.1
  14.6 0.0 copy-done
  14.6 2.8 %shard_map.48 = (f32[4,256,128]{2,1,0:T(8,128)S(1)}, f32[4,256,128]{2,1,0:T(8,128)S(1)}, f32[3,64,128]{2,1,0:T(8,128)S(1)}, f32[2,3,2,4,56,128]{5,4,3,2,1,0:T(8,...) custom-call(f32[8,128]{1,0:T(8,128)S(1)} %get-tuple-element.45.reaction, ...), custom_call_target="tpu_custom_call" | custom-call | flops 100000000 | bytes 350000000 | tf_op jit(solution)/shard_map/pallas_call | solution.py:770
  17.4 0.0 collective-permute-done.7.kin_odd
  17.4 0.0 collective-permute-done.6.kin_even
  17.4 0.0 collective-permute-done.3.below
  17.4 0.0 collective-permute-done.4.kabove
  17.4 1.3 %collective-permute-done.5.kbelow = f32[160,128]{1,0:T(8,128)S(1)} collective-permute-done((f32[160,128]{1,0:T(8,128)S(1)}, f32[160,128]{1,0:T(8,128)S(1)}, u32[]{:S(2)}, u32[]{:S(2)}) %collective-permute-start.5) | collective-permute-done | bytes 81952 | tf_op jit(solution)/shard_map/ppermute | solution.py:793
  18.7 0.0 copy-done.2
  18.7 3.4 %shard_map.49 = (f32[4,512,128]{2,1,0:T(8,128)S(1)}, f32[4,640,128]{2,1,0:T(8,128)S(1)}, f32[28,56,128]{2,1,0:T(8,128)S(1)}, f32[3,160,128]{2,1,0:T(8,128)S(1)},...) custom-call(f32[8,128]{1,0:T(8,128)S(1)} %get-tuple-element.45.react, ...), custom_call_target="tpu_custom_call" | custom-call | flops 100000 | bytes 350000 | tf_op jit(solution)/shard_map/pallas_call | solution.py:770
  22.2 1.6 %collective-permute-start.10 = (f32[488,128]{1,0:T(8,128)S(1)}, f32[488,128]{1,0:T(8,128)S(1)}, u32[]{:S(2)}, u32[]{:S(2)}) collective-permute-start(f32[488,128]{1,0:T(8,128)S(1)} %get-tuple-element.60), channel_id=1, source_target_pairs={{0,1},{1,0},{2,3},{3,2},{4,5},{5,4},{6,7},{7,6},{8,9},{9,8},{10,11... | collective-permute-start | bytes 749576 | tf_op jit(solution)/shard_map/ppermute | solution.py:808
  23.8 1.0 %collective-permute-start.8 = (f32[560,128]{1,0:T(8,128)S(1)}, f32[560,128]{1,0:T(8,128)S(1)}, u32[]{:S(2)}, u32[]{:S(2)}) collective-permute-start(f32[560,128]{1,0:T(8,128)S(1)} %get-tuple-element.58), channel_id=1, source_target_pairs={{0,16},{16,32},{32,48},{48,64},{64,80},{80,96},{96,112},{112,0},{1... | collective-permute-start | bytes 860168 | tf_op jit(solution)/shard_map/ppermute | solution.py:788
  24.8 0.4 collective-permute-start.11
  25.2 0.2 collective-permute-start.15
  25.3 1.6 %collective-permute-start.14 = (f32[3,256,128]{2,1,0:T(8,128)S(1)}, f32[3,256,128]{2,1,0:T(8,128)S(1)}, u32[]{:S(2)}, u32[]{:S(2)}) collective-permute-start(f32[3,256,128]{2,1,0:T(8,128)S(1)} %get-tuple-element.65.kin), channel_id=1, source_target_pairs={{0,16},{16,32},{32,48},{48,64},{64,80},{80,96},{96,112},{112,0},{1... | collective-permute-start | bytes 1179656 | tf_op jit(solution)/shard_map/ppermute | solution.py:788
  26.9 1.8 %collective-permute-done.10.first.even = f32[488,128]{1,0:T(8,128)S(1)} collective-permute-done((f32[488,128]{1,0:T(8,128)S(1)}, f32[488,128]{1,0:T(8,128)S(1)}, u32[]{:S(2)}, u32[]{:S(2)}) %collective-permute-start.10) | collective-permute-done | bytes 249888 | tf_op jit(solution)/shard_map/ppermute | solution.py:808
  28.7 2.0 %collective-permute-start.9 = (f32[560,128]{1,0:T(8,128)S(1)}, f32[560,128]{1,0:T(8,128)S(1)}, u32[]{:S(2)}, u32[]{:S(2)}) collective-permute-start(f32[560,128]{1,0:T(8,128)S(1)} %get-tuple-element.59), channel_id=1, source_target_pairs={{16,0},{32,16},{48,32},{64,48},{80,64},{96,80},{112,96},{0,112},{1... | collective-permute-start | bytes 860168 | tf_op jit(solution)/shard_map/ppermute | solution.py:793
  30.8 0.0 collective-permute-done.11.second.odd
  30.8 0.8 %collective-permute-start.12 = (f32[288,128]{1,0:T(8,128)S(1)}, f32[288,128]{1,0:T(8,128)S(1)}, u32[]{:S(2)}, u32[]{:S(2)}) collective-permute-start(f32[288,128]{1,0:T(8,128)S(1)} %get-tuple-element.62), channel_id=1, source_target_pairs={{0,16},{16,32},{32,48},{48,64},{64,80},{80,96},{96,112},{112,0},{1... | collective-permute-start | bytes 442376 | tf_op jit(solution)/shard_map/ppermute | solution.py:788
  31.6 0.0 collective-permute-done.8.above
  31.6 0.9 %collective-permute-start.13 = (f32[288,128]{1,0:T(8,128)S(1)}, f32[288,128]{1,0:T(8,128)S(1)}, u32[]{:S(2)}, u32[]{:S(2)}) collective-permute-start(f32[288,128]{1,0:T(8,128)S(1)} %get-tuple-element.63), channel_id=1, source_target_pairs={{16,0},{32,16},{48,32},{64,48},{80,64},{96,80},{112,96},{0,112},{1... | collective-permute-start | bytes 442376 | tf_op jit(solution)/shard_map/ppermute | solution.py:793
  32.5 3.7 %collective-permute-done.9.below = f32[560,128]{1,0:T(8,128)S(1)} collective-permute-done((f32[560,128]{1,0:T(8,128)S(1)}, f32[560,128]{1,0:T(8,128)S(1)}, u32[]{:S(2)}, u32[]{:S(2)}) %collective-permute-start.9) | collective-permute-done | bytes 286752 | tf_op jit(solution)/shard_map/ppermute | solution.py:793
  36.2 0.0 collective-permute-done.12.kabove
  36.2 1.6 %collective-permute-done.13.kbelow = f32[288,128]{1,0:T(8,128)S(1)} collective-permute-done((f32[288,128]{1,0:T(8,128)S(1)}, f32[288,128]{1,0:T(8,128)S(1)}, u32[]{:S(2)}, u32[]{:S(2)}) %collective-permute-start.13) | collective-permute-done | bytes 147488 | tf_op jit(solution)/shard_map/ppermute | solution.py:793
  37.7 2.4 %shard_map.51 = (f32[2,12,32,128]{3,2,1,0:T(8,128)S(1)}, f32[2,18,32,128]{3,2,1,0:T(8,128)S(1)}, f32[2,18,32,128]{3,2,1,0:T(8,128)S(1)}, f32[128,128]{1,0:T(8,128)S(1)}) custom-call(f32[8,128]{1,0:T(8,128)S(1)} %get-tuple-element.45.reaction, f32[3,160,128]{2,1,0:T(8,128)S(1)} %get-tuple-element.57.coarse, f32[560,128]{1,0:T(8,128)S(1)} %collective-permute-done.8.above, ...), custom_call_target="tpu_custom_call" | custom-call | flops 2500000 | bytes 8750000 | tf_op jit(solution)/shard_map/pallas_call | solution.py:770
  40.2 0.0 collective-permute-done.15.kin_below
  40.2 0.0 collective-permute-done.14.kin_above
  40.2 23.2 %all_to_all.11 = f32[128,1,128]{2,1,0:T(1,128)S(1)} all-to-all(f32[128,1,128]{2,1,0:T(1,128)S(1)} %bitcast.15), channel_id=1, replica_groups=mesh['row'=8,'col'=16] {'row','col'}, dimensions={0} | all-to-all | bytes 131072 | tf_op jit(solution)/shard_map/all_to_all | solution.py:872
  63.4 5.9 %shard_map.52 = f32[4,512,128]{2,1,0:T(8,128)} custom-call(f32[8,128]{1,0:T(8,128)S(1)} %get-tuple-element.45.reaction, f32[128,128]{1,0:T(8,128)S(1)} %bitcast.14, f32[3,256,128]{2,1,0:T(8,128)S(1)} %get-tuple-element.65.kin, f32[3,256,128]{2,1,0:T(8,128)S(1)} %collective-permute-done.14.kin_above, f32[3,256,128]{2,1,0:T(8,128)S(1)} %collective-permute-done.15.kin_below, ...), custom_call_target="tpu_custom_call" | custom-call | flops 7000000 | bytes 24500000 | tf_op jit(solution)/shard_map/pallas_call | solution.py:770
  (1 shorter events, 0.0 us)
Async XLA Ops:
  0.0 14.6 %copy-start.1 = (s32[16,32,128]{2,1,0:T(8,128)S(1)}, s32[16,32,128]{2,1,0:T(8,128)}, u32[]{:S(2)}) copy-start(s32[16,32,128]{2,1,0:T(8,128)} %param.5) | copy-start | bytes 786436
  0.0 14.6 %copy-start = (f32[4,16,32,128]{3,2,1,0:T(8,128)S(1)}, f32[4,16,32,128]{3,2,1,0:T(8,128)}, u32[]{:S(2)}) copy-start(f32[4,16,32,128]{3,2,1,0:T(8,128)} %param.4) | copy-start | bytes 3145732
  0.0 11.1 %copy-start.3 = (f32[4,2]{0,1:T(2,128)S(1)}, f32[4,2]{0,1:T(2,128)}, u32[]{:S(2)}) copy-start(f32[4,2]{0,1:T(2,128)} %param.6) | copy-start | bytes 100
  2.4 16.4 %copy-start.2 = (f32[256,128]{1,0:T(8,128)S(1)}, f32[256,128]{1,0:T(8,128)}, u32[]{:S(2)}) copy-start(f32[256,128]{1,0:T(8,128)} %get-tuple-element.50.own) | copy-start | bytes 393220
  2.4 8.7 %collective-permute-start.2 = (f32[960,128]{1,0:T(8,128)}, f32[960,128]{1,0:T(8,128)S(1)}, u32[]{:S(2)}, u32[]{:S(2)}) collective-permute-start(f32[960,128]{1,0:T(8,128)} %get-tuple-element.42), channel_id=1, source_target_pairs={{0,16},{16,32},{32,48},{48,64},{64,80},{80,96},{96,112},{112,0},{1... | collective-permute-start | bytes 1474568 | tf_op jit(solution)/shard_map/ppermute | solution.py:788
  5.0 12.4 %collective-permute-start.3 = (f32[960,128]{1,0:T(8,128)}, f32[960,128]{1,0:T(8,128)S(1)}, u32[]{:S(2)}, u32[]{:S(2)}) collective-permute-start(f32[960,128]{1,0:T(8,128)} %get-tuple-element.47), channel_id=1, source_target_pairs={{16,0},{32,16},{48,32},{64,48},{80,64},{96,80},{112,96},{0,112},{1... | collective-permute-start | bytes 1474568 | tf_op jit(solution)/shard_map/ppermute | solution.py:793
  5.0 4.7 %collective-permute-start = (f32[320,128]{1,0:T(8,128)}, f32[320,128]{1,0:T(8,128)S(1)}, u32[]{:S(2)}, u32[]{:S(2)}) collective-permute-start(f32[320,128]{1,0:T(8,128)} %get-tuple-element.40), channel_id=1, source_target_pairs={{0,1},{1,0},{2,3},{3,2},{4,5},{5,4},{6,7},{7,6},{8,9},{9,8},{10,11... | collective-permute-start | bytes 491528 | tf_op jit(solution)/shard_map/ppermute | solution.py:808
  6.3 4.7 %collective-permute-start.1 = (f32[320,128]{1,0:T(8,128)}, f32[320,128]{1,0:T(8,128)S(1)}, u32[]{:S(2)}, u32[]{:S(2)}) collective-permute-start(f32[320,128]{1,0:T(8,128)} %get-tuple-element.41), channel_id=1, source_target_pairs={{0,16},{1,2},{2,1},{3,4},{4,3},{5,6},{6,5},{7,8},{8,7},{9,10},{10,... | collective-permute-start | bytes 491528 | tf_op jit(solution)/shard_map/ppermute | solution.py:808
  8.4 9.0 %collective-permute-start.7 = (f32[256,128]{1,0:T(8,128)}, f32[256,128]{1,0:T(8,128)S(1)}, u32[]{:S(2)}, u32[]{:S(2)}) collective-permute-start(f32[256,128]{1,0:T(8,128)} %get-tuple-element.50.own), channel_id=1, source_target_pairs={{0,16},{1,2},{2,1},{3,4},{4,3},{5,6},{6,5},{7,8},{8,7},{9,10},{10,... | collective-permute-start | bytes 393224 | tf_op jit(solution)/shard_map/ppermute | solution.py:808
  9.7 7.7 %collective-permute-start.6 = (f32[256,128]{1,0:T(8,128)}, f32[256,128]{1,0:T(8,128)S(1)}, u32[]{:S(2)}, u32[]{:S(2)}) collective-permute-start(f32[256,128]{1,0:T(8,128)} %get-tuple-element.50.own), channel_id=1, source_target_pairs={{0,1},{1,0},{2,3},{3,2},{4,5},{5,4},{6,7},{7,6},{8,9},{9,8},{10,11... | collective-permute-start | bytes 393224 | tf_op jit(solution)/shard_map/ppermute | solution.py:808
  11.2 6.3 %collective-permute-start.4 = (f32[160,128]{1,0:T(8,128)S(1)}, f32[160,128]{1,0:T(8,128)S(1)}, u32[]{:S(2)}, u32[]{:S(2)}) collective-permute-start(f32[160,128]{1,0:T(8,128)S(1)} %get-tuple-element.48), channel_id=1, source_target_pairs={{0,16},{16,32},{32,48},{48,64},{64,80},{80,96},{96,112},{112,0},{1... | collective-permute-start | bytes 245768 | tf_op jit(solution)/shard_map/ppermute | solution.py:788
  14.6 4.1 %collective-permute-start.5 = (f32[160,128]{1,0:T(8,128)S(1)}, f32[160,128]{1,0:T(8,128)S(1)}, u32[]{:S(2)}, u32[]{:S(2)}) collective-permute-start(f32[160,128]{1,0:T(8,128)S(1)} %get-tuple-element.49), channel_id=1, source_target_pairs={{16,0},{32,16},{48,32},{64,48},{80,64},{96,80},{112,96},{0,112},{1... | collective-permute-start | bytes 245768 | tf_op jit(solution)/shard_map/ppermute | solution.py:793
  22.2 6.5 %collective-permute-start.10 = (f32[488,128]{1,0:T(8,128)S(1)}, f32[488,128]{1,0:T(8,128)S(1)}, u32[]{:S(2)}, u32[]{:S(2)}) collective-permute-start(f32[488,128]{1,0:T(8,128)S(1)} %get-tuple-element.60), channel_id=1, source_target_pairs={{0,1},{1,0},{2,3},{3,2},{4,5},{5,4},{6,7},{7,6},{8,9},{9,8},{10,11... | collective-permute-start | bytes 749576 | tf_op jit(solution)/shard_map/ppermute | solution.py:808
  23.8 7.9 %collective-permute-start.8 = (f32[560,128]{1,0:T(8,128)S(1)}, f32[560,128]{1,0:T(8,128)S(1)}, u32[]{:S(2)}, u32[]{:S(2)}) collective-permute-start(f32[560,128]{1,0:T(8,128)S(1)} %get-tuple-element.58), channel_id=1, source_target_pairs={{0,16},{16,32},{32,48},{48,64},{64,80},{80,96},{96,112},{112,0},{1... | collective-permute-start | bytes 860168 | tf_op jit(solution)/shard_map/ppermute | solution.py:788
  24.8 6.0 %collective-permute-start.11 = (f32[488,128]{1,0:T(8,128)S(1)}, f32[488,128]{1,0:T(8,128)S(1)}, u32[]{:S(2)}, u32[]{:S(2)}) collective-permute-start(f32[488,128]{1,0:T(8,128)S(1)} %get-tuple-element.61), channel_id=1, source_target_pairs={{0,16},{1,2},{2,1},{3,4},{4,3},{5,6},{6,5},{7,8},{8,7},{9,10},{10,... | collective-permute-start | bytes 749576 | tf_op jit(solution)/shard_map/ppermute | solution.py:808
  25.2 15.0 %collective-permute-start.15 = (f32[3,256,128]{2,1,0:T(8,128)S(1)}, f32[3,256,128]{2,1,0:T(8,128)S(1)}, u32[]{:S(2)}, u32[]{:S(2)}) collective-permute-start(f32[3,256,128]{2,1,0:T(8,128)S(1)} %get-tuple-element.65.kin), channel_id=1, source_target_pairs={{16,0},{32,16},{48,32},{64,48},{80,64},{96,80},{112,96},{0,112},{1... | collective-permute-start | bytes 1179656 | tf_op jit(solution)/shard_map/ppermute | solution.py:793
  25.3 14.9 %collective-permute-start.14 = (f32[3,256,128]{2,1,0:T(8,128)S(1)}, f32[3,256,128]{2,1,0:T(8,128)S(1)}, u32[]{:S(2)}, u32[]{:S(2)}) collective-permute-start(f32[3,256,128]{2,1,0:T(8,128)S(1)} %get-tuple-element.65.kin), channel_id=1, source_target_pairs={{0,16},{16,32},{32,48},{48,64},{64,80},{80,96},{96,112},{112,0},{1... | collective-permute-start | bytes 1179656 | tf_op jit(solution)/shard_map/ppermute | solution.py:788
  28.7 7.4 %collective-permute-start.9 = (f32[560,128]{1,0:T(8,128)S(1)}, f32[560,128]{1,0:T(8,128)S(1)}, u32[]{:S(2)}, u32[]{:S(2)}) collective-permute-start(f32[560,128]{1,0:T(8,128)S(1)} %get-tuple-element.59), channel_id=1, source_target_pairs={{16,0},{32,16},{48,32},{64,48},{80,64},{96,80},{112,96},{0,112},{1... | collective-permute-start | bytes 860168 | tf_op jit(solution)/shard_map/ppermute | solution.py:793
  30.8 5.4 %collective-permute-start.12 = (f32[288,128]{1,0:T(8,128)S(1)}, f32[288,128]{1,0:T(8,128)S(1)}, u32[]{:S(2)}, u32[]{:S(2)}) collective-permute-start(f32[288,128]{1,0:T(8,128)S(1)} %get-tuple-element.62), channel_id=1, source_target_pairs={{0,16},{16,32},{32,48},{48,64},{64,80},{80,96},{96,112},{112,0},{1... | collective-permute-start | bytes 442376 | tf_op jit(solution)/shard_map/ppermute | solution.py:788
  31.6 6.1 %collective-permute-start.13 = (f32[288,128]{1,0:T(8,128)S(1)}, f32[288,128]{1,0:T(8,128)S(1)}, u32[]{:S(2)}, u32[]{:S(2)}) collective-permute-start(f32[288,128]{1,0:T(8,128)S(1)} %get-tuple-element.63), channel_id=1, source_target_pairs={{16,0},{32,16},{48,32},{64,48},{80,64},{96,80},{112,96},{0,112},{1... | collective-permute-start | bytes 442376 | tf_op jit(solution)/shard_map/ppermute | solution.py:793
